TPU v7x, 256 devices: a whole 4x4x8 slice. The times are simulated.
256 devices in a mesh: seq: 64 (over y, z_lo, x, core), tp: 4 (over z_hi).
Axes of the slice: x: 4, y: 4, z: 8 (z_hi: 4, z_lo: 2; z = z_hi * 2 + z_lo), core: 2. Of those that a mesh axis runs over, the one named last changes fastest.
Arguments:
- tokens: bfloat16 [256, 64, 1152], P(None, 'seq'), may hold values from -6 to 6
- grad_out: bfloat16 [256, 64, 1152], P('seq'), may hold values from -6 to 6
- qkv_weight: bfloat16 [2, 1152, 3, 1152], P(None, None, None, 'tp'), may hold values from -1 to 1
- out_weight: bfloat16 [2, 1152, 1152], P(None, 'tp'), may hold values from -0.1875 to 0.1875
- mod_shift: float32 [2, 1152], replicated, may hold values from -3 to 3
- mod_scale: float32 [2, 1152], replicated, may hold values from -1.8 to 1.8
- mod_gate: float32 [2, 1152], replicated, may hold values from 0.5 to 1.5
Outputs:
- result: bfloat16 [256, 64, 1152], P('seq')
- grad_in: bfloat16 [256, 64, 1152], P(None, 'seq')
All inputs are finite; a program needn't handle non-finite values.
Results may differ from a plain program's by a relative error of at most 0.035.
Values may be sent and summed in bfloat16 or wider, within the bound.
No kernel may reach another device: no remote copies, remote signals or barrier semaphores. Data moves between devices by JAX's collectives and lax.ppermute only.
A program may use at most 64 MiB of HBM per device.

v0:
```python
import math

import jax
import jax.numpy as jnp
from jax import lax
from jax.sharding import PartitionSpec as P

HEAD_DIM = 72


SPATIAL = ("pfhd,qfhd->fhpq", "fhpq,qfhd->pfhd", "fhpq,pfhd->qfhd")
TEMPORAL = ("pfhd,pghd->phfg", "phfg,pghd->pfhd", "phfg,pfhd->pghd")


def normalize(tokens, shift_row, scale_row):
    widened = tokens.astype(jnp.float32)
    center = widened - jnp.mean(widened, axis=-1, keepdims=True)
    inv_std = lax.rsqrt(jnp.mean(center * center, axis=-1, keepdims=True) + 1e-06)
    normed = center * inv_std
    modded = (normed * (1.0 + scale_row) + shift_row).astype(jnp.bfloat16)
    return (modded, normed, inv_std)


def attend(tokens, qkv_weights, shift_row, scale_row, layout_forms):
    modded, normed, inv_std = normalize(tokens, shift_row, scale_row)
    projected = jnp.einsum(
        "abd,dce->abce", modded, qkv_weights, preferred_element_type=jnp.float32
    ).astype(jnp.bfloat16)
    heads_here = qkv_weights.shape[2] // HEAD_DIM
    projected = projected.reshape(tokens.shape[0], tokens.shape[1], 3, heads_here, HEAD_DIM)
    queries, key_heads, value_heads = (projected[:, :, 0], projected[:, :, 1], projected[:, :, 2])
    scores = jnp.einsum(
        layout_forms[0], queries, key_heads, preferred_element_type=jnp.float32
    ) / math.sqrt(HEAD_DIM)
    probs_high = jax.nn.softmax(scores, axis=-1)
    probs_low = probs_high.astype(jnp.bfloat16)
    attended = jnp.einsum(
        layout_forms[1], probs_low, value_heads, preferred_element_type=jnp.float32
    ).astype(jnp.bfloat16)
    attended = attended.reshape(tokens.shape[0], tokens.shape[1], -1)
    return (attended, (normed, inv_std, queries, key_heads, value_heads, probs_high, probs_low))


def attend_back(grad, cache, out_matrix, gate_row, layout_forms):
    normed, inv_std, queries, key_heads, value_heads, probs_high, probs_low = cache
    grad_proj = (gate_row * grad.astype(jnp.float32)).astype(jnp.bfloat16)
    grad_attn = jnp.einsum(
        "abd,ed->abe", grad_proj, out_matrix, preferred_element_type=jnp.float32
    ).astype(jnp.bfloat16)
    grad_attn = grad_attn.reshape(queries.shape)
    grad_probs = jnp.einsum(
        layout_forms[0], grad_attn, value_heads, preferred_element_type=jnp.float32
    )
    grad_scores = (
        probs_high
        * (grad_probs - jnp.sum(probs_high * grad_probs, axis=-1, keepdims=True))
        / math.sqrt(HEAD_DIM)
    ).astype(jnp.bfloat16)
    grad_query = jnp.einsum(
        layout_forms[1], grad_scores, key_heads, preferred_element_type=jnp.float32
    ).astype(jnp.bfloat16)
    grad_keys = jnp.einsum(
        layout_forms[2], grad_scores, queries, preferred_element_type=jnp.float32
    ).astype(jnp.bfloat16)
    grad_values = jnp.einsum(
        layout_forms[2], probs_low, grad_attn, preferred_element_type=jnp.float32
    ).astype(jnp.bfloat16)
    stacked = jnp.stack([grad_query, grad_keys, grad_values], axis=2)
    return stacked.reshape(queries.shape[0], queries.shape[1], 3, -1)


def norm_back(grad_mod, normed, inv_std, scale_row):
    grad_norm = grad_mod * (1.0 + scale_row)
    return inv_std * (
        grad_norm
        - jnp.mean(grad_norm, axis=-1, keepdims=True)
        - normed * jnp.mean(grad_norm * normed, axis=-1, keepdims=True)
    )


def head_total(partial_value):
    return lax.psum(partial_value.astype(jnp.bfloat16), "tp").astype(jnp.float32)


def to_patches(frame_rows):
    return lax.all_to_all(frame_rows, "seq", split_axis=0, concat_axis=1, tiled=True)


def to_frames(patch_rows):
    return lax.all_to_all(patch_rows, "seq", split_axis=1, concat_axis=0, tiled=True)


def per_device(tokens, grad_out, qkv_weight, out_weight, mod_shift, mod_scale, mod_gate):
    attended, cache_s = attend(tokens, qkv_weight[0], mod_shift[0], mod_scale[0], SPATIAL)
    partial_value = jnp.einsum(
        "abe,ed->abd", attended, out_weight[0], preferred_element_type=jnp.float32
    )
    middle = (tokens.astype(jnp.float32) + mod_gate[0] * head_total(partial_value)).astype(
        jnp.bfloat16
    )
    mid_patch = to_patches(middle)
    attended_t, cache_t = attend(mid_patch, qkv_weight[1], mod_shift[1], mod_scale[1], TEMPORAL)
    partial_t = jnp.einsum(
        "abe,ed->abd", attended_t, out_weight[1], preferred_element_type=jnp.float32
    )
    result = (mid_patch.astype(jnp.float32) + mod_gate[1] * head_total(partial_t)).astype(
        jnp.bfloat16
    )
    stacked_t = attend_back(grad_out, cache_t, out_weight[1], mod_gate[1], TEMPORAL)
    normed_t, inv_std_t = (cache_t[0], cache_t[1])
    grad_mod = head_total(
        jnp.einsum("abce,dce->abd", stacked_t, qkv_weight[1], preferred_element_type=jnp.float32)
    )
    grad_patch = (
        grad_out.astype(jnp.float32) + norm_back(grad_mod, normed_t, inv_std_t, mod_scale[1])
    ).astype(jnp.bfloat16)
    grad_mid = to_frames(grad_patch)
    stacked_s = attend_back(grad_mid, cache_s, out_weight[0], mod_gate[0], SPATIAL)
    grad_mod_s = head_total(
        jnp.einsum("abce,dce->abd", stacked_s, qkv_weight[0], preferred_element_type=jnp.float32)
    )
    grad_in = (
        grad_mid.astype(jnp.float32) + norm_back(grad_mod_s, cache_s[0], cache_s[1], mod_scale[0])
    ).astype(jnp.bfloat16)
    return (result, grad_in)


def solution(mesh):
    in_specs = (
        P(None, "seq", None),
        P("seq", None, None),
        P(None, None, None, "tp"),
        P(None, "tp", None),
        P(),
        P(),
        P(),
    )
    out_specs = (P("seq", None, None), P(None, "seq", None))
    return jax.shard_map(
        per_device, mesh=mesh, in_specs=in_specs, out_specs=out_specs, check_vma=False
    )
```

profile of v0, /device:TPU:1, one launch (start us, length us, event | category | flops | bytes accessed | tf_op | source)
XLA Modules:
  0.0 294.2 jit_solution(8375402490085572498)
XLA Ops:
  7.2 1.3 convert_reduce_fusion
  8.5 1.4 fusion.48
  10.0 2.4 fusion.33
  12.5 1.5 fusion.132
  14.0 0.7 convolution_convert_fusion.10
  14.8 0.6 copy-done.6
  15.3 1.3 fusion.6
  16.8 58.4 %all-reduce.5.cloned.1.call-done = bf16[256,1,1152]{2,0,1:T(8,128)(2,1)} async-done(((bf16[256,1,1152]{2,0,1:T(8,128)(2,1)}), bf16[256,1,1152]{2,0,1:T(8,128)(2,1)}) %all-reduce.5.cloned.1.call-update) | async-done | bytes 589840 | tf_op jit(solution)/shard_map/psum | solution.py:82
  75.2 1.2 fusion.51
  76.4 0.5 broadcast.200
  76.9 1.0 reduce.23
  78.0 1.2 reshape.318
  79.2 9.4 %all-to-all-start = ((bf16[64,2,2304]{2,1,0:T(2,128)(2,1)}), bf16[64,2,2304]{2,1,0:T(2,128)(2,1)S(1)}, u32[]{:S(2)}, u32[]{:S(2)}) async-start(bf16[64,2,2304]{2,1,0:T(2,128)(2,1)} %reshape.318), calls=%async_computation | async-start | bytes 1179648 | tf_op jit(solution)/shard_map/all_to_all | solution.py:86
  88.8 1.6 convolution_convert_fusion.6
  90.6 11.2 %all-to-all-done = bf16[64,2,2304]{2,1,0:T(2,128)(2,1)S(1)} async-done(((bf16[64,2,2304]{2,1,0:T(2,128)(2,1)}), bf16[64,2,2304]{2,1,0:T(2,128)(2,1)S(1)}, u32[]{:S(2)}, u32[]{:S(2)}) %all-to-all-start) | async-done | bytes 589856 | tf_op jit(solution)/shard_map/all_to_all | solution.py:86
  101.7 0.5 reshape.319
  102.3 1.2 bitcast_convert_fusion
  103.9 0.5 copy-done.23
  104.4 1.9 fusion.28
  106.3 2.2 reshape.296
  108.4 1.0 fusion.131
  109.7 2.1 fusion.133
  111.8 1.4 fusion.62
  113.2 1.7 fusion.60
  114.9 2.3 fusion.61
  117.6 1.2 copy.74
  119.3 3.3 %fusion.4 = bf16[4,64,1152]{2,1,0:T(8,128)(2,1)} fusion(bf16[2,1152,3,288]{1,3,2,0:T(8,128)(2,1)} %param.9, bf16[4,64,1,288]{3,1,2,0:T(8,128)(2,1)S(1)} %bitcast.218, bf16[4,64,1,288]{3,1,2,0:T(8,128)(2,1)S(1)} %bitcast.219, bf16[4,64,1,288]{3,1,2,0:T(8,128)(2,1)S(1)} %bitcast.220), kind=kOutput, calls=%fused_computation.6 | convolution fusion | flops 510345216 | bytes 3022848 | tf_op jit(solution)/shard_map/abce,dce->abd/dot_general | solution.py:112
  122.6 50.1 %all-reduce.7.cloned.1.call-done = bf16[4,64,1152]{2,1,0:T(8,128)(2,1)} async-done(((bf16[4,64,1152]{2,1,0:T(8,128)(2,1)}), bf16[4,64,1152]{2,1,0:T(8,128)(2,1)}) %all-reduce.7.cloned.1.call-update) | async-done | bytes 589840 | tf_op jit(solution)/shard_map/psum | solution.py:82
  172.7 1.5 fusion.58
  174.3 0.5 fusion.50
  174.8 1.3 copy.80
  176.1 9.4 %all-to-all-start.1 = ((bf16[4,64,1152]{2,0,1:T(4,128)(2,1)}), bf16[4,64,1152]{2,0,1:T(4,128)(2,1)S(1)}, u32[]{:S(2)}, u32[]{:S(2)}) async-start(bf16[4,64,1152]{2,0,1:T(4,128)(2,1)} %copy.80), calls=%async_computation.1 | async-start | bytes 1179648 | tf_op jit(solution)/shard_map/all_to_all | solution.py:90
  185.8 1.4 fusion.59
  187.6 2.4 convolution_convert_fusion
  190.0 8.7 %all-to-all-done.1 = bf16[4,64,1152]{2,0,1:T(4,128)(2,1)S(1)} async-done(((bf16[4,64,1152]{2,0,1:T(4,128)(2,1)}), bf16[4,64,1152]{2,0,1:T(4,128)(2,1)S(1)}, u32[]{:S(2)}, u32[]{:S(2)}) %all-to-all-start.1) | async-done | bytes 589856 | tf_op jit(solution)/shard_map/all_to_all | solution.py:90
  198.7 2.4 reshape.302
  201.1 2.2 multiply_convert_fusion
  203.7 0.6 copy-done.13
  204.3 1.4 convolution_convert_fusion.7
  205.7 1.3 fusion.116
  207.1 3.4 %convolution_convert_fusion.9 = bf16[4,72,256]{2,1,0:T(8,128)(2,1)} fusion(f32[4,256,256]{1,2,0:T(8,128)} %fusion.116, bf16[256,1,3,4,72]{0,4,3,2,1:T(8,128)(2,1)S(1)} %bitcast.228, f32[4,256,256]{1,2,0:T(8,128)} %get-tuple-element.18, f32[4,256]{1,0:T(4,128)S(1)} %copy-done.28), kind=kOutput, calls=%fused_computation.87 | convolution fusion | flops 39658752 | bytes 4497408 | tf_op jit(solution)/shard_map/fhpq,qfhd->pfhd/dot_general | solution.py:59
  210.4 3.4 %convolution_convert_fusion.8 = bf16[4,72,256]{2,1,0:T(8,128)(2,1)} fusion(f32[4,256,256]{1,2,0:T(8,128)} %fusion.116, bf16[256,1,3,4,72]{0,4,3,2,1:T(8,128)(2,1)S(1)} %bitcast.229, f32[4,256,256]{1,2,0:T(8,128)} %get-tuple-element.18, f32[4,256]{1,0:T(4,128)S(1)} %copy-done.28), kind=kOutput, calls=%fused_computation.86 | convolution fusion | flops 39658752 | bytes 4497408 | tf_op jit(solution)/shard_map/fhpq,pfhd->qfhd/dot_general | solution.py:62
  213.8 3.4 %fusion.7 = bf16[256,1,1152]{2,0,1:T(8,128)(2,1)} fusion(bf16[2,1152,3,288]{1,3,2,0:T(8,128)(2,1)} %param.9, bf16[256,1,1,288]{0,3,2,1:T(8,128)(2,1)S(1)} %bitcast.230, bf16[256,1,1,288]{0,3,2,1:T(8,128)(2,1)} %bitcast.232, bf16[256,1,1,288]{0,3,2,1:T(8,128)(2,1)} %bitcast.231), kind=kOutput, calls=%fused_computation.11 | convolution fusion | flops 510345216 | bytes 3022848 | tf_op jit(solution)/shard_map/abce,dce->abd/dot_general | solution.py:120
  217.3 1.4 reshape.301
  218.7 64.3 %all-reduce.9.cloned.1.call-done = (bf16[4,64,1152]{2,1,0:T(8,128)(2,1)}, bf16[256,1,1152]{2,0,1:T(8,128)(2,1)}) async-done(((bf16[4,64,1152]{2,1,0:T(8,128)(2,1)}, bf16[256,1,1152]{2,0,1:T(8,128)(2,1)}), (bf16[4,64,1152]{2,1,0:T(8,128)(2,1)}, bf16[256,1,1152]{2,0,1:T(8,128)(2,1)})) %all-reduce.9.cloned.1.call-update) | async-done | bytes 1179664 | tf_op jit(solution)/shard_map/psum | solution.py:82
  283.0 2.1 fusion.52
  285.5 0.8 copy-done.1
  286.4 1.3 fusion.47
  (84 shorter events, 3.9 us)
Async XLA Ops:
  7.2 2.8 copy-start
  7.2 2.7 copy-start.21
  7.2 2.7 copy-start.20
  7.2 68.0 %all-reduce.5.cloned.1.call-start = ((), (), s32[]{:S(2)}) async-start(), calls=%async_computation.2 | async-start | bytes 1179648 | tf_op jit(solution)/shard_map/psum | solution.py:82
  8.5 3.9 %copy-start.16 = (f32[256]{0:T(256)}, f32[256]{0:T(256)S(1)}, u32[]{:S(2)}) copy-start(f32[256]{0:T(256)S(1)} %broadcast_multiply_fusion.5) | copy-start | bytes 3076
  9.9 2.5 copy-start.18
  12.5 2.3 copy-start.12
  14.0 0.7 copy-start.27
  14.0 1.3 copy-start.6
  14.8 1.9 copy-start.22
  16.7 72.0 %copy-start.14 = (f32[1152]{0:T(1024)}, f32[1152]{0:T(1024)S(1)}, u32[]{:S(2)}) copy-start(f32[1152]{0:T(1024)S(1)} %get-tuple-element.6) | copy-start | bytes 13828
  78.0 10.8 %copy-start.4 = (bf16[4,64,1152]{2,1,0:T(8,128)(2,1)S(1)}, bf16[4,64,1152]{2,1,0:T(8,128)(2,1)}, u32[]{:S(2)}) copy-start(bf16[4,64,1152]{2,1,0:T(8,128)(2,1)} %param.8) | copy-start | bytes 1769476
  79.2 22.6 %all-to-all-start = ((bf16[64,2,2304]{2,1,0:T(2,128)(2,1)}), bf16[64,2,2304]{2,1,0:T(2,128)(2,1)S(1)}, u32[]{:S(2)}, u32[]{:S(2)}) async-start(bf16[64,2,2304]{2,1,0:T(2,128)(2,1)} %reshape.318), calls=%async_computation | async-start | bytes 1179648 | tf_op jit(solution)/shard_map/all_to_all | solution.py:86
  88.6 84.1 %all-reduce.7.cloned.1.call-start = ((), (), s32[]{:S(2)}) async-start(), calls=%async_computation.3 | async-start | bytes 1179648 | tf_op jit(solution)/shard_map/psum | solution.py:82
  102.2 2.1 copy-start.23
  109.5 2.3 copy-start.8
  109.5 2.3 copy-start.9
  111.8 3.1 %copy-start.25 = (f32[4,4,64]{2,1,0:T(4,128)}, f32[4,4,64]{2,1,0:T(4,128)S(1)}, u32[]{:S(2)}) copy-start(f32[4,4,64]{2,1,0:T(4,128)S(1)} %get-tuple-element.19) | copy-start | bytes 12292
  113.2 1.7 copy-start.10
  122.6 51.7 %copy-start.5 = (bf16[4,64,1152]{2,1,0:T(8,128)(2,1)S(1)}, bf16[4,64,1152]{2,1,0:T(8,128)(2,1)}, u32[]{:S(2)}) copy-start(bf16[4,64,1152]{2,1,0:T(8,128)(2,1)} %param.8) | copy-start | bytes 1769476
  172.7 1.6 copy-start.2
  174.8 10.9 %copy-start.11 = (bf16[4,64,1,4,72]{4,3,1,2,0:T(4,128)(2,1)S(1)}, bf16[4,64,1,4,72]{4,3,1,2,0:T(4,128)(2,1)}, u32[]{:S(2)}) copy-start(bf16[4,64,1,4,72]{4,3,1,2,0:T(4,128)(2,1)} %get-tuple-element.15) | copy-start | bytes 442372
  174.8 10.9 %copy-start.26 = (f32[4,4,64]{2,1,0:T(4,128)S(1)}, f32[4,4,64]{2,1,0:T(4,128)}, u32[]{:S(2)}) copy-start(f32[4,4,64]{2,1,0:T(4,128)} %copy-done.25) | copy-start | bytes 12292
  176.1 22.6 %all-to-all-start.1 = ((bf16[4,64,1152]{2,0,1:T(4,128)(2,1)}), bf16[4,64,1152]{2,0,1:T(4,128)(2,1)S(1)}, u32[]{:S(2)}, u32[]{:S(2)}) async-start(bf16[4,64,1152]{2,0,1:T(4,128)(2,1)} %copy.80), calls=%async_computation.1 | async-start | bytes 1179648 | tf_op jit(solution)/shard_map/all_to_all | solution.py:90
  185.5 97.5 %all-reduce.9.cloned.1.call-start = ((), (), s32[]{:S(2)}) async-start(), calls=%async_computation.4 | async-start | bytes 2359296 | tf_op jit(solution)/shard_map/psum | solution.py:82
  201.1 2.2 copy-start.7
  203.3 1.0 copy-start.13
  203.3 1.0 copy-start.28
  210.4 3.4 %copy-start.24 = (bf16[4,72,256]{2,1,0:T(8,128)(2,1)S(1)}, bf16[4,72,256]{2,1,0:T(8,128)(2,1)}, u32[]{:S(2)}) copy-start(bf16[4,72,256]{2,1,0:T(8,128)(2,1)} %convolution_convert_fusion.7) | copy-start | bytes 442372
  217.2 65.7 %copy-start.15 = (f32[1152]{0:T(1024)S(1)}, f32[1152]{0:T(1024)}, u32[]{:S(2)}) copy-start(f32[1152]{0:T(1024)} %copy-done.14) | copy-start | bytes 13828
  283.0 2.1 copy-start.3
  283.0 2.1 copy-start.17
  283.0 2.1 copy-start.19
  285.1 1.3 copy-start.1
Sparse Core Ops, SparseCore 0:
  16.8 58.3 all-reduce.4
  122.7 49.9 all-reduce.6
  217.4 65.5 all-reduce.8
where the time goes:
time: 295 us; the launch traced here: 294 us
  waiting for transfers between devices  193 us (65%)
  matrix products  37.5 us (13%)
  starting transfers between devices  19.3 us (7%)
  local copies, waits for them, and re-layouts  15.8 us (5%)
  other arithmetic  14.7 us (5%)
  between operations  14.3 us (5%)
    psum x3, waiting for transfers between devices, head_total(): lax.psum(partial_value.astype(jnp.bfloat16), 'tp').astype(jnp.float32)  173 us
    all_to_all x1, waiting for transfers between devices, to_patches(): lax.all_to_all(frame_rows, 'seq', split_axis=0, concat_axis=1, tiled=True)  11.2 us
    all_to_all x1, starting transfers between devices, to_patches(): lax.all_to_all(frame_rows, 'seq', split_axis=0, concat_axis=1, tiled=True)  9.37 us
    all_to_all x1, starting transfers between devices, to_frames(): lax.all_to_all(patch_rows, 'seq', split_axis=1, concat_axis=0, tiled=True)  9.37 us
    all_to_all x1, waiting for transfers between devices, to_frames(): lax.all_to_all(patch_rows, 'seq', split_axis=1, concat_axis=0, tiled=True)  8.65 us
  transfers between devices with their start and end apart: 5, of which 5 were waited for; matrix products, arithmetic and copies ran while one was open for 3% of the time, Pallas kernels for 0%

commit v1 on v0

v1 whole, which is shorter than its diff:
```python
import math

import jax
import jax.numpy as jnp
from jax import lax
from jax.experimental import pallas as pl
from jax.experimental.pallas import tpu as pltpu
from jax.sharding import PartitionSpec as P

D = 1152
HEAD_DIM = 72
HERE = 4
GW = HERE * HEAD_DIM
N_TP = 4
ROWS = 64
INV_ROOT = 1.0 / math.sqrt(HEAD_DIM)
F32 = jnp.float32
BF16 = jnp.bfloat16


def nn(a, b):
    return lax.dot_general(a, b, (((1,), (0,)), ((), ())), preferred_element_type=F32)


def nt(a, b):
    return lax.dot_general(a, b, (((1,), (1,)), ((), ())), preferred_element_type=F32)


def tn(a, b):
    return lax.dot_general(a, b, (((0,), (0,)), ((), ())), preferred_element_type=F32)


def normalize(tokens):
    widened = tokens.astype(F32)
    center = widened - jnp.mean(widened, axis=-1, keepdims=True)
    inv_std = lax.rsqrt(jnp.mean(center * center, axis=-1, keepdims=True) + 1e-06)
    return center * inv_std, inv_std


def norm_back(grad_mod, normed, inv_std, scale_row):
    grad_norm = grad_mod * (1.0 + scale_row)
    return inv_std * (
        grad_norm
        - jnp.mean(grad_norm, axis=-1, keepdims=True)
        - normed * jnp.mean(grad_norm * normed, axis=-1, keepdims=True)
    )


def softmax(scores):
    top = jnp.max(scores, axis=-1, keepdims=True)
    raised = jnp.exp(scores - top)
    return raised / jnp.sum(raised, axis=-1, keepdims=True)


def of_head(array, head):
    lane = lax.broadcasted_iota(jnp.int32, array.shape, 1)
    keep = (lane >= head * HEAD_DIM) & (lane < (head + 1) * HEAD_DIM)
    return jnp.where(keep, array, jnp.zeros_like(array))


def order_matrix(me, rows):
    place = lax.broadcasted_iota(jnp.int32, (rows, 256), 0)
    patch = lax.broadcasted_iota(jnp.int32, (rows, 256), 1)
    wanted = 4 * (place % ROWS) + (me + place // ROWS) % 4
    return (patch == wanted).astype(F32).astype(BF16)


def spatial_forward(me_ref, x_ref, w_ref, ow_ref, shift_ref, scale_ref, p0, p1, p2, p3, qkv_ref, own_ref):
    me = me_ref[0]
    tokens = x_ref[...]
    normed, _ = normalize(tokens)
    modded = (normed * (1.0 + scale_ref[0]) + shift_ref[0]).astype(BF16)
    order = order_matrix(me, 256)
    modded = nn(order, modded).astype(BF16)
    own_ref[...] = nn(order[:ROWS], tokens).astype(BF16)
    queries = nt(modded, w_ref[0, 0]).astype(BF16)
    key_heads = nt(modded, w_ref[0, 1]).astype(BF16)
    value_heads = nt(modded, w_ref[0, 2]).astype(BF16)
    qkv_ref[0] = queries
    qkv_ref[1] = key_heads
    qkv_ref[2] = value_heads
    attended = jnp.zeros((256, GW), F32)
    for head in range(HERE):
        probs = softmax(nt(of_head(queries, head), key_heads) * INV_ROOT)
        attended = attended + nn(probs.astype(BF16), of_head(value_heads, head))
    attended = attended.astype(BF16)
    for k, part in enumerate((p0, p1, p2, p3)):
        part[...] = nn(attended[k * ROWS : (k + 1) * ROWS], ow_ref[0]).astype(BF16)


def temporal(me_ref, m_ref, g_ref, w_ref, ow_ref, shift_ref, scale_ref, gate_ref, *rest):
    part_ref, out_part_ref, kept_ref = rest[-3:]
    mid = m_ref[...]
    kept_ref[0] = mid
    normed, _ = normalize(mid)
    modded = (normed * (1.0 + scale_ref[0]) + shift_ref[0]).astype(BF16)
    queries = nt(modded, w_ref[0, 0]).astype(BF16)
    key_heads = nt(modded, w_ref[0, 1]).astype(BF16)
    value_heads = nt(modded, w_ref[0, 2]).astype(BF16)

    def spread(array):
        return jnp.concatenate([of_head(array, head) for head in range(HERE)], axis=0)

    def gather_heads(array):
        total = of_head(array[:ROWS], 0)
        for head in range(1, HERE):
            total = total + of_head(array[head * ROWS : (head + 1) * ROWS], head)
        return total

    queries_4 = spread(queries)
    probs = softmax(nt(queries_4, key_heads) * INV_ROOT)
    probs_low = probs.astype(BF16)
    grad_proj = (gate_ref[0] * g_ref[0].astype(F32)).astype(BF16)
    grad_attn_4 = spread(nt(grad_proj, ow_ref[0]).astype(BF16))
    grad_probs = nt(grad_attn_4, value_heads)
    grad_scores = (
        probs * (grad_probs - jnp.sum(probs * grad_probs, axis=-1, keepdims=True)) * INV_ROOT
    ).astype(BF16)
    grad_query = gather_heads(nn(grad_scores, key_heads)).astype(BF16)
    grad_keys = tn(grad_scores, queries_4).astype(BF16)
    grad_values = tn(probs_low, grad_attn_4).astype(BF16)
    part = nn(grad_query, w_ref[0, 0]) + nn(grad_keys, w_ref[0, 1]) + nn(grad_values, w_ref[0, 2])
    part_ref[...] = part.astype(BF16)
    attended = gather_heads(nn(probs_low, value_heads)).astype(BF16)
    out_part_ref[0] = nn(attended, ow_ref[0]).astype(BF16)


def spatial_backward(g0, g1, g2, g3, qkv_ref, w_ref, ow_ref, gate_ref, p0, p1, p2, p3):
    grad = jnp.concatenate([g0[...], g1[...], g2[...], g3[...]], axis=0)
    grad_proj = (gate_ref[0] * grad.astype(F32)).astype(BF16)
    grad_attn = nt(grad_proj, ow_ref[0]).astype(BF16)
    queries, key_heads, value_heads = qkv_ref[0], qkv_ref[1], qkv_ref[2]
    grad_query = jnp.zeros((256, GW), F32)
    grad_keys = jnp.zeros((256, GW), F32)
    grad_values = jnp.zeros((256, GW), F32)
    for head in range(HERE):
        query = of_head(queries, head)
        grad_head = of_head(grad_attn, head)
        probs = softmax(nt(query, key_heads) * INV_ROOT)
        grad_probs = nt(grad_head, value_heads)
        grad_scores = (
            probs * (grad_probs - jnp.sum(probs * grad_probs, axis=-1, keepdims=True)) * INV_ROOT
        ).astype(BF16)
        grad_query = grad_query + nn(grad_scores, of_head(key_heads, head))
        grad_keys = grad_keys + tn(grad_scores, query)
        grad_values = grad_values + tn(probs.astype(BF16), grad_head)
    total = (
        nn(grad_query.astype(BF16), w_ref[0, 0])
        + nn(grad_keys.astype(BF16), w_ref[0, 1])
        + nn(grad_values.astype(BF16), w_ref[0, 2])
    )
    for k, part in enumerate((p0, p1, p2, p3)):
        part[...] = total[k * ROWS : (k + 1) * ROWS].astype(BF16)


def mid_of(x_ref, p0, p1, p2, p3, gate_ref, mid_ref):
    total = (p0[...].astype(F32) + p1[...].astype(F32)) + (p2[...].astype(F32) + p3[...].astype(F32))
    mid_ref[...] = (x_ref[...].astype(F32) + gate_ref[0] * total).astype(BF16)


def grad_of(x_ref, g_ref, p0, p1, p2, p3, scale_ref, grad_ref):
    total = (p0[...].astype(F32) + p1[...].astype(F32)) + (p2[...].astype(F32) + p3[...].astype(F32))
    normed, inv_std = normalize(x_ref[...])
    grad = g_ref[...].reshape(ROWS, D).astype(F32)
    grad_ref[...] = (grad + norm_back(total, normed, inv_std, scale_ref[0])).astype(BF16)


def reorder(me_ref, g0, g1, g2, g3, out_ref):
    stacked = jnp.concatenate([g0[...], g1[...], g2[...], g3[...]], axis=0)
    out_ref[...] = tn(order_matrix(me_ref[0], 256), stacked).astype(BF16)


SEMANTICS = pltpu.CompilerParams(vmem_limit_bytes=24 * 1024 * 1024)


def whole(shape):
    return pl.BlockSpec(shape, lambda *_: (0,) * len(shape))


def row_of(block):
    return pl.BlockSpec((1, 1, D), lambda *_: (block, 0, 0))


def rows_out():
    return jax.ShapeDtypeStruct((ROWS, D), BF16)


def run(body, me, operands, specs, out_shape, out_specs, flops, aliases=None):
    return pl.pallas_call(
        body,
        grid_spec=pltpu.PrefetchScalarGridSpec(
            num_scalar_prefetch=0 if me is None else 1,
            grid=(1,),
            in_specs=specs,
            out_specs=out_specs,
        ),
        out_shape=out_shape,
        input_output_aliases=aliases or {},
        compiler_params=SEMANTICS,
        cost_estimate=pl.CostEstimate(flops=flops, bytes_accessed=3_000_000, transcendentals=0),
    )(*(() if me is None else (me,)), *operands)


def shift(array, k):
    return lax.ppermute(array, "tp", [(i, (i + k) % N_TP) for i in range(N_TP)])


def across(array):
    return lax.all_to_all(array, "seq", split_axis=0, concat_axis=0, tiled=True)


def per_device(tokens, grad_out, qkv_weight, out_weight, mod_shift, mod_scale, mod_gate):
    me = lax.axis_index("tp").astype(jnp.int32).reshape(1)
    tokens = tokens.reshape(256, D)
    weights = jnp.transpose(qkv_weight, (0, 2, 3, 1))
    mod_shift, mod_scale, mod_gate = (row.reshape(2, 1, D) for row in (mod_shift, mod_scale, mod_gate))
    quarter = whole((ROWS, D))

    def w_of(block):
        return pl.BlockSpec((1, 3, GW, D), lambda *_: (block, 0, 0, 0))

    def ow_of(block):
        return pl.BlockSpec((1, GW, D), lambda *_: (block, 0, 0))

    p0, p1, p2, p3, qkv_s, own = run(
        spatial_forward,
        me,
        (tokens, weights, out_weight, mod_shift, mod_scale),
        [whole((256, D)), w_of(0), ow_of(0), row_of(0), row_of(0)],
        (rows_out(),) * 4 + (jax.ShapeDtypeStruct((3, 256, GW), BF16), rows_out()),
        (quarter,) * 4 + (whole((3, 256, GW)), quarter),
        1_000_000_000,
    )
    p1, p3, p2 = shift(p1, 1), shift(p3, 3), shift(p2, 2)
    middle = run(
        mid_of, None, (own, p0, p1, p2, p3, mod_gate), [quarter] * 5 + [row_of(0)],
        rows_out(), quarter, 1_000_000,
    )
    mid_own = across(middle)

    mids = [mid_own, shift(mid_own, 1), shift(mid_own, 2), shift(mid_own, 3)]
    parts = [None] * 4
    kept = None
    whole_4 = jax.ShapeDtypeStruct((4, ROWS, D), BF16)
    for k in (0, 1, 3, 2):
        chunk = pl.BlockSpec((1, ROWS, D), lambda _, at, k=k: ((at[0] + 4 - k) % 4, 0, 0))
        anywhere = pl.BlockSpec(memory_space=pl.ANY)
        operands = (mids[k], grad_out, weights, out_weight, mod_shift, mod_scale, mod_gate)
        specs = [quarter, chunk, w_of(1), ow_of(1), row_of(1), row_of(1), row_of(1)]
        aliases = None
        if kept is not None:
            operands, specs, aliases = operands + kept, specs + [anywhere] * 2, {8: 1, 9: 2}
        part, out_part, mid_4 = run(
            temporal, me, operands, specs, (rows_out(), whole_4, whole_4),
            (quarter, chunk, chunk), 500_000_000, aliases,
        )
        kept = (out_part, mid_4)
        parts[k] = shift(part, 4 - k) if k else part
    out_total = lax.psum(kept[0], "tp").astype(F32)
    result = (kept[1].astype(F32) + mod_gate[1] * out_total).astype(BF16)

    own_grad = pl.BlockSpec((1, ROWS, D), lambda _, at: (at[0], 0, 0))
    grad_patch = run(
        lambda me_ref, *refs: grad_of(*refs),
        me, (mid_own, grad_out, *parts, mod_scale), [quarter, own_grad] + [quarter] * 4 + [row_of(1)],
        rows_out(), quarter, 1_000_000,
    )
    grad_own = across(grad_patch)

    grads = [grad_own, shift(grad_own, 3), shift(grad_own, 2), shift(grad_own, 1)]
    b0, b1, b2, b3 = run(
        spatial_backward, None, (*grads, qkv_s, weights, out_weight, mod_gate),
        [quarter] * 4 + [whole((3, 256, GW)), w_of(0), ow_of(0), row_of(0)],
        (rows_out(),) * 4, (quarter,) * 4, 1_500_000_000,
    )
    b1, b3, b2 = shift(b1, 1), shift(b3, 3), shift(b2, 2)
    grad_in_own = run(
        grad_of, None, (own, grad_own, b0, b1, b2, b3, mod_scale), [quarter] * 6 + [row_of(0)],
        rows_out(), quarter, 1_000_000,
    )
    ends = (grad_in_own, shift(grad_in_own, 3), shift(grad_in_own, 2), shift(grad_in_own, 1))
    grad_in = run(
        reorder, me, ends, [quarter] * 4,
        jax.ShapeDtypeStruct((256, D), BF16), whole((256, D)), 100_000_000,
    )
    return (result, grad_in.reshape(256, 1, D))


def solution(mesh):
    in_specs = (
        P(None, "seq", None),
        P("seq", None, None),
        P(None, None, None, "tp"),
        P(None, "tp", None),
        P(),
        P(),
        P(),
    )
    out_specs = (P("seq", None, None), P(None, "seq", None))
    return jax.shard_map(
        per_device, mesh=mesh, in_specs=in_specs, out_specs=out_specs, check_vma=False
    )
```

time: 295 us -> 198 us (0.67)
  waiting for transfers between devices: 193 us -> 72.5 us
  matrix products: 37.5 us -> 0 us
  starting transfers between devices: 19.3 us -> 53.3 us
  Pallas kernels: 0 us -> 23.3 us
  blocking collectives: 0 us -> 16.6 us
  other arithmetic: 14.7 us -> 3.44 us
    psum x3 -> x1, waiting for transfers between devices: 173 us -> 3.71 us  [per_device(): out_total = lax.psum(kept[0], 'tp').astype(F32)]
    ppermute x0 -> x18, waiting for transfers between devices: none -> 60.1 us  [shift(): return lax.ppermute(array, 'tp', [(i, (i + k) % N_TP) for i in range(N_TP)])]
    ppermute x0 -> x18, starting transfers between devices: none -> 45.6 us  [shift(): return lax.ppermute(array, 'tp', [(i, (i + k) % N_TP) for i in range(N_TP)])]
    dot_general x18 -> x0, matrix products: 33.9 us -> none  [the longest x2 5.63 us: attend_back(): jnp.einsum(layout_forms[2], grad_scores, queries, preferred_element_type=...]
    pallas_call x0 -> x10, Pallas kernels: none -> 23.3 us  [run(): pl.pallas_call(body, grid_spec=pltpu.PrefetchScalarGridSpec(num_scalar_pr...]
    all_to_all x0 -> x1, blocking collectives: none -> 16.6 us  [across(): return lax.all_to_all(array, 'seq', split_axis=0, concat_axis=0, tiled=True)]
    all_to_all x2 -> x1, waiting for transfers between devices: 19.8 us -> 8.04 us  [across(): return lax.all_to_all(array, 'seq', split_axis=0, concat_axis=0, tiled=True)]
    all_to_all x2 -> x1, starting transfers between devices: 18.7 us -> 7.6 us  [across(): return lax.all_to_all(array, 'seq', split_axis=0, concat_axis=0, tiled=True)]
  transfers between devices with their start and end apart: 5 -> 20, of which waited for: 5 -> 15; matrix products, arithmetic and copies ran while one was open for 3% -> 2% of each run, Pallas kernels for 0% -> 7%
where the time goes in v1:
time: 198 us; the launch traced here: 197 us
  waiting for transfers between devices  72.5 us (37%)
  starting transfers between devices  53.3 us (27%)
  Pallas kernels  23.3 us (12%)
  blocking collectives  16.6 us (8%)
  between operations  14.1 us (7%)
  local copies, waits for them, and re-layouts  13.6 us (7%)
  other arithmetic  3.44 us (2%)
    ppermute x18, waiting for transfers between devices, shift(): return lax.ppermute(array, 'tp', [(i, (i + k) % N_TP) for i in range(N_TP)])  60.1 us
    ppermute x18, starting transfers between devices, shift(): return lax.ppermute(array, 'tp', [(i, (i + k) % N_TP) for i in range(N_TP)])  45.6 us
    pallas_call x10, Pallas kernels, run(): pl.pallas_call(body, grid_spec=pltpu.PrefetchScalarGridSpec(num_scalar_pr...  23.3 us
    all_to_all x1, blocking collectives, across(): return lax.all_to_all(array, 'seq', split_axis=0, concat_axis=0, tiled=True)  16.6 us
    unnamed x22, local copies, waits for them, and re-layouts  11.6 us
    all_to_all x1, waiting for transfers between devices, across(): return lax.all_to_all(array, 'seq', split_axis=0, concat_axis=0, tiled=True)  8.04 us
    all_to_all x1, starting transfers between devices, across(): return lax.all_to_all(array, 'seq', split_axis=0, concat_axis=0, tiled=True)  7.6 us
  transfers between devices with their start and end apart: 20, of which 15 were waited for; matrix products, arithmetic and copies ran while one was open for 2% of the time, Pallas kernels for 7%

profile of v1, /device:TPU:1, one launch (start us, length us, event | category | flops | bytes accessed | tf_op | source)
XLA Modules:
  0.0 196.9 jit_solution(7193658147431057587)
XLA Ops:
  8.6 2.1 %copy-done = bf16[2,1152,3,288]{1,3,2,0:T(8,128)(2,1)S(1)} copy-done((bf16[2,1152,3,288]{1,3,2,0:T(8,128)(2,1)S(1)}, bf16[2,1152,3,288]{1,3,2,0:T(8,128)(2,1)}, u32[]{:S(2)}) %copy-start) | copy-done | bytes 3981336
  10.7 1.3 copy-done.3
  12.0 1.1 copy-done.6
  13.1 4.1 %shard_map.86 = (bf16[64,1152]{1,0:T(8,128)(2,1)S(1)}, bf16[64,1152]{1,0:T(8,128)(2,1)S(1)}, bf16[64,1152]{1,0:T(8,128)(2,1)S(1)}, bf16[64,1152]{1,0:T(8,128)(2,...) custom-call(s32[1]{0:T(128)} %bitcast.me_ref, bf16[256,1152]{1,0:T(8,128)(2,1)S(1)} %bitcast.30, ...), custom_call_target="tpu_custom_call" | custom-call | flops 1000000000 | bytes 3000000 | tf_op jit(solution)/shard_map/pallas_call | solution.py:189
  17.2 3.9 %collective-permute-start = (bf16[64,1152]{1,0:T(8,128)(2,1)S(1)}, bf16[64,1152]{1,0:T(8,128)(2,1)S(1)}, u32[]{:S(2)}, u32[]{:S(2)}) collective-permute-start(bf16[64,1152]{1,0:T(8,128)(2,1)S(1)} %get-tuple-element.26), channel_id=1, source_target_pairs={{0,1},{1,2},{2,3},{3,0},{4,5},{5,6},{6,7},{7,4},{8,9},{9,10},{10,1... | collective-permute-start | bytes 442376 | tf_op jit(solution)/shard_map/ppermute | solution.py:205
  21.1 5.1 %collective-permute-start.1 = (bf16[64,1152]{1,0:T(8,128)(2,1)S(1)}, bf16[64,1152]{1,0:T(8,128)(2,1)S(1)}, u32[]{:S(2)}, u32[]{:S(2)}) collective-permute-start(bf16[64,1152]{1,0:T(8,128)(2,1)S(1)} %get-tuple-element.27), channel_id=1, source_target_pairs={{0,2},{1,3},{2,0},{3,1},{4,6},{5,7},{6,4},{7,5},{8,10},{9,11},{10,... | collective-permute-start | bytes 442376 | tf_op jit(solution)/shard_map/ppermute | solution.py:205
  26.2 2.4 %collective-permute-start.2 = (bf16[64,1152]{1,0:T(8,128)(2,1)S(1)}, bf16[64,1152]{1,0:T(8,128)(2,1)S(1)}, u32[]{:S(2)}, u32[]{:S(2)}) collective-permute-start(bf16[64,1152]{1,0:T(8,128)(2,1)S(1)} %get-tuple-element.28), channel_id=1, source_target_pairs={{0,3},{1,0},{2,1},{3,2},{4,7},{5,4},{6,5},{7,6},{8,11},{9,8},{10,9... | collective-permute-start | bytes 442376 | tf_op jit(solution)/shard_map/ppermute | solution.py:205
  28.6 7.3 %collective-permute-done.1.p2 = bf16[64,1152]{1,0:T(8,128)(2,1)S(1)} collective-permute-done((bf16[64,1152]{1,0:T(8,128)(2,1)S(1)}, bf16[64,1152]{1,0:T(8,128)(2,1)S(1)}, u32[]{:S(2)}, u32[]{:S(2)}) %collective-permute-start.1) | collective-permute-done | bytes 147488 | tf_op jit(solution)/shard_map/ppermute | solution.py:205
  35.8 4.7 %collective-permute-done.2.p3 = bf16[64,1152]{1,0:T(8,128)(2,1)S(1)} collective-permute-done((bf16[64,1152]{1,0:T(8,128)(2,1)S(1)}, bf16[64,1152]{1,0:T(8,128)(2,1)S(1)}, u32[]{:S(2)}, u32[]{:S(2)}) %collective-permute-start.2) | collective-permute-done | bytes 147488 | tf_op jit(solution)/shard_map/ppermute | solution.py:205
  42.0 16.6 %all_to_all.22 = bf16[64,2,576]{2,1,0:T(2,128)(2,1)S(1)} all-to-all(bf16[64,2,576]{2,1,0:T(2,128)(2,1)S(1)} %reshape.35), channel_id=1, replica_groups=mesh['seq'=64,'tp'=4] {'seq'}, dimensions={0} | all-to-all | bytes 294912 | tf_op jit(solution)/shard_map/all_to_all | solution.py:209
  58.9 1.4 collective-permute-start.5
  60.3 2.2 %collective-permute-start.4 = (bf16[64,1152]{1,0:T(8,128)(2,1)S(1)}, bf16[64,1152]{1,0:T(8,128)(2,1)S(1)}, u32[]{:S(2)}, u32[]{:S(2)}) collective-permute-start(bf16[64,1152]{1,0:T(8,128)(2,1)S(1)} %bitcast.19), channel_id=1, source_target_pairs={{0,3},{1,0},{2,1},{3,2},{4,7},{5,4},{6,5},{7,6},{8,11},{9,8},{10,9... | collective-permute-start | bytes 442376 | tf_op jit(solution)/shard_map/ppermute | solution.py:205
  62.6 4.0 %collective-permute-start.3 = (bf16[64,1152]{1,0:T(8,128)(2,1)S(1)}, bf16[64,1152]{1,0:T(8,128)(2,1)S(1)}, u32[]{:S(2)}, u32[]{:S(2)}) collective-permute-start(bf16[64,1152]{1,0:T(8,128)(2,1)S(1)} %bitcast.20), channel_id=1, source_target_pairs={{0,2},{1,3},{2,0},{3,1},{4,6},{5,7},{6,4},{7,5},{8,10},{9,11},{10,... | collective-permute-start | bytes 442376 | tf_op jit(solution)/shard_map/ppermute | solution.py:205
  66.5 2.1 %copy-done.1 = bf16[2,1152,3,288]{1,3,2,0:T(8,128)(2,1)S(1)} copy-done((bf16[2,1152,3,288]{1,3,2,0:T(8,128)(2,1)S(1)}, bf16[2,1152,3,288]{1,3,2,0:T(8,128)(2,1)}, u32[]{:S(2)}) %copy-start.1) | copy-done | bytes 3981336
  68.7 3.3 %shard_map.88 = (bf16[64,1152]{1,0:T(8,128)(2,1)S(1)}, bf16[4,64,1152]{2,1,0:T(8,128)(2,1)}, bf16[4,64,1152]{2,1,0:T(8,128)(2,1)S(1)}) custom-call(s32[1]{0:T(128)} %bitcast.me_ref, bf16[64,1152]{1,0:T(8,128)(2,1)S(1)} %bitcast.21, bf16[4,64,1152]{2,1,0:T(8,128)(2,1)S(1)} %copy-done.5, bf16[2,3,288,1152]{3,2,1,0:T(8,128)(2,1)S(1)} %bitcast.13, ...), custom_call_target="tpu_custom_call" | custom-call | flops 500000000 | bytes 3000000 | tf_op jit(solution)/shard_map/pallas_call | solution.py:189
  71.9 3.3 %shard_map.89 = (bf16[64,1152]{1,0:T(8,128)(2,1)S(1)}, bf16[4,64,1152]{2,1,0:T(8,128)(2,1)}, bf16[4,64,1152]{2,1,0:T(8,128)(2,1)S(1)}) custom-call(s32[1]{0:T(128)} %bitcast.me_ref, bf16[64,1152]{1,0:T(8,128)(2,1)S(1)} %collective-permute-done.5.m_ref, bf16[4,64,1152]{2,1,0:T(8,128)(2,1)S(1)} %copy-done.5, ...), custom_call_target="tpu_custom_call", output_to_operand_aliasing={{1}: (8, {}), {2}: (9, {})} | custom-call | flops 500000000 | bytes 3000000 | tf_op jit(solution)/shard_map/pallas_call | solution.py:189
  75.2 3.3 %shard_map.90 = (bf16[64,1152]{1,0:T(8,128)(2,1)S(1)}, bf16[4,64,1152]{2,1,0:T(8,128)(2,1)}, bf16[4,64,1152]{2,1,0:T(8,128)(2,1)S(1)}) custom-call(s32[1]{0:T(128)} %bitcast.me_ref, bf16[64,1152]{1,0:T(8,128)(2,1)S(1)} %collective-permute-done.4.m_ref, bf16[4,64,1152]{2,1,0:T(8,128)(2,1)S(1)} %copy-done.5, ...), custom_call_target="tpu_custom_call", output_to_operand_aliasing={{1}: (8, {}), {2}: (9, {})} | custom-call | flops 500000000 | bytes 3000000 | tf_op jit(solution)/shard_map/pallas_call | solution.py:189
  78.5 3.3 %shard_map.91 = (bf16[64,1152]{1,0:T(8,128)(2,1)S(1)}, bf16[4,64,1152]{2,1,0:T(8,128)(2,1)}, bf16[4,64,1152]{2,1,0:T(8,128)(2,1)S(1)}) custom-call(s32[1]{0:T(128)} %bitcast.me_ref, bf16[64,1152]{1,0:T(8,128)(2,1)S(1)} %collective-permute-done.3.m_ref, bf16[4,64,1152]{2,1,0:T(8,128)(2,1)S(1)} %copy-done.5, ...), custom_call_target="tpu_custom_call", output_to_operand_aliasing={{1}: (8, {}), {2}: (9, {})} | custom-call | flops 500000000 | bytes 3000000 | tf_op jit(solution)/shard_map/pallas_call | solution.py:189
  81.7 2.7 %collective-permute-start.7 = (bf16[64,1152]{1,0:T(8,128)(2,1)S(1)}, bf16[64,1152]{1,0:T(8,128)(2,1)S(1)}, u32[]{:S(2)}, u32[]{:S(2)}) collective-permute-start(bf16[64,1152]{1,0:T(8,128)(2,1)S(1)} %get-tuple-element.39), channel_id=1, source_target_pairs={{0,2},{1,3},{2,0},{3,1},{4,6},{5,7},{6,4},{7,5},{8,10},{9,11},{10,... | collective-permute-start | bytes 442376 | tf_op jit(solution)/shard_map/ppermute | solution.py:205
  84.4 1.4 collective-permute-start.8
  85.7 2.2 %collective-permute-start.6 = (bf16[64,1152]{1,0:T(8,128)(2,1)S(1)}, bf16[64,1152]{1,0:T(8,128)(2,1)S(1)}, u32[]{:S(2)}, u32[]{:S(2)}) collective-permute-start(bf16[64,1152]{1,0:T(8,128)(2,1)S(1)} %get-tuple-element.38), channel_id=1, source_target_pairs={{0,3},{1,0},{2,1},{3,2},{4,7},{5,4},{6,5},{7,6},{8,11},{9,8},{10,9... | collective-permute-start | bytes 442376 | tf_op jit(solution)/shard_map/ppermute | solution.py:205
  88.0 2.0 collective-permute-done.7.refs_4_
  89.9 8.0 %collective-permute-done.8.refs_5_ = bf16[64,1152]{1,0:T(8,128)(2,1)S(1)} collective-permute-done((bf16[64,1152]{1,0:T(8,128)(2,1)S(1)}, bf16[64,1152]{1,0:T(8,128)(2,1)S(1)}, u32[]{:S(2)}, u32[]{:S(2)}) %collective-permute-start.8) | collective-permute-done | bytes 147488 | tf_op jit(solution)/shard_map/ppermute | solution.py:205
  100.5 7.6 %all-to-all-start.1 = ((bf16[64,2,576]{2,1,0:T(2,128)(2,1)}), bf16[64,2,576]{2,1,0:T(2,128)(2,1)}, u32[]{:S(2)}, u32[]{:S(2)}) async-start(bf16[64,2,576]{2,1,0:T(2,128)(2,1)} %reshape.37), calls=%async_computation.1 | async-start | bytes 327680 | tf_op jit(solution)/shard_map/all_to_all | solution.py:209
  108.8 8.0 %all-to-all-done.1 = bf16[64,2,576]{2,1,0:T(2,128)(2,1)} async-done(((bf16[64,2,576]{2,1,0:T(2,128)(2,1)}), bf16[64,2,576]{2,1,0:T(2,128)(2,1)}, u32[]{:S(2)}, u32[]{:S(2)}) %all-to-all-start.1) | async-done | bytes 147488 | tf_op jit(solution)/shard_map/all_to_all | solution.py:209
  116.9 1.5 reshape.38
  118.5 2.4 %collective-permute-start.10 = (bf16[64,1152]{1,0:T(8,128)(2,1)S(1)}, bf16[64,1152]{1,0:T(8,128)(2,1)S(1)}, u32[]{:S(2)}, u32[]{:S(2)}) collective-permute-start(bf16[64,1152]{1,0:T(8,128)(2,1)S(1)} %bitcast.23), channel_id=1, source_target_pairs={{0,2},{1,3},{2,0},{3,1},{4,6},{5,7},{6,4},{7,5},{8,10},{9,11},{10,... | collective-permute-start | bytes 442376 | tf_op jit(solution)/shard_map/ppermute | solution.py:205
  120.8 1.2 collective-permute-start.11
  122.0 2.4 %collective-permute-start.9 = (bf16[64,1152]{1,0:T(8,128)(2,1)S(1)}, bf16[64,1152]{1,0:T(8,128)(2,1)S(1)}, u32[]{:S(2)}, u32[]{:S(2)}) collective-permute-start(bf16[64,1152]{1,0:T(8,128)(2,1)S(1)} %bitcast.25), channel_id=1, source_target_pairs={{0,3},{1,0},{2,1},{3,2},{4,7},{5,4},{6,5},{7,6},{8,11},{9,8},{10,9... | collective-permute-start | bytes 442376 | tf_op jit(solution)/shard_map/ppermute | solution.py:205
  124.4 6.4 %collective-permute-done.10.g2 = bf16[64,1152]{1,0:T(8,128)(2,1)S(1)} collective-permute-done((bf16[64,1152]{1,0:T(8,128)(2,1)S(1)}, bf16[64,1152]{1,0:T(8,128)(2,1)S(1)}, u32[]{:S(2)}, u32[]{:S(2)}) %collective-permute-start.10) | collective-permute-done | bytes 147488 | tf_op jit(solution)/shard_map/ppermute | solution.py:205
  130.8 3.6 %collective-permute-done.11.g3 = bf16[64,1152]{1,0:T(8,128)(2,1)S(1)} collective-permute-done((bf16[64,1152]{1,0:T(8,128)(2,1)S(1)}, bf16[64,1152]{1,0:T(8,128)(2,1)S(1)}, u32[]{:S(2)}, u32[]{:S(2)}) %collective-permute-start.11) | collective-permute-done | bytes 147488 | tf_op jit(solution)/shard_map/ppermute | solution.py:205
  134.4 5.0 %collective-permute-done.9.g1 = bf16[64,1152]{1,0:T(8,128)(2,1)S(1)} collective-permute-done((bf16[64,1152]{1,0:T(8,128)(2,1)S(1)}, bf16[64,1152]{1,0:T(8,128)(2,1)S(1)}, u32[]{:S(2)}, u32[]{:S(2)}) %collective-permute-start.9) | collective-permute-done | bytes 147488 | tf_op jit(solution)/shard_map/ppermute | solution.py:205
  139.4 2.1 %copy-done.2 = bf16[2,1152,3,288]{1,3,2,0:T(8,128)(2,1)S(1)} copy-done((bf16[2,1152,3,288]{1,3,2,0:T(8,128)(2,1)S(1)}, bf16[2,1152,3,288]{1,3,2,0:T(8,128)(2,1)}, u32[]{:S(2)}) %copy-start.2) | copy-done | bytes 3981336
  141.5 4.1 %shard_map.93 = (bf16[64,1152]{1,0:T(8,128)(2,1)S(1)}, bf16[64,1152]{1,0:T(8,128)(2,1)S(1)}, bf16[64,1152]{1,0:T(8,128)(2,1)S(1)}, bf16[64,1152]{1,0:T(8,128)(2,1)S(1)}) custom-call(bf16[64,1152]{1,0:T(8,128)(2,1)S(1)} %bitcast.26, bf16[64,1152]{1,0:T(8,128)(2,1)S(1)} %collective-permute-done.9.g1, bf16[64,1152]{1,0:T(8,128)(2,1)S(1)} %collective-permute-done.10.g2, ...), custom_call_target="tpu_custom_call" | custom-call | flops 1500000000 | bytes 3000000 | tf_op jit(solution)/shard_map/pallas_call | solution.py:189
  145.6 3.7 %collective-permute-start.12 = (bf16[64,1152]{1,0:T(8,128)(2,1)S(1)}, bf16[64,1152]{1,0:T(8,128)(2,1)S(1)}, u32[]{:S(2)}, u32[]{:S(2)}) collective-permute-start(bf16[64,1152]{1,0:T(8,128)(2,1)S(1)} %get-tuple-element.43), channel_id=1, source_target_pairs={{0,1},{1,2},{2,3},{3,0},{4,5},{5,6},{6,7},{7,4},{8,9},{9,10},{10,1... | collective-permute-start | bytes 442376 | tf_op jit(solution)/shard_map/ppermute | solution.py:205
  149.3 1.8 collective-permute-start.13
  151.0 1.6 collective-permute-start.14
  152.7 1.3 collective-permute-done.12.p1
  154.0 9.3 %collective-permute-done.13.p2 = bf16[64,1152]{1,0:T(8,128)(2,1)S(1)} collective-permute-done((bf16[64,1152]{1,0:T(8,128)(2,1)S(1)}, bf16[64,1152]{1,0:T(8,128)(2,1)S(1)}, u32[]{:S(2)}, u32[]{:S(2)}) %collective-permute-start.13) | collective-permute-done | bytes 147488 | tf_op jit(solution)/shard_map/ppermute | solution.py:205
  163.3 7.2 %collective-permute-done.14.p3 = bf16[64,1152]{1,0:T(8,128)(2,1)S(1)} collective-permute-done((bf16[64,1152]{1,0:T(8,128)(2,1)S(1)}, bf16[64,1152]{1,0:T(8,128)(2,1)S(1)}, u32[]{:S(2)}, u32[]{:S(2)}) %collective-permute-start.14) | collective-permute-done | bytes 147488 | tf_op jit(solution)/shard_map/ppermute | solution.py:205
  170.8 1.6 collective-permute-start.15
  172.4 3.5 %collective-permute-start.16 = (bf16[64,1152]{1,0:T(8,128)(2,1)S(1)}, bf16[64,1152]{1,0:T(8,128)(2,1)S(1)}, u32[]{:S(2)}, u32[]{:S(2)}) collective-permute-start(bf16[64,1152]{1,0:T(8,128)(2,1)S(1)} %shard_map.94.g0), channel_id=1, source_target_pairs={{0,2},{1,3},{2,0},{3,1},{4,6},{5,7},{6,4},{7,5},{8,10},{9,11},{10,... | collective-permute-start | bytes 442376 | tf_op jit(solution)/shard_map/ppermute | solution.py:205
  175.9 2.3 %collective-permute-start.17 = (bf16[64,1152]{1,0:T(8,128)(2,1)S(1)}, bf16[64,1152]{1,0:T(8,128)(2,1)S(1)}, u32[]{:S(2)}, u32[]{:S(2)}) collective-permute-start(bf16[64,1152]{1,0:T(8,128)(2,1)S(1)} %shard_map.94.g0), channel_id=1, source_target_pairs={{0,1},{1,2},{2,3},{3,0},{4,5},{5,6},{6,7},{7,4},{8,9},{9,10},{10,1... | collective-permute-start | bytes 442376 | tf_op jit(solution)/shard_map/ppermute | solution.py:205
  178.2 3.7 %all-reduce.2.cloned.1.call-done = bf16[4,64,1152]{2,1,0:T(8,128)(2,1)} async-done(((bf16[4,64,1152]{2,1,0:T(8,128)(2,1)}), bf16[4,64,1152]{2,1,0:T(8,128)(2,1)}) %all-reduce.2.cloned.1.call-update) | async-done | bytes 589840 | tf_op jit(solution)/shard_map/psum | solution.py:259
  181.9 2.1 %add_convert_fusion = bf16[4,64,1152]{2,1,0:T(8,128)(2,1)} fusion(bf16[4,64,1152]{2,1,0:T(8,128)(2,1)} %all-reduce.2.cloned.1.call-done, bf16[4,64,1152]{2,1,0:T(8,128)(2,1)S(1)} %get-tuple-element.35, f32[1152]{0:T(1024)S(1)} %slice_reduce_fusion), kind=kLoop, calls=%fused_computation | loop fusion | flops 1474560 | bytes 1774080 | tf_op jit(solution)/shard_map/convert_element_type | solution.py:260
  184.0 1.6 collective-permute-done.15.g1
  185.6 3.2 %collective-permute-done.17.g3 = bf16[64,1152]{1,0:T(8,128)(2,1)S(1)} collective-permute-done((bf16[64,1152]{1,0:T(8,128)(2,1)S(1)}, bf16[64,1152]{1,0:T(8,128)(2,1)S(1)}, u32[]{:S(2)}, u32[]{:S(2)}) %collective-permute-start.17) | collective-permute-done | bytes 147488 | tf_op jit(solution)/shard_map/ppermute | solution.py:205
  188.8 1.3 shard_map.95
  (34 shorter events, 6.9 us)
Async XLA Ops:
  8.6 2.1 %copy-start = (bf16[2,1152,3,288]{1,3,2,0:T(8,128)(2,1)S(1)}, bf16[2,1152,3,288]{1,3,2,0:T(8,128)(2,1)}, u32[]{:S(2)}) copy-start(bf16[2,1152,3,288]{1,3,2,0:T(8,128)(2,1)} %param.9) | copy-start | bytes 11943940
  10.7 1.3 copy-start.3
  12.0 1.1 copy-start.6
  13.1 15.5 %copy-start.7 = (f32[2,1152]{1,0:T(2,128)S(1)}, f32[2,1152]{1,0:T(2,128)}, u32[]{:S(2)}) copy-start(f32[2,1152]{1,0:T(2,128)} %param.13) | copy-start | bytes 27652
  17.2 11.4 %collective-permute-start = (bf16[64,1152]{1,0:T(8,128)(2,1)S(1)}, bf16[64,1152]{1,0:T(8,128)(2,1)S(1)}, u32[]{:S(2)}, u32[]{:S(2)}) collective-permute-start(bf16[64,1152]{1,0:T(8,128)(2,1)S(1)} %get-tuple-element.26), channel_id=1, source_target_pairs={{0,1},{1,2},{2,3},{3,0},{4,5},{5,6},{6,7},{7,4},{8,9},{9,10},{10,1... | collective-permute-start | bytes 442376 | tf_op jit(solution)/shard_map/ppermute | solution.py:205
  21.1 14.8 %collective-permute-start.1 = (bf16[64,1152]{1,0:T(8,128)(2,1)S(1)}, bf16[64,1152]{1,0:T(8,128)(2,1)S(1)}, u32[]{:S(2)}, u32[]{:S(2)}) collective-permute-start(bf16[64,1152]{1,0:T(8,128)(2,1)S(1)} %get-tuple-element.27), channel_id=1, source_target_pairs={{0,2},{1,3},{2,0},{3,1},{4,6},{5,7},{6,4},{7,5},{8,10},{9,11},{10,... | collective-permute-start | bytes 442376 | tf_op jit(solution)/shard_map/ppermute | solution.py:205
  26.2 14.3 %collective-permute-start.2 = (bf16[64,1152]{1,0:T(8,128)(2,1)S(1)}, bf16[64,1152]{1,0:T(8,128)(2,1)S(1)}, u32[]{:S(2)}, u32[]{:S(2)}) collective-permute-start(bf16[64,1152]{1,0:T(8,128)(2,1)S(1)} %get-tuple-element.28), channel_id=1, source_target_pairs={{0,3},{1,0},{2,1},{3,2},{4,7},{5,4},{6,5},{7,6},{8,11},{9,8},{10,9... | collective-permute-start | bytes 442376 | tf_op jit(solution)/shard_map/ppermute | solution.py:205
  40.5 26.0 %copy-start.4 = (bf16[2,288,1152]{2,1,0:T(8,128)(2,1)S(1)}, bf16[2,288,1152]{2,1,0:T(8,128)(2,1)}, u32[]{:S(2)}) copy-start(bf16[2,288,1152]{2,1,0:T(8,128)(2,1)} %ow_ref.11) | copy-start | bytes 3981316
  40.5 26.0 %copy-start.5 = (bf16[4,64,1152]{2,1,0:T(8,128)(2,1)S(1)}, bf16[4,64,1152]{2,1,0:T(8,128)(2,1)}, u32[]{:S(2)}) copy-start(bf16[4,64,1152]{2,1,0:T(8,128)(2,1)} %refs_1_.1) | copy-start | bytes 1769476
  58.9 13.0 %collective-permute-start.5 = (bf16[64,1152]{1,0:T(8,128)(2,1)S(1)}, bf16[64,1152]{1,0:T(8,128)(2,1)S(1)}, u32[]{:S(2)}, u32[]{:S(2)}) collective-permute-start(bf16[64,1152]{1,0:T(8,128)(2,1)S(1)} %bitcast.18), channel_id=1, source_target_pairs={{0,1},{1,2},{2,3},{3,0},{4,5},{5,6},{6,7},{7,4},{8,9},{9,10},{10,1... | collective-permute-start | bytes 442376 | tf_op jit(solution)/shard_map/ppermute | solution.py:205
  60.3 14.9 %collective-permute-start.4 = (bf16[64,1152]{1,0:T(8,128)(2,1)S(1)}, bf16[64,1152]{1,0:T(8,128)(2,1)S(1)}, u32[]{:S(2)}, u32[]{:S(2)}) collective-permute-start(bf16[64,1152]{1,0:T(8,128)(2,1)S(1)} %bitcast.19), channel_id=1, source_target_pairs={{0,3},{1,0},{2,1},{3,2},{4,7},{5,4},{6,5},{7,6},{8,11},{9,8},{10,9... | collective-permute-start | bytes 442376 | tf_op jit(solution)/shard_map/ppermute | solution.py:205
  62.6 15.9 %collective-permute-start.3 = (bf16[64,1152]{1,0:T(8,128)(2,1)S(1)}, bf16[64,1152]{1,0:T(8,128)(2,1)S(1)}, u32[]{:S(2)}, u32[]{:S(2)}) collective-permute-start(bf16[64,1152]{1,0:T(8,128)(2,1)S(1)} %bitcast.20), channel_id=1, source_target_pairs={{0,2},{1,3},{2,0},{3,1},{4,6},{5,7},{6,4},{7,5},{8,10},{9,11},{10,... | collective-permute-start | bytes 442376 | tf_op jit(solution)/shard_map/ppermute | solution.py:205
  66.5 2.1 %copy-start.1 = (bf16[2,1152,3,288]{1,3,2,0:T(8,128)(2,1)S(1)}, bf16[2,1152,3,288]{1,3,2,0:T(8,128)(2,1)}, u32[]{:S(2)}) copy-start(bf16[2,1152,3,288]{1,3,2,0:T(8,128)(2,1)} %param.9) | copy-start | bytes 11943940
  81.7 8.2 %collective-permute-start.7 = (bf16[64,1152]{1,0:T(8,128)(2,1)S(1)}, bf16[64,1152]{1,0:T(8,128)(2,1)S(1)}, u32[]{:S(2)}, u32[]{:S(2)}) collective-permute-start(bf16[64,1152]{1,0:T(8,128)(2,1)S(1)} %get-tuple-element.39), channel_id=1, source_target_pairs={{0,2},{1,3},{2,0},{3,1},{4,6},{5,7},{6,4},{7,5},{8,10},{9,11},{10,... | collective-permute-start | bytes 442376 | tf_op jit(solution)/shard_map/ppermute | solution.py:205
  84.4 13.6 %collective-permute-start.8 = (bf16[64,1152]{1,0:T(8,128)(2,1)S(1)}, bf16[64,1152]{1,0:T(8,128)(2,1)S(1)}, u32[]{:S(2)}, u32[]{:S(2)}) collective-permute-start(bf16[64,1152]{1,0:T(8,128)(2,1)S(1)} %get-tuple-element.40), channel_id=1, source_target_pairs={{0,1},{1,2},{2,3},{3,0},{4,5},{5,6},{6,7},{7,4},{8,9},{9,10},{10,1... | collective-permute-start | bytes 442376 | tf_op jit(solution)/shard_map/ppermute | solution.py:205
  85.7 12.8 %collective-permute-start.6 = (bf16[64,1152]{1,0:T(8,128)(2,1)S(1)}, bf16[64,1152]{1,0:T(8,128)(2,1)S(1)}, u32[]{:S(2)}, u32[]{:S(2)}) collective-permute-start(bf16[64,1152]{1,0:T(8,128)(2,1)S(1)} %get-tuple-element.38), channel_id=1, source_target_pairs={{0,3},{1,0},{2,1},{3,2},{4,7},{5,4},{6,5},{7,6},{8,11},{9,8},{10,9... | collective-permute-start | bytes 442376 | tf_op jit(solution)/shard_map/ppermute | solution.py:205
  100.5 16.4 %all-to-all-start.1 = ((bf16[64,2,576]{2,1,0:T(2,128)(2,1)}), bf16[64,2,576]{2,1,0:T(2,128)(2,1)}, u32[]{:S(2)}, u32[]{:S(2)}) async-start(bf16[64,2,576]{2,1,0:T(2,128)(2,1)} %reshape.37), calls=%async_computation.1 | async-start | bytes 327680 | tf_op jit(solution)/shard_map/all_to_all | solution.py:209
  108.1 73.8 %all-reduce.2.cloned.1.call-start = ((), (), s32[]{:S(2)}) async-start(), calls=%async_computation.2 | async-start | bytes 1179648 | tf_op jit(solution)/shard_map/psum | solution.py:259
  118.5 12.4 %collective-permute-start.10 = (bf16[64,1152]{1,0:T(8,128)(2,1)S(1)}, bf16[64,1152]{1,0:T(8,128)(2,1)S(1)}, u32[]{:S(2)}, u32[]{:S(2)}) collective-permute-start(bf16[64,1152]{1,0:T(8,128)(2,1)S(1)} %bitcast.23), channel_id=1, source_target_pairs={{0,2},{1,3},{2,0},{3,1},{4,6},{5,7},{6,4},{7,5},{8,10},{9,11},{10,... | collective-permute-start | bytes 442376 | tf_op jit(solution)/shard_map/ppermute | solution.py:205
  120.8 13.6 %collective-permute-start.11 = (bf16[64,1152]{1,0:T(8,128)(2,1)S(1)}, bf16[64,1152]{1,0:T(8,128)(2,1)S(1)}, u32[]{:S(2)}, u32[]{:S(2)}) collective-permute-start(bf16[64,1152]{1,0:T(8,128)(2,1)S(1)} %bitcast.24), channel_id=1, source_target_pairs={{0,1},{1,2},{2,3},{3,0},{4,5},{5,6},{6,7},{7,4},{8,9},{9,10},{10,1... | collective-permute-start | bytes 442376 | tf_op jit(solution)/shard_map/ppermute | solution.py:205
  122.0 17.4 %collective-permute-start.9 = (bf16[64,1152]{1,0:T(8,128)(2,1)S(1)}, bf16[64,1152]{1,0:T(8,128)(2,1)S(1)}, u32[]{:S(2)}, u32[]{:S(2)}) collective-permute-start(bf16[64,1152]{1,0:T(8,128)(2,1)S(1)} %bitcast.25), channel_id=1, source_target_pairs={{0,3},{1,0},{2,1},{3,2},{4,7},{5,4},{6,5},{7,6},{8,11},{9,8},{10,9... | collective-permute-start | bytes 442376 | tf_op jit(solution)/shard_map/ppermute | solution.py:205
  139.4 2.1 %copy-start.2 = (bf16[2,1152,3,288]{1,3,2,0:T(8,128)(2,1)S(1)}, bf16[2,1152,3,288]{1,3,2,0:T(8,128)(2,1)}, u32[]{:S(2)}) copy-start(bf16[2,1152,3,288]{1,3,2,0:T(8,128)(2,1)} %param.9) | copy-start | bytes 11943940
  145.6 8.4 %collective-permute-start.12 = (bf16[64,1152]{1,0:T(8,128)(2,1)S(1)}, bf16[64,1152]{1,0:T(8,128)(2,1)S(1)}, u32[]{:S(2)}, u32[]{:S(2)}) collective-permute-start(bf16[64,1152]{1,0:T(8,128)(2,1)S(1)} %get-tuple-element.43), channel_id=1, source_target_pairs={{0,1},{1,2},{2,3},{3,0},{4,5},{5,6},{6,7},{7,4},{8,9},{9,10},{10,1... | collective-permute-start | bytes 442376 | tf_op jit(solution)/shard_map/ppermute | solution.py:205
  149.3 14.0 %collective-permute-start.13 = (bf16[64,1152]{1,0:T(8,128)(2,1)S(1)}, bf16[64,1152]{1,0:T(8,128)(2,1)S(1)}, u32[]{:S(2)}, u32[]{:S(2)}) collective-permute-start(bf16[64,1152]{1,0:T(8,128)(2,1)S(1)} %get-tuple-element.44), channel_id=1, source_target_pairs={{0,2},{1,3},{2,0},{3,1},{4,6},{5,7},{6,4},{7,5},{8,10},{9,11},{10,... | collective-permute-start | bytes 442376 | tf_op jit(solution)/shard_map/ppermute | solution.py:205
  151.0 19.4 %collective-permute-start.14 = (bf16[64,1152]{1,0:T(8,128)(2,1)S(1)}, bf16[64,1152]{1,0:T(8,128)(2,1)S(1)}, u32[]{:S(2)}, u32[]{:S(2)}) collective-permute-start(bf16[64,1152]{1,0:T(8,128)(2,1)S(1)} %get-tuple-element.45), channel_id=1, source_target_pairs={{0,3},{1,0},{2,1},{3,2},{4,7},{5,4},{6,5},{7,6},{8,11},{9,8},{10,9... | collective-permute-start | bytes 442376 | tf_op jit(solution)/shard_map/ppermute | solution.py:205
  170.8 14.8 %collective-permute-start.15 = (bf16[64,1152]{1,0:T(8,128)(2,1)S(1)}, bf16[64,1152]{1,0:T(8,128)(2,1)S(1)}, u32[]{:S(2)}, u32[]{:S(2)}) collective-permute-start(bf16[64,1152]{1,0:T(8,128)(2,1)S(1)} %shard_map.94.g0), channel_id=1, source_target_pairs={{0,3},{1,0},{2,1},{3,2},{4,7},{5,4},{6,5},{7,6},{8,11},{9,8},{10,9... | collective-permute-start | bytes 442376 | tf_op jit(solution)/shard_map/ppermute | solution.py:205
  172.4 13.1 %collective-permute-start.16 = (bf16[64,1152]{1,0:T(8,128)(2,1)S(1)}, bf16[64,1152]{1,0:T(8,128)(2,1)S(1)}, u32[]{:S(2)}, u32[]{:S(2)}) collective-permute-start(bf16[64,1152]{1,0:T(8,128)(2,1)S(1)} %shard_map.94.g0), channel_id=1, source_target_pairs={{0,2},{1,3},{2,0},{3,1},{4,6},{5,7},{6,4},{7,5},{8,10},{9,11},{10,... | collective-permute-start | bytes 442376 | tf_op jit(solution)/shard_map/ppermute | solution.py:205
  175.9 12.9 %collective-permute-start.17 = (bf16[64,1152]{1,0:T(8,128)(2,1)S(1)}, bf16[64,1152]{1,0:T(8,128)(2,1)S(1)}, u32[]{:S(2)}, u32[]{:S(2)}) collective-permute-start(bf16[64,1152]{1,0:T(8,128)(2,1)S(1)} %shard_map.94.g0), channel_id=1, source_target_pairs={{0,1},{1,2},{2,3},{3,0},{4,5},{5,6},{6,7},{7,4},{8,9},{9,10},{10,1... | collective-permute-start | bytes 442376 | tf_op jit(solution)/shard_map/ppermute | solution.py:205
Sparse Core Ops, SparseCore 0:
  112.2 69.6 all-reduce.1

commit v2 on v1

v2 whole, which is shorter than its diff:
```python
import math

import jax
import jax.numpy as jnp
from jax import lax
from jax.experimental import pallas as pl
from jax.experimental.pallas import tpu as pltpu
from jax.sharding import PartitionSpec as P

D = 1152
HEAD_DIM = 72
HERE = 4
GW = HERE * HEAD_DIM
N_TP = 4
ROWS = 64
HALF = 32
INV_ROOT = 1.0 / math.sqrt(HEAD_DIM)
F32 = jnp.float32
BF16 = jnp.bfloat16


def nn(a, b):
    return lax.dot_general(a, b, (((1,), (0,)), ((), ())), preferred_element_type=F32)


def nt(a, b):
    return lax.dot_general(a, b, (((1,), (1,)), ((), ())), preferred_element_type=F32)


def tn(a, b):
    return lax.dot_general(a, b, (((0,), (0,)), ((), ())), preferred_element_type=F32)


def normalize(tokens):
    widened = tokens.astype(F32)
    center = widened - jnp.mean(widened, axis=-1, keepdims=True)
    inv_std = lax.rsqrt(jnp.mean(center * center, axis=-1, keepdims=True) + 1e-06)
    return center * inv_std, inv_std


def norm_back(grad_mod, normed, inv_std, scale_row):
    grad_norm = grad_mod * (1.0 + scale_row)
    return inv_std * (
        grad_norm
        - jnp.mean(grad_norm, axis=-1, keepdims=True)
        - normed * jnp.mean(grad_norm * normed, axis=-1, keepdims=True)
    )


def softmax(scores):
    top = jnp.max(scores, axis=-1, keepdims=True)
    raised = jnp.exp(scores - top)
    return raised / jnp.sum(raised, axis=-1, keepdims=True)


def of_head(array, head):
    lane = lax.broadcasted_iota(jnp.int32, array.shape, 1)
    keep = (lane >= head * HEAD_DIM) & (lane < (head + 1) * HEAD_DIM)
    return jnp.where(keep, array, jnp.zeros_like(array))


def order_matrix(first, rows):
    place = lax.broadcasted_iota(jnp.int32, (rows, 256), 0)
    patch = lax.broadcasted_iota(jnp.int32, (rows, 256), 1)
    return (patch == 4 * (place % ROWS) + first + place // ROWS).astype(F32).astype(BF16)


def chunk_rows(chunk):
    return pl.ds(pl.multiple_of(chunk * ROWS, ROWS), ROWS)


def fetch(sources, buffers, sems):
    copies = [
        pltpu.make_async_copy(source, buffer, sems.at[i])
        for i, (source, buffer) in enumerate(zip(sources, buffers))
    ]
    for copy in copies:
        copy.start()
    return copies


def project(modded, weights):
    joined = nt(modded, weights)
    return tuple(joined[:, i * GW : (i + 1) * GW].astype(BF16) for i in range(3))


def spatial_forward(
    me_ref, x_hbm, w_hbm, ow_hbm, shift_ref, scale_ref,
    p0, p1, p2, p3, qkv_ref, own_ref, x_ref, w_ref, ow_ref, attended_ref, sems,
):
    x_copy, w_copy, ow_copy = fetch(
        (x_hbm, w_hbm.at[0], ow_hbm.at[0]), (x_ref, w_ref, ow_ref), sems
    )
    me = me_ref[0]
    x_copy.wait()
    tokens = x_ref[...]
    normed, _ = normalize(tokens)
    modded = (normed * (1.0 + scale_ref[0:1]) + shift_ref[0:1]).astype(BF16)
    modded = nn(order_matrix(0, 256), modded).astype(BF16)
    own_ref[...] = nn(order_matrix(me, ROWS), tokens).astype(BF16)
    w_copy.wait()
    queries, key_heads, value_heads = project(modded, w_ref[...])
    qkv_ref[0] = queries
    qkv_ref[1] = key_heads
    qkv_ref[2] = value_heads
    attended = jnp.zeros((256, GW), F32)
    for head in range(HERE):
        probs = softmax(nt(of_head(queries, head), key_heads) * INV_ROOT)
        attended = attended + nn(probs.astype(BF16), of_head(value_heads, head))
    ow_copy.wait()
    attended_ref[...] = nn(attended.astype(BF16), ow_ref[...]).astype(BF16)
    for k, part in enumerate((p0, p1, p2, p3)):
        part[...] = attended_ref[chunk_rows((me + k) % 4), :]


def temporal(me_ref, m_ref, g_ref, w_ref, ow_ref, shift_ref, scale_ref, gate_ref, both_ref):
    part_ref, out_part_ref = both_ref.at[:ROWS], both_ref.at[ROWS:]
    mid = m_ref[...]
    normed, _ = normalize(mid)
    modded = (normed * (1.0 + scale_ref[1:2]) + shift_ref[1:2]).astype(BF16)
    grad_proj = (gate_ref[1:2] * g_ref[...].astype(F32)).astype(BF16)
    queries, key_heads, value_heads = project(modded, w_ref[...])

    def spread(array):
        return jnp.concatenate([of_head(array, head) for head in range(HERE)], axis=0)

    def gather_heads(array):
        total = of_head(array[:ROWS], 0)
        for head in range(1, HERE):
            total = total + of_head(array[head * ROWS : (head + 1) * ROWS], head)
        return total

    queries_4 = spread(queries)
    probs = softmax(nt(queries_4, key_heads) * INV_ROOT)
    probs_low = probs.astype(BF16)
    grad_attn_4 = spread(nt(grad_proj, ow_ref[...]).astype(BF16))
    grad_probs = nt(grad_attn_4, value_heads)
    grad_scores = (
        probs * (grad_probs - jnp.sum(probs * grad_probs, axis=-1, keepdims=True)) * INV_ROOT
    ).astype(BF16)
    grad_query = gather_heads(nn(grad_scores, key_heads))
    grad_keys = tn(grad_scores, queries_4)
    grad_values = tn(probs_low, grad_attn_4)
    joined = jnp.concatenate([grad_query, grad_keys, grad_values], axis=1).astype(BF16)
    part_ref[...] = nn(joined, w_ref[...]).astype(BF16)
    attended = gather_heads(nn(probs_low, value_heads)).astype(BF16)
    out_part_ref[...] = nn(attended, ow_ref[...]).astype(BF16)


def spatial_backward(
    me_ref, grad_ref, qkv_ref, w_ref, ow_ref, gate_ref, p0, p1, p2, p3, total_ref
):
    grad = jnp.concatenate([grad_ref[chunk] for chunk in range(4)], axis=0)
    grad_proj = (gate_ref[0:1] * grad.astype(F32)).astype(BF16)
    grad_attn = nt(grad_proj, ow_ref[...]).astype(BF16)
    queries, key_heads, value_heads = qkv_ref[0], qkv_ref[1], qkv_ref[2]
    grad_query = jnp.zeros((256, GW), F32)
    grad_keys = jnp.zeros((256, GW), F32)
    grad_values = jnp.zeros((256, GW), F32)
    for head in range(HERE):
        query = of_head(queries, head)
        grad_head = of_head(grad_attn, head)
        probs = softmax(nt(query, key_heads) * INV_ROOT)
        grad_probs = nt(grad_head, value_heads)
        grad_scores = (
            probs * (grad_probs - jnp.sum(probs * grad_probs, axis=-1, keepdims=True)) * INV_ROOT
        ).astype(BF16)
        grad_query = grad_query + nn(grad_scores, of_head(key_heads, head))
        grad_keys = grad_keys + tn(grad_scores, query)
        grad_values = grad_values + tn(probs.astype(BF16), grad_head)
    joined = jnp.concatenate([grad_query, grad_keys, grad_values], axis=1).astype(BF16)
    total_ref[...] = nn(joined, w_ref[...]).astype(BF16)
    for k, part in enumerate((p0, p1, p2, p3)):
        part[...] = total_ref[chunk_rows((me_ref[0] + k) % 4), :]


def add_in(a_ref, b_ref, sum_ref):
    sum_ref[...] = a_ref[...].astype(F32) + b_ref[...].astype(F32)


def block_out(block, x_ref, gate_ref, *refs):
    total = refs[0][...].astype(F32)
    for ref in refs[1:-1]:
        total = total + ref[...].astype(F32)
    refs[-1][...] = (x_ref[...].astype(F32) + gate_ref[block : block + 1] * total).astype(BF16)


def grad_of(block, x_ref, g_ref, scale_ref, *refs):
    total = refs[0][...].astype(F32)
    for ref in refs[1:-1]:
        total = total + ref[...].astype(F32)
    normed, inv_std = normalize(x_ref[...])
    grad = g_ref[...].astype(F32)
    back = norm_back(total, normed, inv_std, scale_ref[block : block + 1])
    refs[-1][...] = (grad + back).astype(BF16)


def pack(grad_ref, x_ref, gate_ref, *refs):
    sent_ref, later_ref = refs[-2:]
    total = refs[0][...].astype(F32)
    for ref in refs[1:-2]:
        total = total + ref[...].astype(F32)
    result = (x_ref[...].astype(F32) + gate_ref[1:2] * total).astype(BF16)
    sent_ref[:ROWS] = grad_ref[...]
    sent_ref[ROWS:] = result[:HALF]
    later_ref[...] = result[HALF:]


def pack_last(x_ref, g_ref, scale_ref, b0, b1, b2, b3, later_ref, sent_ref):
    grad_of(0, x_ref, g_ref, scale_ref, b0, b1, b2, b3, sent_ref.at[:ROWS])
    sent_ref[ROWS:] = later_ref[...]


def unpack(first_ref, last_ref, ends_ref, result_ref, grad_ref):
    stacked = jnp.concatenate([ends_ref[chunk] for chunk in range(4)], axis=0)
    grad_ref[...] = tn(order_matrix(0, 256), stacked).astype(BF16)
    result_ref[:, :HALF] = first_ref[...]
    result_ref[:, HALF:] = last_ref[...]


IN_HBM = pl.BlockSpec(memory_space=pltpu.HBM)


def whole(shape):
    return pl.BlockSpec(shape, lambda *_: (0,) * len(shape))


QUARTER = whole((ROWS, D))
VECTORS = whole((2, D))


def rows_out(dtype=BF16):
    return jax.ShapeDtypeStruct((ROWS, D), dtype)


def run(
    body, me, operands, specs, out_shape, out_specs, flops,
    aliases=None, scratch=(), mib=24, moved=0,
):
    return pl.pallas_call(
        body,
        grid_spec=pltpu.PrefetchScalarGridSpec(
            num_scalar_prefetch=0 if me is None else 1,
            grid=(1,),
            in_specs=specs,
            out_specs=out_specs,
            scratch_shapes=list(scratch),
        ),
        out_shape=out_shape,
        input_output_aliases=aliases or {},
        compiler_params=pltpu.CompilerParams(vmem_limit_bytes=mib * 1024 * 1024),
        cost_estimate=pl.CostEstimate(flops=flops, bytes_accessed=moved, transcendentals=0),
    )(*(() if me is None else (me,)), *operands)


def shift(array, k):
    return lax.ppermute(array, "tp", [(i, (i + k) % N_TP) for i in range(N_TP)])


def across(array):
    return lax.all_to_all(array, "seq", split_axis=0, concat_axis=0, tiled=True)


def weights_of(block, weights, out_weight, after):
    weights, out_weight, _ = lax.optimization_barrier((weights, out_weight, after))
    return weights[block], out_weight[block]


def per_device(tokens, grad_out, qkv_weight, out_weight, mod_shift, mod_scale, mod_gate):
    me = lax.axis_index("tp").astype(jnp.int32).reshape(1)
    tokens = tokens.reshape(256, D)
    weights = jnp.transpose(qkv_weight, (0, 2, 3, 1)).reshape(2, 3 * GW, D)
    qkv_spec = whole((3, 256, GW))

    p0, p1, p2, p3, qkv_s, own = run(
        spatial_forward,
        me,
        (tokens, weights, out_weight, mod_shift, mod_scale),
        [IN_HBM, IN_HBM, IN_HBM, VECTORS, VECTORS],
        (rows_out(),) * 4 + (jax.ShapeDtypeStruct((3, 256, GW), BF16), rows_out()),
        (QUARTER,) * 4 + (qkv_spec, QUARTER),
        1_000_000_000,
        scratch=(
            pltpu.VMEM((256, D), BF16),
            pltpu.VMEM((3 * GW, D), BF16),
            pltpu.VMEM((GW, D), BF16),
            pltpu.VMEM((256, D), BF16),
            pltpu.SemaphoreType.DMA((3,)),
        ),
        mib=58,
    )
    p1, p3, p2 = shift(p1, 1), shift(p3, 3), shift(p2, 2)
    early = run(add_in, None, (p0, p1), [QUARTER] * 2, rows_out(F32), QUARTER, 350_000_000)
    middle = run(
        lambda *refs: block_out(0, *refs),
        None, (own, mod_gate, early, p3, p2), [QUARTER, VECTORS] + [QUARTER] * 3,
        rows_out(), QUARTER, 1_000_000,
    )
    mid_own = across(middle)
    w_spec, ow_spec = whole((3 * GW, D)), whole((GW, D))
    w1, ow1 = weights_of(1, weights, out_weight, mid_own)

    mids = lax.all_gather(mid_own, "tp")
    both = jax.ShapeDtypeStruct((2 * ROWS, D), BF16)
    sent = {}
    for k in (2, 1, 3, 0):
        chunk = pl.BlockSpec((None, ROWS, D), lambda _, at, k=k: ((at[0] + 4 - k) % 4, 0, 0))
        sent[k] = run(
            temporal, me, (mids, grad_out, w1, ow1, mod_shift, mod_scale, mod_gate),
            [chunk, chunk, w_spec, ow_spec, VECTORS, VECTORS, VECTORS],
            both, whole((2 * ROWS, D)), 50_000_000 if k else 350_000_000,
        )
        if k:
            sent[k] = shift(sent[k], 4 - k)
    later = pl.BlockSpec((ROWS, D), lambda *_: (1, 0))
    total = sent[0]
    for k in (2, 1):
        total = run(
            add_in, None, (total, sent[k]), [QUARTER] * 2, rows_out(F32), QUARTER, 350_000_000
        )

    own_grad = pl.BlockSpec((None, ROWS, D), lambda _, at: (at[0], 0, 0))
    grad_patch = run(
        lambda me_ref, *refs: grad_of(1, *refs),
        me, (mid_own, grad_out, mod_scale, total, sent[3]),
        [QUARTER, own_grad, VECTORS] + [QUARTER] * 2,
        rows_out(), QUARTER, 1_000_000,
    )
    grad_own = across(grad_patch)
    w0, ow0 = weights_of(0, weights, out_weight, grad_own)
    message = jax.ShapeDtypeStruct((ROWS + HALF, D), BF16)
    half = whole((HALF, D))
    packed, result_later = run(
        pack, None, (grad_own, mid_own, mod_gate, *(sent[k] for k in range(4))),
        [QUARTER, QUARTER, VECTORS] + [later] * 4,
        (message, jax.ShapeDtypeStruct((HALF, D), BF16)),
        (whole((ROWS + HALF, D)), half), 1_000_000,
    )
    grads = lax.all_gather(packed, "tp")
    front, back = whole((4, ROWS, D)), pl.BlockSpec((4, HALF, D), lambda *_: (0, 2, 0))
    b0, b1, b2, b3 = run(
        spatial_backward, me, (grads, qkv_s, w0, ow0, mod_gate),
        [front, qkv_spec, w_spec, ow_spec, VECTORS],
        (rows_out(),) * 4, (QUARTER,) * 4, 1_500_000_000,
        scratch=(pltpu.VMEM((256, D), BF16),),
    )
    b1, b3, b2 = shift(b1, 1), shift(b3, 3), shift(b2, 2)
    packed = run(
        pack_last, None, (own, grad_own, mod_scale, b0, b1, b2, b3, result_later),
        [QUARTER] * 2 + [VECTORS] + [QUARTER] * 4 + [half],
        message, whole((ROWS + HALF, D)), 1_000_000,
    )
    ends = lax.all_gather(packed, "tp")
    result, grad_in = run(
        unpack, None, (grads, ends, ends), [back, back, front],
        (jax.ShapeDtypeStruct((4, ROWS, D), BF16), jax.ShapeDtypeStruct((256, D), BF16)),
        (whole((4, ROWS, D)), whole((256, D))), 100_000_000,
    )
    return (result, grad_in.reshape(256, 1, D))


def solution(mesh):
    in_specs = (
        P(None, "seq", None),
        P("seq", None, None),
        P(None, None, None, "tp"),
        P(None, "tp", None),
        P(),
        P(),
        P(),
    )
    out_specs = (P("seq", None, None), P(None, "seq", None))
    return jax.shard_map(
        per_device, mesh=mesh, in_specs=in_specs, out_specs=out_specs, check_vma=False
    )
```

time: 198 us -> 183 us (0.924)
  blocking collectives: 16.6 us -> 88 us
  waiting for transfers between devices: 72.5 us -> 38.1 us
  starting transfers between devices: 53.3 us -> 23.6 us
  between operations: 14.1 us -> 0.86 us
  local copies, waits for them, and re-layouts: 13.6 us -> 6.22 us
  other arithmetic: 3.44 us -> 1.38 us
    all_gather x0 -> x3, blocking collectives: none -> 53.3 us  [the longest x1 20.1 us: per_device(): grads = lax.all_gather(packed, 'tp')]
    ppermute x18 -> x9, waiting for transfers between devices: 60.1 us -> 38.1 us  [shift(): return lax.ppermute(array, 'tp', [(i, (i + k) % N_TP) for i in range(N_TP)])]
    ppermute x18 -> x9, starting transfers between devices: 45.6 us -> 23.6 us  [shift(): return lax.ppermute(array, 'tp', [(i, (i + k) % N_TP) for i in range(N_TP)])]
    all_to_all x1 -> x2, blocking collectives: 16.6 us -> 34.7 us  [across(): return lax.all_to_all(array, 'seq', split_axis=0, concat_axis=0, tiled=True)]
    all_to_all x1 -> x0, waiting for transfers between devices: 8.04 us -> none  [across(): return lax.all_to_all(array, 'seq', split_axis=0, concat_axis=0, tiled=True)]
    unnamed x22 -> x27, local copies, waits for them, and re-layouts: 11.6 us -> 3.68 us
    all_to_all x1 -> x0, starting transfers between devices: 7.6 us -> none  [across(): return lax.all_to_all(array, 'seq', split_axis=0, concat_axis=0, tiled=True)]
    psum x1 -> x0, waiting for transfers between devices: 3.71 us -> none  [per_device(): out_total = lax.psum(kept[0], 'tp').astype(F32)]
  transfers between devices with their start and end apart: 20 -> 9, of which waited for: 15 -> 7; matrix products, arithmetic and copies ran while one was open for 2% -> 0% of each run, Pallas kernels for 7% -> 5%
where the time goes in v2:
time: 183 us; the launch traced here: 182 us
  blocking collectives  88 us (48%)
  waiting for transfers between devices  38.1 us (21%)
  Pallas kernels  24.1 us (13%)
  starting transfers between devices  23.6 us (13%)
  local copies, waits for them, and re-layouts  6.22 us (3%)
    ppermute x9, waiting for transfers between devices, shift(): return lax.ppermute(array, 'tp', [(i, (i + k) % N_TP) for i in range(N_TP)])  38.1 us
    all_to_all x2, blocking collectives, across(): return lax.all_to_all(array, 'seq', split_axis=0, concat_axis=0, tiled=True)  34.7 us
    pallas_call x14, Pallas kernels, run(): pl.pallas_call(body, grid_spec=pltpu.PrefetchScalarGridSpec(num_scalar_pr...  24.1 us
    ppermute x9, starting transfers between devices, shift(): return lax.ppermute(array, 'tp', [(i, (i + k) % N_TP) for i in range(N_TP)])  23.6 us
    all_gather x1, blocking collectives, per_device(): grads = lax.all_gather(packed, 'tp')  20.1 us
    all_gather x1, blocking collectives, per_device(): ends = lax.all_gather(packed, 'tp')  18.2 us
    all_gather x1, blocking collectives, per_device(): mids = lax.all_gather(mid_own, 'tp')  15 us
    unnamed x27, local copies, waits for them, and re-layouts  3.68 us
  transfers between devices with their start and end apart: 9, of which 7 were waited for; matrix products, arithmetic and copies ran while one was open for 0% of the time, Pallas kernels for 5%

profile of v2, /device:TPU:1, one launch (start us, length us, event | category | flops | bytes accessed | tf_op | source)
XLA Modules:
  0.0 182.2 jit_solution(14906218061227760009)
XLA Ops:
  0.6 6.7 %shard_map.86 = (bf16[64,1152]{1,0:T(8,128)(2,1)}, bf16[64,1152]{1,0:T(8,128)(2,1)}, bf16[64,1152]{1,0:T(8,128)(2,1)}, bf16[64,1152]{1,0:T(8,128)(2,1)}, bf16[3,...) custom-call(s32[1]{0:T(128)} %bitcast.me_ref, bf16[256,1152]{1,0:T(8,128)(2,1)} %bitcast.42, ...), custom_call_target="tpu_custom_call" | custom-call | flops 1000000000 | tf_op jit(solution)/shard_map/pallas_call | solution.py:240
  7.4 3.9 %collective-permute-start = (bf16[64,1152]{1,0:T(8,128)(2,1)}, bf16[64,1152]{1,0:T(8,128)(2,1)S(1)}, u32[]{:S(2)}, u32[]{:S(2)}) collective-permute-start(bf16[64,1152]{1,0:T(8,128)(2,1)} %get-tuple-element.22), channel_id=1, source_target_pairs={{0,1},{1,2},{2,3},{3,0},{4,5},{5,6},{6,7},{7,4},{8,9},{9,10},{10,1... | collective-permute-start | bytes 442376 | tf_op jit(solution)/shard_map/ppermute | solution.py:257
  11.3 3.1 %collective-permute-start.1 = (bf16[64,1152]{1,0:T(8,128)(2,1)}, bf16[64,1152]{1,0:T(8,128)(2,1)S(1)}, u32[]{:S(2)}, u32[]{:S(2)}) collective-permute-start(bf16[64,1152]{1,0:T(8,128)(2,1)} %get-tuple-element.23), channel_id=1, source_target_pairs={{0,3},{1,0},{2,1},{3,2},{4,7},{5,4},{6,5},{7,6},{8,11},{9,8},{10,9... | collective-permute-start | bytes 442376 | tf_op jit(solution)/shard_map/ppermute | solution.py:257
  14.4 4.4 %collective-permute-start.2 = (bf16[64,1152]{1,0:T(8,128)(2,1)}, bf16[64,1152]{1,0:T(8,128)(2,1)S(1)}, u32[]{:S(2)}, u32[]{:S(2)}) collective-permute-start(bf16[64,1152]{1,0:T(8,128)(2,1)} %get-tuple-element.24), channel_id=1, source_target_pairs={{0,2},{1,3},{2,0},{3,1},{4,6},{5,7},{6,4},{7,5},{8,10},{9,11},{10,... | collective-permute-start | bytes 442376 | tf_op jit(solution)/shard_map/ppermute | solution.py:257
  18.8 0.9 copy-done.7
  19.7 6.4 %collective-permute-done.1.refs_3_ = bf16[64,1152]{1,0:T(8,128)(2,1)S(1)} collective-permute-done((bf16[64,1152]{1,0:T(8,128)(2,1)}, bf16[64,1152]{1,0:T(8,128)(2,1)S(1)}, u32[]{:S(2)}, u32[]{:S(2)}) %collective-permute-start.1) | collective-permute-done | bytes 147488 | tf_op jit(solution)/shard_map/ppermute | solution.py:257
  26.1 1.8 collective-permute-done.2.refs_4_
  27.8 0.9 copy-done.1
  28.8 0.1 shard_map.88
  28.8 0.5 broadcast
  29.4 0.7 reduce
  30.0 0.2 reshape.28
  30.2 21.4 %all_to_all.22 = bf16[64,2,576]{2,1,0:T(2,128)(2,1)S(1)} all-to-all(bf16[64,2,576]{2,1,0:T(2,128)(2,1)S(1)} %reshape.28), channel_id=1, replica_groups=mesh['seq'=64,'tp'=4] {'seq'}, dimensions={0} | all-to-all | bytes 294912 | tf_op jit(solution)/shard_map/all_to_all | solution.py:261
  51.7 0.2 reshape.29
  52.0 15.0 %all-gather = bf16[256,1,1152]{2,0,1:T(8,128)(2,1)S(1)} all-gather(bf16[64,1,1152]{2,0,1:T(8,128)(2,1)S(1)} %copy.14), channel_id=2, replica_groups=mesh['seq'=64,'tp'=4] {'tp'}, dimensions={0}, use_global_device_ids=true | all-gather | bytes 737280 | tf_op jit(solution)/shard_map/all_gather | solution.py:303
  67.0 0.1 slice_bitcast_fusion.3.ow_ref
  67.1 0.0 copy-start.5
  67.1 1.8 slice_bitcast_fusion.1.w_ref
  68.9 2.8 %shard_map.90 = bf16[128,1152]{1,0:T(8,128)(2,1)S(1)} custom-call(s32[1]{0:T(128)} %bitcast.me_ref, bf16[4,64,1152]{2,1,0:T(8,128)(2,1)S(1)} %bitcast.25, bf16[4,64,1152]{2,1,0:T(8,128)(2,1)S(1)} %copy-done, bf16[864,1152]{1,0:T(8,128)(2,1)S(1)} %slice_bitcast_fusion.1.w_ref, bf16[288,1152]{1,0:T(8,128)(2,1)S(1)} %slice_bitcast_fusion.3.ow_ref, ...), custom_call_target="tpu_custom_call" | custom-call | flops 50000000 | tf_op jit(solution)/shard_map/pallas_call | solution.py:240
  71.7 3.5 %collective-permute-start.3 = (bf16[128,1152]{1,0:T(8,128)(2,1)S(1)}, bf16[128,1152]{1,0:T(8,128)(2,1)S(1)}, u32[]{:S(2)}, u32[]{:S(2)}) collective-permute-start(bf16[128,1152]{1,0:T(8,128)(2,1)S(1)} %shard_map.90), channel_id=1, source_target_pairs={{0,2},{1,3},{2,0},{3,1},{4,6},{5,7},{6,4},{7,5},{8,10},{9,11},{10,... | collective-permute-start | bytes 884744 | tf_op jit(solution)/shard_map/ppermute | solution.py:257
  75.2 2.8 %shard_map.92 = bf16[128,1152]{1,0:T(8,128)(2,1)S(1)} custom-call(s32[1]{0:T(128)} %bitcast.me_ref, bf16[4,64,1152]{2,1,0:T(8,128)(2,1)S(1)} %bitcast.26, bf16[4,64,1152]{2,1,0:T(8,128)(2,1)S(1)} %copy-done, bf16[864,1152]{1,0:T(8,128)(2,1)S(1)} %slice_bitcast_fusion.1.w_ref, bf16[288,1152]{1,0:T(8,128)(2,1)S(1)} %slice_bitcast_fusion.3.ow_ref, ...), custom_call_target="tpu_custom_call" | custom-call | flops 50000000 | tf_op jit(solution)/shard_map/pallas_call | solution.py:240
  78.0 2.3 %collective-permute-start.4 = (bf16[128,1152]{1,0:T(8,128)(2,1)S(1)}, bf16[128,1152]{1,0:T(8,128)(2,1)S(1)}, u32[]{:S(2)}, u32[]{:S(2)}) collective-permute-start(bf16[128,1152]{1,0:T(8,128)(2,1)S(1)} %shard_map.92), channel_id=1, source_target_pairs={{0,3},{1,0},{2,1},{3,2},{4,7},{5,4},{6,5},{7,6},{8,11},{9,8},{10,9... | collective-permute-start | bytes 884744 | tf_op jit(solution)/shard_map/ppermute | solution.py:257
  80.2 2.8 %shard_map.94 = bf16[128,1152]{1,0:T(8,128)(2,1)S(1)} custom-call(s32[1]{0:T(128)} %bitcast.me_ref, bf16[4,64,1152]{2,1,0:T(8,128)(2,1)S(1)} %bitcast.27, bf16[4,64,1152]{2,1,0:T(8,128)(2,1)S(1)} %copy-done, bf16[864,1152]{1,0:T(8,128)(2,1)S(1)} %slice_bitcast_fusion.1.w_ref, bf16[288,1152]{1,0:T(8,128)(2,1)S(1)} %slice_bitcast_fusion.3.ow_ref, ...), custom_call_target="tpu_custom_call" | custom-call | flops 50000000 | tf_op jit(solution)/shard_map/pallas_call | solution.py:240
  83.0 0.4 collective-permute-start.5
  83.5 2.8 %shard_map.89.a_ref.refs_0_ = bf16[128,1152]{1,0:T(8,128)(2,1)S(1)} custom-call(s32[1]{0:T(128)} %bitcast.me_ref, bf16[4,64,1152]{2,1,0:T(8,128)(2,1)S(1)} %bitcast.28, bf16[4,64,1152]{2,1,0:T(8,128)(2,1)S(1)} %copy-done, bf16[864,1152]{1,0:T(8,128)(2,1)S(1)} %slice_bitcast_fusion.1.w_ref, bf16[288,1152]{1,0:T(8,128)(2,1)S(1)} %slice_bitcast_fusion.3.ow_ref, ...), custom_call_target="tpu_custom_call" | custom-call | flops 350000000 | tf_op jit(solution)/shard_map/pallas_call | solution.py:240
  86.3 15.6 %collective-permute-done.4.b_ref.refs_1_ = bf16[128,1152]{1,0:T(8,128)(2,1)S(1)} collective-permute-done((bf16[128,1152]{1,0:T(8,128)(2,1)S(1)}, bf16[128,1152]{1,0:T(8,128)(2,1)S(1)}, u32[]{:S(2)}, u32[]{:S(2)}) %collective-permute-start.4) | collective-permute-done | bytes 294944 | tf_op jit(solution)/shard_map/ppermute | solution.py:257
  102.0 1.6 collective-permute-done.5.refs_4_.refs_3_
  103.6 0.3 shard_map.95
  103.9 0.7 reduce.1
  104.6 0.2 reshape.30
  104.8 13.2 %all_to_all.23 = bf16[64,2,576]{2,1,0:T(2,128)(2,1)S(1)} all-to-all(bf16[64,2,576]{2,1,0:T(2,128)(2,1)S(1)} %reshape.30), channel_id=1, replica_groups=mesh['seq'=64,'tp'=4] {'seq'}, dimensions={0} | all-to-all | bytes 294912 | tf_op jit(solution)/shard_map/all_to_all | solution.py:261
  118.0 0.2 reshape.31
  118.3 0.0 copy-start.8
  118.3 0.1 slice_bitcast_fusion.2.ow_ref
  118.4 0.1 shard_map.96
  118.5 20.1 %all-gather.1 = bf16[384,1152]{1,0:T(8,128)(2,1)S(1)} all-gather(bf16[96,1152]{1,0:T(8,128)(2,1)S(1)} %get-tuple-element.27), channel_id=3, replica_groups=mesh['seq'=64,'tp'=4] {'tp'}, dimensions={0}, use_global_device_ids=true | all-gather | bytes 1105920 | tf_op jit(solution)/shard_map/all_gather | solution.py:339
  138.6 0.2 slice_bitcast_fusion.w_ref
  138.8 0.9 copy-done.6
  139.7 3.8 %shard_map.97 = (bf16[64,1152]{1,0:T(8,128)(2,1)S(1)}, bf16[64,1152]{1,0:T(8,128)(2,1)S(1)}, bf16[64,1152]{1,0:T(8,128)(2,1)S(1)}, bf16[64,1152]{1,0:T(8,128)(2,1)S(1)}) custom-call(s32[1]{0:T(128)} %bitcast.me_ref, bf16[4,96,1152]{2,1,0:T(8,128)(2,1)S(1)} %bitcast.31, bf16[3,256,288]{2,1,0:T(8,128)(2,1)S(1)} %copy-done.6, ...), custom_call_target="tpu_custom_call" | custom-call | flops 1500000000 | tf_op jit(solution)/shard_map/pallas_call | solution.py:240
  143.5 1.5 collective-permute-start.6
  145.0 2.8 %collective-permute-start.7 = (bf16[64,1152]{1,0:T(8,128)(2,1)S(1)}, bf16[64,1152]{1,0:T(8,128)(2,1)S(1)}, u32[]{:S(2)}, u32[]{:S(2)}) collective-permute-start(bf16[64,1152]{1,0:T(8,128)(2,1)S(1)} %get-tuple-element.33), channel_id=1, source_target_pairs={{0,2},{1,3},{2,0},{3,1},{4,6},{5,7},{6,4},{7,5},{8,10},{9,11},{10,... | collective-permute-start | bytes 442376 | tf_op jit(solution)/shard_map/ppermute | solution.py:257
  147.7 1.8 collective-permute-start.8
  149.5 0.5 collective-permute-done.6.b1
  150.0 6.6 %collective-permute-done.7.b2 = bf16[64,1152]{1,0:T(8,128)(2,1)S(1)} collective-permute-done((bf16[64,1152]{1,0:T(8,128)(2,1)S(1)}, bf16[64,1152]{1,0:T(8,128)(2,1)S(1)}, u32[]{:S(2)}, u32[]{:S(2)}) %collective-permute-start.7) | collective-permute-done | bytes 147488 | tf_op jit(solution)/shard_map/ppermute | solution.py:257
  156.7 5.6 %collective-permute-done.8.b3 = bf16[64,1152]{1,0:T(8,128)(2,1)S(1)} collective-permute-done((bf16[64,1152]{1,0:T(8,128)(2,1)S(1)}, bf16[64,1152]{1,0:T(8,128)(2,1)S(1)}, u32[]{:S(2)}, u32[]{:S(2)}) %collective-permute-start.8) | collective-permute-done | bytes 147488 | tf_op jit(solution)/shard_map/ppermute | solution.py:257
  162.3 0.4 shard_map.98
  162.6 18.2 %all-gather.2 = bf16[384,1152]{1,0:T(8,128)(2,1)S(1)} all-gather(bf16[96,1152]{1,0:T(8,128)(2,1)S(1)} %shard_map.98), channel_id=4, replica_groups=mesh['seq'=64,'tp'=4] {'tp'}, dimensions={0}, use_global_device_ids=true | all-gather | bytes 1105920 | tf_op jit(solution)/shard_map/all_gather | solution.py:353
  180.8 1.4 shard_map.99
  (23 shorter events, 0.2 us)
Async XLA Ops:
  0.6 27.2 %copy-start.4 = (f32[2,1152]{1,0:T(2,128)S(1)}, f32[2,1152]{1,0:T(2,128)}, u32[]{:S(2)}) copy-start(f32[2,1152]{1,0:T(2,128)} %gate_ref.11) | copy-start | bytes 27652
  7.4 11.4 %collective-permute-start = (bf16[64,1152]{1,0:T(8,128)(2,1)}, bf16[64,1152]{1,0:T(8,128)(2,1)S(1)}, u32[]{:S(2)}, u32[]{:S(2)}) collective-permute-start(bf16[64,1152]{1,0:T(8,128)(2,1)} %get-tuple-element.22), channel_id=1, source_target_pairs={{0,1},{1,2},{2,3},{3,0},{4,5},{5,6},{6,7},{7,4},{8,9},{9,10},{10,1... | collective-permute-start | bytes 442376 | tf_op jit(solution)/shard_map/ppermute | solution.py:257
  11.3 14.8 %collective-permute-start.1 = (bf16[64,1152]{1,0:T(8,128)(2,1)}, bf16[64,1152]{1,0:T(8,128)(2,1)S(1)}, u32[]{:S(2)}, u32[]{:S(2)}) collective-permute-start(bf16[64,1152]{1,0:T(8,128)(2,1)} %get-tuple-element.23), channel_id=1, source_target_pairs={{0,3},{1,0},{2,1},{3,2},{4,7},{5,4},{6,5},{7,6},{8,11},{9,8},{10,9... | collective-permute-start | bytes 442376 | tf_op jit(solution)/shard_map/ppermute | solution.py:257
  14.4 13.5 %collective-permute-start.2 = (bf16[64,1152]{1,0:T(8,128)(2,1)}, bf16[64,1152]{1,0:T(8,128)(2,1)S(1)}, u32[]{:S(2)}, u32[]{:S(2)}) collective-permute-start(bf16[64,1152]{1,0:T(8,128)(2,1)} %get-tuple-element.24), channel_id=1, source_target_pairs={{0,2},{1,3},{2,0},{3,1},{4,6},{5,7},{6,4},{7,5},{8,10},{9,11},{10,... | collective-permute-start | bytes 442376 | tf_op jit(solution)/shard_map/ppermute | solution.py:257
  18.7 0.9 copy-start.7
  27.8 0.9 copy-start.1
  28.8 38.2 %copy-start.9 = (bf16[2,288,1152]{2,1,0:T(8,128)(2,1)S(1)}, bf16[2,288,1152]{2,1,0:T(8,128)(2,1)}, u32[]{:S(2)}) copy-start(bf16[2,288,1152]{2,1,0:T(8,128)(2,1)} %ow_hbm.1) | copy-start | bytes 3981316
  67.1 1.8 copy-start
  67.1 1.8 copy-start.3
  67.1 1.8 copy-start.5
  71.7 14.6 %collective-permute-start.3 = (bf16[128,1152]{1,0:T(8,128)(2,1)S(1)}, bf16[128,1152]{1,0:T(8,128)(2,1)S(1)}, u32[]{:S(2)}, u32[]{:S(2)}) collective-permute-start(bf16[128,1152]{1,0:T(8,128)(2,1)S(1)} %shard_map.90), channel_id=1, source_target_pairs={{0,2},{1,3},{2,0},{3,1},{4,6},{5,7},{6,4},{7,5},{8,10},{9,11},{10,... | collective-permute-start | bytes 884744 | tf_op jit(solution)/shard_map/ppermute | solution.py:257
  78.0 23.9 %collective-permute-start.4 = (bf16[128,1152]{1,0:T(8,128)(2,1)S(1)}, bf16[128,1152]{1,0:T(8,128)(2,1)S(1)}, u32[]{:S(2)}, u32[]{:S(2)}) collective-permute-start(bf16[128,1152]{1,0:T(8,128)(2,1)S(1)} %shard_map.92), channel_id=1, source_target_pairs={{0,3},{1,0},{2,1},{3,2},{4,7},{5,4},{6,5},{7,6},{8,11},{9,8},{10,9... | collective-permute-start | bytes 884744 | tf_op jit(solution)/shard_map/ppermute | solution.py:257
  83.0 20.5 %collective-permute-start.5 = (bf16[128,1152]{1,0:T(8,128)(2,1)S(1)}, bf16[128,1152]{1,0:T(8,128)(2,1)S(1)}, u32[]{:S(2)}, u32[]{:S(2)}) collective-permute-start(bf16[128,1152]{1,0:T(8,128)(2,1)S(1)} %shard_map.94), channel_id=1, source_target_pairs={{0,1},{1,2},{2,3},{3,0},{4,5},{5,6},{6,7},{7,4},{8,9},{9,10},{10,1... | collective-permute-start | bytes 884744 | tf_op jit(solution)/shard_map/ppermute | solution.py:257
  118.3 20.4 %copy-start.8 = (bf16[2,1152,3,288]{1,3,2,0:T(8,128)(2,1)S(1)}, bf16[2,1152,3,288]{1,3,2,0:T(8,128)(2,1)}, u32[]{:S(2)}) copy-start(bf16[2,1152,3,288]{1,3,2,0:T(8,128)(2,1)} %param.9) | copy-start | bytes 11943940
  138.6 1.1 copy-start.6
  139.7 22.6 %copy-start.2 = (bf16[64,1152]{1,0:T(8,128)(2,1)S(1)}, bf16[64,1152]{1,0:T(8,128)(2,1)}, u32[]{:S(2)}) copy-start(bf16[64,1152]{1,0:T(8,128)(2,1)} %get-tuple-element.20.refs_0_.x_ref) | copy-start | bytes 442372
  143.5 6.5 %collective-permute-start.6 = (bf16[64,1152]{1,0:T(8,128)(2,1)S(1)}, bf16[64,1152]{1,0:T(8,128)(2,1)S(1)}, u32[]{:S(2)}, u32[]{:S(2)}) collective-permute-start(bf16[64,1152]{1,0:T(8,128)(2,1)S(1)} %get-tuple-element.32), channel_id=1, source_target_pairs={{0,1},{1,2},{2,3},{3,0},{4,5},{5,6},{6,7},{7,4},{8,9},{9,10},{10,1... | collective-permute-start | bytes 442376 | tf_op jit(solution)/shard_map/ppermute | solution.py:257
  145.0 11.7 %collective-permute-start.7 = (bf16[64,1152]{1,0:T(8,128)(2,1)S(1)}, bf16[64,1152]{1,0:T(8,128)(2,1)S(1)}, u32[]{:S(2)}, u32[]{:S(2)}) collective-permute-start(bf16[64,1152]{1,0:T(8,128)(2,1)S(1)} %get-tuple-element.33), channel_id=1, source_target_pairs={{0,2},{1,3},{2,0},{3,1},{4,6},{5,7},{6,4},{7,5},{8,10},{9,11},{10,... | collective-permute-start | bytes 442376 | tf_op jit(solution)/shard_map/ppermute | solution.py:257
  147.7 14.5 %collective-permute-start.8 = (bf16[64,1152]{1,0:T(8,128)(2,1)S(1)}, bf16[64,1152]{1,0:T(8,128)(2,1)S(1)}, u32[]{:S(2)}, u32[]{:S(2)}) collective-permute-start(bf16[64,1152]{1,0:T(8,128)(2,1)S(1)} %get-tuple-element.34), channel_id=1, source_target_pairs={{0,3},{1,0},{2,1},{3,2},{4,7},{5,4},{6,5},{7,6},{8,11},{9,8},{10,9... | collective-permute-start | bytes 442376 | tf_op jit(solution)/shard_map/ppermute | solution.py:257

commit v3 on v2

--- a/solution.py
+++ b/solution.py
@@ -14,6 +14,7 @@
 N_TP = 4
 ROWS = 64
 HALF = 32
+RESULT_FLOPS = 3_000_000_000
 INV_ROOT = 1.0 / math.sqrt(HEAD_DIM)
 F32 = jnp.float32
 BF16 = jnp.bfloat16
@@ -113,8 +114,7 @@
         part[...] = attended_ref[chunk_rows((me + k) % 4), :]
 
 
-def temporal(me_ref, m_ref, g_ref, w_ref, ow_ref, shift_ref, scale_ref, gate_ref, both_ref):
-    part_ref, out_part_ref = both_ref.at[:ROWS], both_ref.at[ROWS:]
+def temporal(me_ref, m_ref, g_ref, w_ref, ow_ref, shift_ref, scale_ref, gate_ref, part_ref, out_part_ref):
     mid = m_ref[...]
     normed, _ = normalize(mid)
     modded = (normed * (1.0 + scale_ref[1:2]) + shift_ref[1:2]).astype(BF16)
@@ -195,20 +195,14 @@
     refs[-1][...] = (grad + back).astype(BF16)
 
 
-def pack(grad_ref, x_ref, gate_ref, *refs):
-    sent_ref, later_ref = refs[-2:]
-    total = refs[0][...].astype(F32)
-    for ref in refs[1:-2]:
-        total = total + ref[...].astype(F32)
-    result = (x_ref[...].astype(F32) + gate_ref[1:2] * total).astype(BF16)
+def pack(grad_ref, result_ref, sent_ref):
     sent_ref[:ROWS] = grad_ref[...]
-    sent_ref[ROWS:] = result[:HALF]
-    later_ref[...] = result[HALF:]
-
-
-def pack_last(x_ref, g_ref, scale_ref, b0, b1, b2, b3, later_ref, sent_ref):
+    sent_ref[ROWS:] = result_ref[:HALF]
+
+
+def pack_last(x_ref, g_ref, scale_ref, b0, b1, b2, b3, result_ref, sent_ref):
     grad_of(0, x_ref, g_ref, scale_ref, b0, b1, b2, b3, sent_ref.at[:ROWS])
-    sent_ref[ROWS:] = later_ref[...]
+    sent_ref[ROWS:] = result_ref[HALF:]
 
 
 def unpack(first_ref, last_ref, ends_ref, result_ref, grad_ref):
@@ -301,23 +295,29 @@
     w1, ow1 = weights_of(1, weights, out_weight, mid_own)
 
     mids = lax.all_gather(mid_own, "tp")
-    both = jax.ShapeDtypeStruct((2 * ROWS, D), BF16)
-    sent = {}
+    sent, outs = {}, {}
     for k in (2, 1, 3, 0):
         chunk = pl.BlockSpec((None, ROWS, D), lambda _, at, k=k: ((at[0] + 4 - k) % 4, 0, 0))
-        sent[k] = run(
+        sent[k], outs[k] = run(
             temporal, me, (mids, grad_out, w1, ow1, mod_shift, mod_scale, mod_gate),
             [chunk, chunk, w_spec, ow_spec, VECTORS, VECTORS, VECTORS],
-            both, whole((2 * ROWS, D)), 50_000_000 if k else 350_000_000,
+            (rows_out(), rows_out()), (QUARTER, QUARTER), 50_000_000 if k else 350_000_000,
         )
         if k:
             sent[k] = shift(sent[k], 4 - k)
-    later = pl.BlockSpec((ROWS, D), lambda *_: (1, 0))
     total = sent[0]
     for k in (2, 1):
         total = run(
             add_in, None, (total, sent[k]), [QUARTER] * 2, rows_out(F32), QUARTER, 350_000_000
         )
+    outs = dict(zip(outs, lax.optimization_barrier(tuple(outs.values()))))
+    for k in (2, 1, 3):
+        outs[k] = shift(outs[k], 4 - k)
+    result_own = run(
+        lambda *refs: block_out(1, *refs),
+        None, (mid_own, mod_gate, *(outs[k] for k in range(4))),
+        [QUARTER, VECTORS] + [QUARTER] * 4, rows_out(), QUARTER, RESULT_FLOPS,
+    )
 
     own_grad = pl.BlockSpec((None, ROWS, D), lambda _, at: (at[0], 0, 0))
     grad_patch = run(
@@ -329,12 +329,9 @@
     grad_own = across(grad_patch)
     w0, ow0 = weights_of(0, weights, out_weight, grad_own)
     message = jax.ShapeDtypeStruct((ROWS + HALF, D), BF16)
-    half = whole((HALF, D))
-    packed, result_later = run(
-        pack, None, (grad_own, mid_own, mod_gate, *(sent[k] for k in range(4))),
-        [QUARTER, QUARTER, VECTORS] + [later] * 4,
-        (message, jax.ShapeDtypeStruct((HALF, D), BF16)),
-        (whole((ROWS + HALF, D)), half), 1_000_000,
+    packed = run(
+        pack, None, (grad_own, result_own), [QUARTER, QUARTER],
+        message, whole((ROWS + HALF, D)), 1_000_000,
     )
     grads = lax.all_gather(packed, "tp")
     front, back = whole((4, ROWS, D)), pl.BlockSpec((4, HALF, D), lambda *_: (0, 2, 0))
@@ -346,8 +343,8 @@
     )
     b1, b3, b2 = shift(b1, 1), shift(b3, 3), shift(b2, 2)
     packed = run(
-        pack_last, None, (own, grad_own, mod_scale, b0, b1, b2, b3, result_later),
-        [QUARTER] * 2 + [VECTORS] + [QUARTER] * 4 + [half],
+        pack_last, None, (own, grad_own, mod_scale, b0, b1, b2, b3, result_own),
+        [QUARTER] * 2 + [VECTORS] + [QUARTER] * 5,
         message, whole((ROWS + HALF, D)), 1_000_000,
     )
     ends = lax.all_gather(packed, "tp")

time: 183 us -> 176 us (0.962)
  starting transfers between devices: 23.6 us -> 37.4 us
  blocking collectives: 88 us -> 75.2 us
  waiting for transfers between devices: 38.1 us -> 28.5 us
    ppermute x9 -> x12, waiting for transfers between devices: 38.1 us -> 22.2 us  [shift(): return lax.ppermute(array, 'tp', [(i, (i + k) % N_TP) for i in range(N_TP)])]
    all_to_all x2 -> x1, blocking collectives: 34.7 us -> 21.4 us  [across(): return lax.all_to_all(array, 'seq', split_axis=0, concat_axis=0, tiled=True)]
    all_to_all x0 -> x1, starting transfers between devices: none -> 7.54 us  [across(): return lax.all_to_all(array, 'seq', split_axis=0, concat_axis=0, tiled=True)]
    ppermute x9 -> x12, starting transfers between devices: 23.6 us -> 29.9 us  [shift(): return lax.ppermute(array, 'tp', [(i, (i + k) % N_TP) for i in range(N_TP)])]
    all_to_all x0 -> x1, waiting for transfers between devices: none -> 6.21 us  [across(): return lax.all_to_all(array, 'seq', split_axis=0, concat_axis=0, tiled=True)]
    unnamed x27 -> x25, local copies, waits for them, and re-layouts: 3.68 us -> 3.44 us
    pallas_call x14 -> x15, Pallas kernels: 24.1 us -> 24.1 us  [run(): pl.pallas_call(body, grid_spec=pltpu.PrefetchScalarGridSpec(num_scalar_pr...]
  transfers between devices with their start and end apart: 9 -> 13, of which waited for: 7 -> 8; matrix products, arithmetic and copies ran while one was open for 0% -> 1% of each run, Pallas kernels for 5% -> 5%
where the time goes in v3:
time: 176 us; the launch traced here: 175 us
  blocking collectives  75.2 us (43%)
  starting transfers between devices  37.4 us (21%)
  waiting for transfers between devices  28.5 us (16%)
  Pallas kernels  24.1 us (14%)
  local copies, waits for them, and re-layouts  7.59 us (4%)
    ppermute x12, starting transfers between devices, shift(): return lax.ppermute(array, 'tp', [(i, (i + k) % N_TP) for i in range(N_TP)])  29.9 us
    pallas_call x15, Pallas kernels, run(): pl.pallas_call(body, grid_spec=pltpu.PrefetchScalarGridSpec(num_scalar_pr...  24.1 us
    ppermute x12, waiting for transfers between devices, shift(): return lax.ppermute(array, 'tp', [(i, (i + k) % N_TP) for i in range(N_TP)])  22.2 us
    all_to_all x1, blocking collectives, across(): return lax.all_to_all(array, 'seq', split_axis=0, concat_axis=0, tiled=True)  21.4 us
    all_gather x1, blocking collectives, per_device(): grads = lax.all_gather(packed, 'tp')  20.5 us
    all_gather x1, blocking collectives, per_device(): ends = lax.all_gather(packed, 'tp')  18.2 us
    all_gather x1, blocking collectives, per_device(): mids = lax.all_gather(mid_own, 'tp')  15 us
    all_to_all x1, starting transfers between devices, across(): return lax.all_to_all(array, 'seq', split_axis=0, concat_axis=0, tiled=True)  7.54 us
  transfers between devices with their start and end apart: 13, of which 8 were waited for; matrix products, arithmetic and copies ran while one was open for 1% of the time, Pallas kernels for 5%

profile of v3, /device:TPU:1, one launch (start us, length us, event | category | flops | bytes accessed | tf_op | source)
XLA Modules:
  0.0 175.0 jit_solution(16517484700090587583)
XLA Ops:
  0.6 6.7 %shard_map.86 = (bf16[64,1152]{1,0:T(8,128)(2,1)}, bf16[64,1152]{1,0:T(8,128)(2,1)}, bf16[64,1152]{1,0:T(8,128)(2,1)}, bf16[64,1152]{1,0:T(8,128)(2,1)}, bf16[3,...) custom-call(s32[1]{0:T(128)} %bitcast.me_ref, bf16[256,1152]{1,0:T(8,128)(2,1)} %bitcast.42, ...), custom_call_target="tpu_custom_call" | custom-call | flops 1000000000 | tf_op jit(solution)/shard_map/pallas_call | solution.py:234
  7.3 3.9 %collective-permute-start = (bf16[64,1152]{1,0:T(8,128)(2,1)}, bf16[64,1152]{1,0:T(8,128)(2,1)S(1)}, u32[]{:S(2)}, u32[]{:S(2)}) collective-permute-start(bf16[64,1152]{1,0:T(8,128)(2,1)} %get-tuple-element.32), channel_id=1, source_target_pairs={{0,1},{1,2},{2,3},{3,0},{4,5},{5,6},{6,7},{7,4},{8,9},{9,10},{10,1... | collective-permute-start | bytes 442376 | tf_op jit(solution)/shard_map/ppermute | solution.py:251
  11.3 3.1 %collective-permute-start.1 = (bf16[64,1152]{1,0:T(8,128)(2,1)}, bf16[64,1152]{1,0:T(8,128)(2,1)S(1)}, u32[]{:S(2)}, u32[]{:S(2)}) collective-permute-start(bf16[64,1152]{1,0:T(8,128)(2,1)} %get-tuple-element.33), channel_id=1, source_target_pairs={{0,3},{1,0},{2,1},{3,2},{4,7},{5,4},{6,5},{7,6},{8,11},{9,8},{10,9... | collective-permute-start | bytes 442376 | tf_op jit(solution)/shard_map/ppermute | solution.py:251
  14.4 4.4 %collective-permute-start.2 = (bf16[64,1152]{1,0:T(8,128)(2,1)}, bf16[64,1152]{1,0:T(8,128)(2,1)S(1)}, u32[]{:S(2)}, u32[]{:S(2)}) collective-permute-start(bf16[64,1152]{1,0:T(8,128)(2,1)} %get-tuple-element.34), channel_id=1, source_target_pairs={{0,2},{1,3},{2,0},{3,1},{4,6},{5,7},{6,4},{7,5},{8,10},{9,11},{10,... | collective-permute-start | bytes 442376 | tf_op jit(solution)/shard_map/ppermute | solution.py:251
  18.7 0.9 copy-done.7
  19.7 6.4 %collective-permute-done.1.refs_3_ = bf16[64,1152]{1,0:T(8,128)(2,1)S(1)} collective-permute-done((bf16[64,1152]{1,0:T(8,128)(2,1)}, bf16[64,1152]{1,0:T(8,128)(2,1)S(1)}, u32[]{:S(2)}, u32[]{:S(2)}) %collective-permute-start.1) | collective-permute-done | bytes 147488 | tf_op jit(solution)/shard_map/ppermute | solution.py:251
  26.1 1.8 %collective-permute-done.2.refs_4_ = bf16[64,1152]{1,0:T(8,128)(2,1)S(1)} collective-permute-done((bf16[64,1152]{1,0:T(8,128)(2,1)}, bf16[64,1152]{1,0:T(8,128)(2,1)S(1)}, u32[]{:S(2)}, u32[]{:S(2)}) %collective-permute-start.2) | collective-permute-done | bytes 147488 | tf_op jit(solution)/shard_map/ppermute | solution.py:251
  27.8 0.9 copy-done.1
  28.8 0.1 shard_map.88
  28.8 0.5 broadcast
  29.4 0.7 reduce
  30.0 0.2 reshape.28
  30.2 21.4 %all_to_all.22 = bf16[64,2,576]{2,1,0:T(2,128)(2,1)S(1)} all-to-all(bf16[64,2,576]{2,1,0:T(2,128)(2,1)S(1)} %reshape.28), channel_id=1, replica_groups=mesh['seq'=64,'tp'=4] {'seq'}, dimensions={0} | all-to-all | bytes 294912 | tf_op jit(solution)/shard_map/all_to_all | solution.py:255
  51.7 0.2 reshape.29
  52.0 15.0 %all-gather = bf16[256,1,1152]{2,0,1:T(8,128)(2,1)S(1)} all-gather(bf16[64,1,1152]{2,0,1:T(8,128)(2,1)S(1)} %copy.14), channel_id=2, replica_groups=mesh['seq'=64,'tp'=4] {'tp'}, dimensions={0}, use_global_device_ids=true | all-gather | bytes 737280 | tf_op jit(solution)/shard_map/all_gather | solution.py:297
  67.0 0.1 slice_bitcast_fusion.3.ow_ref
  67.1 1.8 %slice_bitcast_fusion.1.w_ref = bf16[864,1152]{1,0:T(8,128)(2,1)S(1)} fusion(bf16[2,864,1152]{2,1,0:T(8,128)(2,1)} %bitcast.40), kind=kLoop, calls=%fused_computation.1 | loop fusion | bytes 3981312 | tf_op jit(solution)/shard_map/squeeze | solution.py:260
  68.9 2.8 %shard_map.90 = (bf16[64,1152]{1,0:T(8,128)(2,1)S(1)}, bf16[64,1152]{1,0:T(8,128)(2,1)S(1)}) custom-call(s32[1]{0:T(128)} %bitcast.me_ref, bf16[4,64,1152]{2,1,0:T(8,128)(2,1)S(1)} %bitcast.25, bf16[4,64,1152]{2,1,0:T(8,128)(2,1)S(1)} %copy-done, bf16[864,1152]{1,0:T(8,128)(2,1)S(1)} %slice_bitcast_fusion.1.w_ref, ...), custom_call_target="tpu_custom_call" | custom-call | flops 50000000 | tf_op jit(solution)/shard_map/pallas_call | solution.py:234
  71.7 3.5 %collective-permute-start.3 = (bf16[64,1152]{1,0:T(8,128)(2,1)S(1)}, bf16[64,1152]{1,0:T(8,128)(2,1)S(1)}, u32[]{:S(2)}, u32[]{:S(2)}) collective-permute-start(bf16[64,1152]{1,0:T(8,128)(2,1)S(1)} %get-tuple-element.38), channel_id=1, source_target_pairs={{0,2},{1,3},{2,0},{3,1},{4,6},{5,7},{6,4},{7,5},{8,10},{9,11},{10,... | collective-permute-start | bytes 442376 | tf_op jit(solution)/shard_map/ppermute | solution.py:251
  75.2 2.8 %shard_map.92 = (bf16[64,1152]{1,0:T(8,128)(2,1)S(1)}, bf16[64,1152]{1,0:T(8,128)(2,1)S(1)}) custom-call(s32[1]{0:T(128)} %bitcast.me_ref, bf16[4,64,1152]{2,1,0:T(8,128)(2,1)S(1)} %bitcast.26, bf16[4,64,1152]{2,1,0:T(8,128)(2,1)S(1)} %copy-done, bf16[864,1152]{1,0:T(8,128)(2,1)S(1)} %slice_bitcast_fusion.1.w_ref, ...), custom_call_target="tpu_custom_call" | custom-call | flops 50000000 | tf_op jit(solution)/shard_map/pallas_call | solution.py:234
  78.0 2.3 %collective-permute-start.4 = (bf16[64,1152]{1,0:T(8,128)(2,1)S(1)}, bf16[64,1152]{1,0:T(8,128)(2,1)S(1)}, u32[]{:S(2)}, u32[]{:S(2)}) collective-permute-start(bf16[64,1152]{1,0:T(8,128)(2,1)S(1)} %get-tuple-element.39), channel_id=1, source_target_pairs={{0,3},{1,0},{2,1},{3,2},{4,7},{5,4},{6,5},{7,6},{8,11},{9,8},{10,9... | collective-permute-start | bytes 442376 | tf_op jit(solution)/shard_map/ppermute | solution.py:251
  80.2 2.8 %shard_map.94 = (bf16[64,1152]{1,0:T(8,128)(2,1)S(1)}, bf16[64,1152]{1,0:T(8,128)(2,1)S(1)}) custom-call(s32[1]{0:T(128)} %bitcast.me_ref, bf16[4,64,1152]{2,1,0:T(8,128)(2,1)S(1)} %bitcast.27, bf16[4,64,1152]{2,1,0:T(8,128)(2,1)S(1)} %copy-done, bf16[864,1152]{1,0:T(8,128)(2,1)S(1)} %slice_bitcast_fusion.1.w_ref, ...), custom_call_target="tpu_custom_call" | custom-call | flops 50000000 | tf_op jit(solution)/shard_map/pallas_call | solution.py:234
  83.0 0.4 collective-permute-start.5
  83.5 2.8 %shard_map.89 = (bf16[64,1152]{1,0:T(8,128)(2,1)S(1)}, bf16[64,1152]{1,0:T(8,128)(2,1)S(1)}) custom-call(s32[1]{0:T(128)} %bitcast.me_ref, bf16[4,64,1152]{2,1,0:T(8,128)(2,1)S(1)} %bitcast.28, bf16[4,64,1152]{2,1,0:T(8,128)(2,1)S(1)} %copy-done, bf16[864,1152]{1,0:T(8,128)(2,1)S(1)} %slice_bitcast_fusion.1.w_ref, ...), custom_call_target="tpu_custom_call" | custom-call | flops 350000000 | tf_op jit(solution)/shard_map/pallas_call | solution.py:234
  86.3 3.3 %collective-permute-start.6 = (bf16[64,1152]{1,0:T(8,128)(2,1)S(1)}, bf16[64,1152]{1,0:T(8,128)(2,1)S(1)}, u32[]{:S(2)}, u32[]{:S(2)}) collective-permute-start(bf16[64,1152]{1,0:T(8,128)(2,1)S(1)} %get-tuple-element.46), channel_id=1, source_target_pairs={{0,3},{1,0},{2,1},{3,2},{4,7},{5,4},{6,5},{7,6},{8,11},{9,8},{10,9... | collective-permute-start | bytes 442376 | tf_op jit(solution)/shard_map/ppermute | solution.py:251
  89.6 3.0 %collective-permute-start.7 = (bf16[64,1152]{1,0:T(8,128)(2,1)S(1)}, bf16[64,1152]{1,0:T(8,128)(2,1)S(1)}, u32[]{:S(2)}, u32[]{:S(2)}) collective-permute-start(bf16[64,1152]{1,0:T(8,128)(2,1)S(1)} %get-tuple-element.47), channel_id=1, source_target_pairs={{0,2},{1,3},{2,0},{3,1},{4,6},{5,7},{6,4},{7,5},{8,10},{9,11},{10,... | collective-permute-start | bytes 442376 | tf_op jit(solution)/shard_map/ppermute | solution.py:251
  92.7 0.3 shard_map.95
  93.0 0.7 reduce.1
  93.7 0.9 reshape.30
  94.6 7.5 %all-to-all-start.1 = ((bf16[64,2,576]{2,1,0:T(2,128)(2,1)}), bf16[64,2,576]{2,1,0:T(2,128)(2,1)S(1)}, u32[]{:S(2)}, u32[]{:S(2)}) async-start(bf16[64,2,576]{2,1,0:T(2,128)(2,1)} %reshape.30), calls=%async_computation.1 | async-start | bytes 327680 | tf_op jit(solution)/shard_map/all_to_all | solution.py:255
  102.1 1.7 collective-permute-done.7.refs_4_
  103.8 0.9 collective-permute-done.8.refs_5_
  104.8 0.1 shard_map.96.result_ref
  104.9 6.2 %all-to-all-done.1 = bf16[64,2,576]{2,1,0:T(2,128)(2,1)S(1)} async-done(((bf16[64,2,576]{2,1,0:T(2,128)(2,1)}), bf16[64,2,576]{2,1,0:T(2,128)(2,1)S(1)}, u32[]{:S(2)}, u32[]{:S(2)}) %all-to-all-start.1) | async-done | bytes 147488 | tf_op jit(solution)/shard_map/all_to_all | solution.py:255
  111.1 0.2 reshape.31
  111.4 20.5 %all-gather.1 = bf16[384,1152]{1,0:T(8,128)(2,1)S(1)} all-gather(bf16[96,1152]{1,0:T(8,128)(2,1)S(1)} %shard_map.97), channel_id=3, replica_groups=mesh['seq'=64,'tp'=4] {'tp'}, dimensions={0}, use_global_device_ids=true | all-gather | bytes 1105920 | tf_op jit(solution)/shard_map/all_gather | solution.py:336
  131.9 0.1 slice_bitcast_fusion.2.ow_ref
  131.9 1.8 %slice_bitcast_fusion.w_ref = bf16[864,1152]{1,0:T(8,128)(2,1)S(1)} fusion(bf16[2,864,1152]{2,1,0:T(8,128)(2,1)} %bitcast.41), kind=kLoop, calls=%fused_computation | loop fusion | bytes 3981312 | tf_op jit(solution)/shard_map/squeeze | solution.py:260
  133.7 3.8 %shard_map.98 = (bf16[64,1152]{1,0:T(8,128)(2,1)S(1)}, bf16[64,1152]{1,0:T(8,128)(2,1)S(1)}, bf16[64,1152]{1,0:T(8,128)(2,1)S(1)}, bf16[64,1152]{1,0:T(8,128)(2,1)S(1)}) custom-call(s32[1]{0:T(128)} %bitcast.me_ref, bf16[4,96,1152]{2,1,0:T(8,128)(2,1)S(1)} %bitcast.31, bf16[3,256,288]{2,1,0:T(8,128)(2,1)S(1)} %copy-done.6, ...), custom_call_target="tpu_custom_call" | custom-call | flops 1500000000 | tf_op jit(solution)/shard_map/pallas_call | solution.py:234
  137.6 0.5 collective-permute-start.9
  138.1 2.8 %collective-permute-start.10 = (bf16[64,1152]{1,0:T(8,128)(2,1)S(1)}, bf16[64,1152]{1,0:T(8,128)(2,1)S(1)}, u32[]{:S(2)}, u32[]{:S(2)}) collective-permute-start(bf16[64,1152]{1,0:T(8,128)(2,1)S(1)} %get-tuple-element.54), channel_id=1, source_target_pairs={{0,2},{1,3},{2,0},{3,1},{4,6},{5,7},{6,4},{7,5},{8,10},{9,11},{10,... | collective-permute-start | bytes 442376 | tf_op jit(solution)/shard_map/ppermute | solution.py:251
  140.8 2.7 %collective-permute-start.11 = (bf16[64,1152]{1,0:T(8,128)(2,1)S(1)}, bf16[64,1152]{1,0:T(8,128)(2,1)S(1)}, u32[]{:S(2)}, u32[]{:S(2)}) collective-permute-start(bf16[64,1152]{1,0:T(8,128)(2,1)S(1)} %get-tuple-element.55), channel_id=1, source_target_pairs={{0,3},{1,0},{2,1},{3,2},{4,7},{5,4},{6,5},{7,6},{8,11},{9,8},{10,9... | collective-permute-start | bytes 442376 | tf_op jit(solution)/shard_map/ppermute | solution.py:251
  143.6 2.2 %collective-permute-done.9.b1 = bf16[64,1152]{1,0:T(8,128)(2,1)S(1)} collective-permute-done((bf16[64,1152]{1,0:T(8,128)(2,1)S(1)}, bf16[64,1152]{1,0:T(8,128)(2,1)S(1)}, u32[]{:S(2)}, u32[]{:S(2)}) %collective-permute-start.9) | collective-permute-done | bytes 147488 | tf_op jit(solution)/shard_map/ppermute | solution.py:251
  145.7 7.3 %collective-permute-done.10.b2 = bf16[64,1152]{1,0:T(8,128)(2,1)S(1)} collective-permute-done((bf16[64,1152]{1,0:T(8,128)(2,1)S(1)}, bf16[64,1152]{1,0:T(8,128)(2,1)S(1)}, u32[]{:S(2)}, u32[]{:S(2)}) %collective-permute-start.10) | collective-permute-done | bytes 147488 | tf_op jit(solution)/shard_map/ppermute | solution.py:251
  153.0 2.0 %collective-permute-done.11.b3 = bf16[64,1152]{1,0:T(8,128)(2,1)S(1)} collective-permute-done((bf16[64,1152]{1,0:T(8,128)(2,1)S(1)}, bf16[64,1152]{1,0:T(8,128)(2,1)S(1)}, u32[]{:S(2)}, u32[]{:S(2)}) %collective-permute-start.11) | collective-permute-done | bytes 147488 | tf_op jit(solution)/shard_map/ppermute | solution.py:251
  155.1 0.4 shard_map.99
  155.4 18.2 %all-gather.2 = bf16[384,1152]{1,0:T(8,128)(2,1)S(1)} all-gather(bf16[96,1152]{1,0:T(8,128)(2,1)S(1)} %shard_map.99), channel_id=4, replica_groups=mesh['seq'=64,'tp'=4] {'tp'}, dimensions={0}, use_global_device_ids=true | all-gather | bytes 1105920 | tf_op jit(solution)/shard_map/all_gather | solution.py:350
  173.6 1.4 shard_map.100
  (29 shorter events, 0.2 us)
Async XLA Ops:
  0.6 27.2 %copy-start.4 = (f32[2,1152]{1,0:T(2,128)S(1)}, f32[2,1152]{1,0:T(2,128)}, u32[]{:S(2)}) copy-start(f32[2,1152]{1,0:T(2,128)} %gate_ref.9) | copy-start | bytes 27652
  7.3 11.4 %collective-permute-start = (bf16[64,1152]{1,0:T(8,128)(2,1)}, bf16[64,1152]{1,0:T(8,128)(2,1)S(1)}, u32[]{:S(2)}, u32[]{:S(2)}) collective-permute-start(bf16[64,1152]{1,0:T(8,128)(2,1)} %get-tuple-element.32), channel_id=1, source_target_pairs={{0,1},{1,2},{2,3},{3,0},{4,5},{5,6},{6,7},{7,4},{8,9},{9,10},{10,1... | collective-permute-start | bytes 442376 | tf_op jit(solution)/shard_map/ppermute | solution.py:251
  11.3 14.8 %collective-permute-start.1 = (bf16[64,1152]{1,0:T(8,128)(2,1)}, bf16[64,1152]{1,0:T(8,128)(2,1)S(1)}, u32[]{:S(2)}, u32[]{:S(2)}) collective-permute-start(bf16[64,1152]{1,0:T(8,128)(2,1)} %get-tuple-element.33), channel_id=1, source_target_pairs={{0,3},{1,0},{2,1},{3,2},{4,7},{5,4},{6,5},{7,6},{8,11},{9,8},{10,9... | collective-permute-start | bytes 442376 | tf_op jit(solution)/shard_map/ppermute | solution.py:251
  14.4 13.5 %collective-permute-start.2 = (bf16[64,1152]{1,0:T(8,128)(2,1)}, bf16[64,1152]{1,0:T(8,128)(2,1)S(1)}, u32[]{:S(2)}, u32[]{:S(2)}) collective-permute-start(bf16[64,1152]{1,0:T(8,128)(2,1)} %get-tuple-element.34), channel_id=1, source_target_pairs={{0,2},{1,3},{2,0},{3,1},{4,6},{5,7},{6,4},{7,5},{8,10},{9,11},{10,... | collective-permute-start | bytes 442376 | tf_op jit(solution)/shard_map/ppermute | solution.py:251
  18.7 0.9 copy-start.7
  27.8 0.9 copy-start.1
  28.8 38.2 %copy-start.8 = (bf16[2,288,1152]{2,1,0:T(8,128)(2,1)S(1)}, bf16[2,288,1152]{2,1,0:T(8,128)(2,1)}, u32[]{:S(2)}) copy-start(bf16[2,288,1152]{2,1,0:T(8,128)(2,1)} %ow_hbm.1) | copy-start | bytes 3981316
  67.1 1.8 %copy-start = (bf16[4,64,1152]{2,1,0:T(8,128)(2,1)S(1)}, bf16[4,64,1152]{2,1,0:T(8,128)(2,1)}, u32[]{:S(2)}) copy-start(bf16[4,64,1152]{2,1,0:T(8,128)(2,1)} %refs_1_.4) | copy-start | bytes 1769476
  67.1 1.8 %copy-start.3 = (f32[2,1152]{1,0:T(2,128)S(1)}, f32[2,1152]{1,0:T(2,128)}, u32[]{:S(2)}) copy-start(f32[2,1152]{1,0:T(2,128)} %scale_ref.11) | copy-start | bytes 27652
  67.1 1.8 %copy-start.5 = (f32[2,1152]{1,0:T(2,128)S(1)}, f32[2,1152]{1,0:T(2,128)}, u32[]{:S(2)}) copy-start(f32[2,1152]{1,0:T(2,128)} %shift_ref.9) | copy-start | bytes 27652
  71.7 20.9 %collective-permute-start.3 = (bf16[64,1152]{1,0:T(8,128)(2,1)S(1)}, bf16[64,1152]{1,0:T(8,128)(2,1)S(1)}, u32[]{:S(2)}, u32[]{:S(2)}) collective-permute-start(bf16[64,1152]{1,0:T(8,128)(2,1)S(1)} %get-tuple-element.38), channel_id=1, source_target_pairs={{0,2},{1,3},{2,0},{3,1},{4,6},{5,7},{6,4},{7,5},{8,10},{9,11},{10,... | collective-permute-start | bytes 442376 | tf_op jit(solution)/shard_map/ppermute | solution.py:251
  78.0 14.6 %collective-permute-start.4 = (bf16[64,1152]{1,0:T(8,128)(2,1)S(1)}, bf16[64,1152]{1,0:T(8,128)(2,1)S(1)}, u32[]{:S(2)}, u32[]{:S(2)}) collective-permute-start(bf16[64,1152]{1,0:T(8,128)(2,1)S(1)} %get-tuple-element.39), channel_id=1, source_target_pairs={{0,3},{1,0},{2,1},{3,2},{4,7},{5,4},{6,5},{7,6},{8,11},{9,8},{10,9... | collective-permute-start | bytes 442376 | tf_op jit(solution)/shard_map/ppermute | solution.py:251
  83.0 9.6 %collective-permute-start.5 = (bf16[64,1152]{1,0:T(8,128)(2,1)S(1)}, bf16[64,1152]{1,0:T(8,128)(2,1)S(1)}, u32[]{:S(2)}, u32[]{:S(2)}) collective-permute-start(bf16[64,1152]{1,0:T(8,128)(2,1)S(1)} %get-tuple-element.40), channel_id=1, source_target_pairs={{0,1},{1,2},{2,3},{3,0},{4,5},{5,6},{6,7},{7,4},{8,9},{9,10},{10,1... | collective-permute-start | bytes 442376 | tf_op jit(solution)/shard_map/ppermute | solution.py:251
  86.3 15.8 %collective-permute-start.6 = (bf16[64,1152]{1,0:T(8,128)(2,1)S(1)}, bf16[64,1152]{1,0:T(8,128)(2,1)S(1)}, u32[]{:S(2)}, u32[]{:S(2)}) collective-permute-start(bf16[64,1152]{1,0:T(8,128)(2,1)S(1)} %get-tuple-element.46), channel_id=1, source_target_pairs={{0,3},{1,0},{2,1},{3,2},{4,7},{5,4},{6,5},{7,6},{8,11},{9,8},{10,9... | collective-permute-start | bytes 442376 | tf_op jit(solution)/shard_map/ppermute | solution.py:251
  89.6 14.3 %collective-permute-start.7 = (bf16[64,1152]{1,0:T(8,128)(2,1)S(1)}, bf16[64,1152]{1,0:T(8,128)(2,1)S(1)}, u32[]{:S(2)}, u32[]{:S(2)}) collective-permute-start(bf16[64,1152]{1,0:T(8,128)(2,1)S(1)} %get-tuple-element.47), channel_id=1, source_target_pairs={{0,2},{1,3},{2,0},{3,1},{4,6},{5,7},{6,4},{7,5},{8,10},{9,11},{10,... | collective-permute-start | bytes 442376 | tf_op jit(solution)/shard_map/ppermute | solution.py:251
  92.6 12.2 %collective-permute-start.8 = (bf16[64,1152]{1,0:T(8,128)(2,1)S(1)}, bf16[64,1152]{1,0:T(8,128)(2,1)S(1)}, u32[]{:S(2)}, u32[]{:S(2)}) collective-permute-start(bf16[64,1152]{1,0:T(8,128)(2,1)S(1)} %get-tuple-element.48), channel_id=1, source_target_pairs={{0,1},{1,2},{2,3},{3,0},{4,5},{5,6},{6,7},{7,4},{8,9},{9,10},{10,1... | collective-permute-start | bytes 442376 | tf_op jit(solution)/shard_map/ppermute | solution.py:251
  94.6 16.5 %all-to-all-start.1 = ((bf16[64,2,576]{2,1,0:T(2,128)(2,1)}), bf16[64,2,576]{2,1,0:T(2,128)(2,1)S(1)}, u32[]{:S(2)}, u32[]{:S(2)}) async-start(bf16[64,2,576]{2,1,0:T(2,128)(2,1)} %reshape.30), calls=%async_computation.1 | async-start | bytes 327680 | tf_op jit(solution)/shard_map/all_to_all | solution.py:255
  131.9 1.8 %copy-start.6 = (bf16[3,256,288]{2,1,0:T(8,128)(2,1)S(1)}, bf16[3,256,288]{2,1,0:T(8,128)(2,1)}, u32[]{:S(2)}) copy-start(bf16[3,256,288]{2,1,0:T(8,128)(2,1)} %get-tuple-element.49.qkv_ref) | copy-start | bytes 1327108
  133.7 21.3 %copy-start.2 = (bf16[64,1152]{1,0:T(8,128)(2,1)S(1)}, bf16[64,1152]{1,0:T(8,128)(2,1)}, u32[]{:S(2)}) copy-start(bf16[64,1152]{1,0:T(8,128)(2,1)} %get-tuple-element.30.refs_0_.x_ref) | copy-start | bytes 442372
  137.6 8.2 %collective-permute-start.9 = (bf16[64,1152]{1,0:T(8,128)(2,1)S(1)}, bf16[64,1152]{1,0:T(8,128)(2,1)S(1)}, u32[]{:S(2)}, u32[]{:S(2)}) collective-permute-start(bf16[64,1152]{1,0:T(8,128)(2,1)S(1)} %get-tuple-element.53), channel_id=1, source_target_pairs={{0,1},{1,2},{2,3},{3,0},{4,5},{5,6},{6,7},{7,4},{8,9},{9,10},{10,1... | collective-permute-start | bytes 442376 | tf_op jit(solution)/shard_map/ppermute | solution.py:251
  138.1 15.0 %collective-permute-start.10 = (bf16[64,1152]{1,0:T(8,128)(2,1)S(1)}, bf16[64,1152]{1,0:T(8,128)(2,1)S(1)}, u32[]{:S(2)}, u32[]{:S(2)}) collective-permute-start(bf16[64,1152]{1,0:T(8,128)(2,1)S(1)} %get-tuple-element.54), channel_id=1, source_target_pairs={{0,2},{1,3},{2,0},{3,1},{4,6},{5,7},{6,4},{7,5},{8,10},{9,11},{10,... | collective-permute-start | bytes 442376 | tf_op jit(solution)/shard_map/ppermute | solution.py:251
  140.8 14.2 %collective-permute-start.11 = (bf16[64,1152]{1,0:T(8,128)(2,1)S(1)}, bf16[64,1152]{1,0:T(8,128)(2,1)S(1)}, u32[]{:S(2)}, u32[]{:S(2)}) collective-permute-start(bf16[64,1152]{1,0:T(8,128)(2,1)S(1)} %get-tuple-element.55), channel_id=1, source_target_pairs={{0,3},{1,0},{2,1},{3,2},{4,7},{5,4},{6,5},{7,6},{8,11},{9,8},{10,9... | collective-permute-start | bytes 442376 | tf_op jit(solution)/shard_map/ppermute | solution.py:251

commit v4 on v3

--- a/solution.py
+++ b/solution.py
@@ -58,6 +58,10 @@
     lane = lax.broadcasted_iota(jnp.int32, array.shape, 1)
     keep = (lane >= head * HEAD_DIM) & (lane < (head + 1) * HEAD_DIM)
     return jnp.where(keep, array, jnp.zeros_like(array))
+
+
+def pairs(array):
+    return array[:, : GW // 2], array[:, GW // 2 :]
 
 
 def order_matrix(first, rows):
@@ -104,10 +108,14 @@
     qkv_ref[0] = queries
     qkv_ref[1] = key_heads
     qkv_ref[2] = value_heads
-    attended = jnp.zeros((256, GW), F32)
-    for head in range(HERE):
-        probs = softmax(nt(of_head(queries, head), key_heads) * INV_ROOT)
-        attended = attended + nn(probs.astype(BF16), of_head(value_heads, head))
+    attended = []
+    for queries_2, keys_2, values_2 in zip(pairs(queries), pairs(key_heads), pairs(value_heads)):
+        total = jnp.zeros((256, GW // 2), F32)
+        for head in range(2):
+            probs = softmax(nt(of_head(queries_2, head), keys_2) * INV_ROOT)
+            total = total + nn(probs.astype(BF16), of_head(values_2, head))
+        attended.append(total)
+    attended = jnp.concatenate(attended, axis=1)
     ow_copy.wait()
     attended_ref[...] = nn(attended.astype(BF16), ow_ref[...]).astype(BF16)
     for k, part in enumerate((p0, p1, p2, p3)):
@@ -154,21 +162,27 @@
     grad_proj = (gate_ref[0:1] * grad.astype(F32)).astype(BF16)
     grad_attn = nt(grad_proj, ow_ref[...]).astype(BF16)
     queries, key_heads, value_heads = qkv_ref[0], qkv_ref[1], qkv_ref[2]
-    grad_query = jnp.zeros((256, GW), F32)
-    grad_keys = jnp.zeros((256, GW), F32)
-    grad_values = jnp.zeros((256, GW), F32)
-    for head in range(HERE):
-        query = of_head(queries, head)
-        grad_head = of_head(grad_attn, head)
-        probs = softmax(nt(query, key_heads) * INV_ROOT)
-        grad_probs = nt(grad_head, value_heads)
-        grad_scores = (
-            probs * (grad_probs - jnp.sum(probs * grad_probs, axis=-1, keepdims=True)) * INV_ROOT
-        ).astype(BF16)
-        grad_query = grad_query + nn(grad_scores, of_head(key_heads, head))
-        grad_keys = grad_keys + tn(grad_scores, query)
-        grad_values = grad_values + tn(probs.astype(BF16), grad_head)
-    joined = jnp.concatenate([grad_query, grad_keys, grad_values], axis=1).astype(BF16)
+    grads = []
+    for queries_2, keys_2, values_2, grads_2 in zip(
+        pairs(queries), pairs(key_heads), pairs(value_heads), pairs(grad_attn)
+    ):
+        grad_query = jnp.zeros((256, GW // 2), F32)
+        grad_keys, grad_values = grad_query, grad_query
+        for head in range(2):
+            query = of_head(queries_2, head)
+            grad_head = of_head(grads_2, head)
+            probs = softmax(nt(query, keys_2) * INV_ROOT)
+            grad_probs = nt(grad_head, values_2)
+            grad_scores = (
+                probs
+                * (grad_probs - jnp.sum(probs * grad_probs, axis=-1, keepdims=True))
+                * INV_ROOT
+            ).astype(BF16)
+            grad_query = grad_query + nn(grad_scores, of_head(keys_2, head))
+            grad_keys = grad_keys + tn(grad_scores, query)
+            grad_values = grad_values + tn(probs.astype(BF16), grad_head)
+        grads.append((grad_query, grad_keys, grad_values))
+    joined = jnp.concatenate([pair[i] for i in range(3) for pair in grads], axis=1).astype(BF16)
     total_ref[...] = nn(joined, w_ref[...]).astype(BF16)
     for k, part in enumerate((p0, p1, p2, p3)):
         part[...] = total_ref[chunk_rows((me_ref[0] + k) % 4), :]
@@ -176,13 +190,22 @@
 
 def add_in(a_ref, b_ref, sum_ref):
     sum_ref[...] = a_ref[...].astype(F32) + b_ref[...].astype(F32)
+
+
+def put(ref, rows):
+    rows = rows.astype(ref.dtype)
+    if len(ref.shape) == 3:
+        ref[:, 0] = rows[:, : D // 2]
+        ref[:, 1] = rows[:, D // 2 :]
+    else:
+        ref[...] = rows
 
 
 def block_out(block, x_ref, gate_ref, *refs):
     total = refs[0][...].astype(F32)
     for ref in refs[1:-1]:
         total = total + ref[...].astype(F32)
-    refs[-1][...] = (x_ref[...].astype(F32) + gate_ref[block : block + 1] * total).astype(BF16)
+    put(refs[-1], x_ref[...].astype(F32) + gate_ref[block : block + 1] * total)
 
 
 def grad_of(block, x_ref, g_ref, scale_ref, *refs):
@@ -192,11 +215,11 @@
     normed, inv_std = normalize(x_ref[...])
     grad = g_ref[...].astype(F32)
     back = norm_back(total, normed, inv_std, scale_ref[block : block + 1])
-    refs[-1][...] = (grad + back).astype(BF16)
+    put(refs[-1], grad + back)
 
 
 def pack(grad_ref, result_ref, sent_ref):
-    sent_ref[:ROWS] = grad_ref[...]
+    sent_ref[:ROWS] = jnp.concatenate([grad_ref[:, 0], grad_ref[:, 1]], axis=1)
     sent_ref[ROWS:] = result_ref[:HALF]
 
 
@@ -221,6 +244,7 @@
 
 QUARTER = whole((ROWS, D))
 VECTORS = whole((2, D))
+HALVES = jax.ShapeDtypeStruct((ROWS, 2, D // 2), BF16)
 
 
 def rows_out(dtype=BF16):
@@ -284,13 +308,17 @@
         mib=58,
     )
     p1, p3, p2 = shift(p1, 1), shift(p3, 3), shift(p2, 2)
-    early = run(add_in, None, (p0, p1), [QUARTER] * 2, rows_out(F32), QUARTER, 350_000_000)
+    early = run(
+        lambda *refs: block_out(0, *refs),
+        None, (own, mod_gate, p0, p1), [QUARTER, VECTORS, QUARTER, QUARTER],
+        rows_out(F32), QUARTER, 350_000_000,
+    )
     middle = run(
         lambda *refs: block_out(0, *refs),
-        None, (own, mod_gate, early, p3, p2), [QUARTER, VECTORS] + [QUARTER] * 3,
-        rows_out(), QUARTER, 1_000_000,
-    )
-    mid_own = across(middle)
+        None, (early, mod_gate, p3, p2), [QUARTER, VECTORS] + [QUARTER] * 2,
+        HALVES, whole((ROWS, 2, D // 2)), 1_000_000,
+    )
+    mid_own = across(middle).reshape(ROWS, D)
     w_spec, ow_spec = whole((3 * GW, D)), whole((GW, D))
     w1, ow1 = weights_of(1, weights, out_weight, mid_own)
 
@@ -324,13 +352,13 @@
         lambda me_ref, *refs: grad_of(1, *refs),
         me, (mid_own, grad_out, mod_scale, total, sent[3]),
         [QUARTER, own_grad, VECTORS] + [QUARTER] * 2,
-        rows_out(), QUARTER, 1_000_000,
+        HALVES, whole((ROWS, 2, D // 2)), 1_000_000,
     )
     grad_own = across(grad_patch)
     w0, ow0 = weights_of(0, weights, out_weight, grad_own)
     message = jax.ShapeDtypeStruct((ROWS + HALF, D), BF16)
     packed = run(
-        pack, None, (grad_own, result_own), [QUARTER, QUARTER],
+        pack, None, (grad_own, result_own), [whole((ROWS, 2, D // 2)), QUARTER],
         message, whole((ROWS + HALF, D)), 1_000_000,
     )
     grads = lax.all_gather(packed, "tp")
@@ -343,7 +371,7 @@
     )
     b1, b3, b2 = shift(b1, 1), shift(b3, 3), shift(b2, 2)
     packed = run(
-        pack_last, None, (own, grad_own, mod_scale, b0, b1, b2, b3, result_own),
+        pack_last, None, (own, packed, mod_scale, b0, b1, b2, b3, result_own),
         [QUARTER] * 2 + [VECTORS] + [QUARTER] * 5,
         message, whole((ROWS + HALF, D)), 1_000_000,
     )

time: 176 us -> 172 us (0.977)
  local copies, waits for them, and re-layouts: 7.59 us -> 5.77 us
  transfers between devices with their start and end apart: 13 -> 13, of which waited for: 8 -> 9; matrix products, arithmetic and copies ran while one was open for 1% -> 0% of each run, Pallas kernels for 5% -> 6%
where the time goes in v4:
time: 172 us; the launch traced here: 171 us
  blocking collectives  73.9 us (43%)
  starting transfers between devices  37.7 us (22%)
  waiting for transfers between devices  29.2 us (17%)
  Pallas kernels  23.6 us (14%)
  local copies, waits for them, and re-layouts  5.77 us (3%)
    ppermute x12, starting transfers between devices, shift(): return lax.ppermute(array, 'tp', [(i, (i + k) % N_TP) for i in range(N_TP)])  30.1 us
    ppermute x12, waiting for transfers between devices, shift(): return lax.ppermute(array, 'tp', [(i, (i + k) % N_TP) for i in range(N_TP)])  23.8 us
    pallas_call x15, Pallas kernels, run(): pl.pallas_call(body, grid_spec=pltpu.PrefetchScalarGridSpec(num_scalar_pr...  23.6 us
    all_to_all x1, blocking collectives, across(): return lax.all_to_all(array, 'seq', split_axis=0, concat_axis=0, tiled=True)  21.4 us
    all_gather x1, blocking collectives, per_device(): grads = lax.all_gather(packed, 'tp')  19.7 us
    all_gather x1, blocking collectives, per_device(): ends = lax.all_gather(packed, 'tp')  17.7 us
    all_gather x1, blocking collectives, per_device(): mids = lax.all_gather(mid_own, 'tp')  15 us
    all_to_all x1, starting transfers between devices, across(): return lax.all_to_all(array, 'seq', split_axis=0, concat_axis=0, tiled=True)  7.55 us
  transfers between devices with their start and end apart: 13, of which 9 were waited for; matrix products, arithmetic and copies ran while one was open for 0% of the time, Pallas kernels for 6%

profile of v4, /device:TPU:1, one launch (start us, length us, event | category | flops | bytes accessed | tf_op | source)
XLA Modules:
  0.0 171.0 jit_solution(9851090434835094602)
XLA Ops:
  0.7 6.0 %shard_map.86 = (bf16[64,1152]{1,0:T(8,128)(2,1)}, bf16[64,1152]{1,0:T(8,128)(2,1)}, bf16[64,1152]{1,0:T(8,128)(2,1)}, bf16[64,1152]{1,0:T(8,128)(2,1)}, bf16[3,...) custom-call(s32[1]{0:T(128)} %bitcast.me_ref, bf16[256,1152]{1,0:T(8,128)(2,1)} %bitcast.23, ...), custom_call_target="tpu_custom_call" | custom-call | flops 1000000000 | tf_op jit(solution)/shard_map/pallas_call | solution.py:258
  6.7 3.9 %collective-permute-start = (bf16[64,1152]{1,0:T(8,128)(2,1)}, bf16[64,1152]{1,0:T(8,128)(2,1)S(1)}, u32[]{:S(2)}, u32[]{:S(2)}) collective-permute-start(bf16[64,1152]{1,0:T(8,128)(2,1)} %get-tuple-element.32), channel_id=1, source_target_pairs={{0,1},{1,2},{2,3},{3,0},{4,5},{5,6},{6,7},{7,4},{8,9},{9,10},{10,1... | collective-permute-start | bytes 442376 | tf_op jit(solution)/shard_map/ppermute | solution.py:275
  10.6 3.1 %collective-permute-start.1 = (bf16[64,1152]{1,0:T(8,128)(2,1)}, bf16[64,1152]{1,0:T(8,128)(2,1)S(1)}, u32[]{:S(2)}, u32[]{:S(2)}) collective-permute-start(bf16[64,1152]{1,0:T(8,128)(2,1)} %get-tuple-element.33), channel_id=1, source_target_pairs={{0,3},{1,0},{2,1},{3,2},{4,7},{5,4},{6,5},{7,6},{8,11},{9,8},{10,9... | collective-permute-start | bytes 442376 | tf_op jit(solution)/shard_map/ppermute | solution.py:275
  13.7 4.4 %collective-permute-start.2 = (bf16[64,1152]{1,0:T(8,128)(2,1)}, bf16[64,1152]{1,0:T(8,128)(2,1)S(1)}, u32[]{:S(2)}, u32[]{:S(2)}) collective-permute-start(bf16[64,1152]{1,0:T(8,128)(2,1)} %get-tuple-element.34), channel_id=1, source_target_pairs={{0,2},{1,3},{2,0},{3,1},{4,6},{5,7},{6,4},{7,5},{8,10},{9,11},{10,... | collective-permute-start | bytes 442376 | tf_op jit(solution)/shard_map/ppermute | solution.py:275
  18.1 0.9 copy-done.4
  19.0 0.9 copy-done.7
  19.9 0.1 shard_map.87.refs_0_
  20.0 5.4 %collective-permute-done.1.refs_2_ = bf16[64,1152]{1,0:T(8,128)(2,1)S(1)} collective-permute-done((bf16[64,1152]{1,0:T(8,128)(2,1)}, bf16[64,1152]{1,0:T(8,128)(2,1)S(1)}, u32[]{:S(2)}, u32[]{:S(2)}) %collective-permute-start.1) | collective-permute-done | bytes 147488 | tf_op jit(solution)/shard_map/ppermute | solution.py:275
  25.3 1.8 %collective-permute-done.2.refs_3_ = bf16[64,1152]{1,0:T(8,128)(2,1)S(1)} collective-permute-done((bf16[64,1152]{1,0:T(8,128)(2,1)}, bf16[64,1152]{1,0:T(8,128)(2,1)S(1)}, u32[]{:S(2)}, u32[]{:S(2)}) %collective-permute-start.2) | collective-permute-done | bytes 147488 | tf_op jit(solution)/shard_map/ppermute | solution.py:275
  27.1 0.2 shard_map.88
  27.3 21.4 %all_to_all.10 = bf16[64,2,576]{2,1,0:T(2,128)(2,1)S(1)} all-to-all(bf16[64,2,576]{2,1,0:T(2,128)(2,1)S(1)} %shard_map.88), channel_id=1, replica_groups=mesh['seq'=64,'tp'=4] {'seq'}, dimensions={0} | all-to-all | bytes 294912 | tf_op jit(solution)/shard_map/all_to_all | solution.py:279
  48.8 0.1 reshape.22.refs_0_
  48.9 0.1 all_gather_reshape.3
  49.0 15.0 %all_gather.15.m_ref = bf16[4,64,1152]{2,1,0:T(8,128)(2,1)S(1)} all-gather(bf16[1,64,1152]{2,1,0:T(8,128)(2,1)S(1)} %all_gather_reshape.3), channel_id=1, replica_groups=mesh['seq'=64,'tp'=4] {'tp'}, dimensions={0}, use_global_device_ids=true | all-gather | bytes 737280 | tf_op jit(solution)/shard_map/all_gather | solution.py:325
  64.1 0.1 slice_bitcast_fusion.3.ow_ref
  64.1 0.0 copy-start
  64.1 0.0 copy-start.1
  64.2 1.8 %slice_bitcast_fusion.1.w_ref = bf16[864,1152]{1,0:T(8,128)(2,1)S(1)} fusion(bf16[2,864,1152]{2,1,0:T(8,128)(2,1)} %bitcast.21), kind=kLoop, calls=%fused_computation.1 | loop fusion | bytes 3981312 | tf_op jit(solution)/shard_map/squeeze | solution.py:284
  66.0 2.8 %shard_map.90 = (bf16[64,1152]{1,0:T(8,128)(2,1)S(1)}, bf16[64,1152]{1,0:T(8,128)(2,1)S(1)}) custom-call(s32[1]{0:T(128)} %bitcast.me_ref, bf16[4,64,1152]{2,1,0:T(8,128)(2,1)S(1)} %all_gather.15.m_ref, bf16[4,64,1152]{2,1,0:T(8,128)(2,1)S(1)} %copy-done, bf16[864,1152]{1,0:T(8,128)(2,1)S(1)} %slice_bitcast_fusion.1.w_ref, ...), custom_call_target="tpu_custom_call" | custom-call | flops 50000000 | tf_op jit(solution)/shard_map/pallas_call | solution.py:258
  68.8 3.5 %collective-permute-start.3 = (bf16[64,1152]{1,0:T(8,128)(2,1)S(1)}, bf16[64,1152]{1,0:T(8,128)(2,1)S(1)}, u32[]{:S(2)}, u32[]{:S(2)}) collective-permute-start(bf16[64,1152]{1,0:T(8,128)(2,1)S(1)} %get-tuple-element.38), channel_id=1, source_target_pairs={{0,2},{1,3},{2,0},{3,1},{4,6},{5,7},{6,4},{7,5},{8,10},{9,11},{10,... | collective-permute-start | bytes 442376 | tf_op jit(solution)/shard_map/ppermute | solution.py:275
  72.3 2.8 %shard_map.92 = (bf16[64,1152]{1,0:T(8,128)(2,1)S(1)}, bf16[64,1152]{1,0:T(8,128)(2,1)S(1)}) custom-call(s32[1]{0:T(128)} %bitcast.me_ref, bf16[4,64,1152]{2,1,0:T(8,128)(2,1)S(1)} %all_gather.15.m_ref, bf16[4,64,1152]{2,1,0:T(8,128)(2,1)S(1)} %copy-done, bf16[864,1152]{1,0:T(8,128)(2,1)S(1)} %slice_bitcast_fusion.1.w_ref, ...), custom_call_target="tpu_custom_call" | custom-call | flops 50000000 | tf_op jit(solution)/shard_map/pallas_call | solution.py:258
  75.1 2.3 %collective-permute-start.4 = (bf16[64,1152]{1,0:T(8,128)(2,1)S(1)}, bf16[64,1152]{1,0:T(8,128)(2,1)S(1)}, u32[]{:S(2)}, u32[]{:S(2)}) collective-permute-start(bf16[64,1152]{1,0:T(8,128)(2,1)S(1)} %get-tuple-element.39), channel_id=1, source_target_pairs={{0,3},{1,0},{2,1},{3,2},{4,7},{5,4},{6,5},{7,6},{8,11},{9,8},{10,9... | collective-permute-start | bytes 442376 | tf_op jit(solution)/shard_map/ppermute | solution.py:275
  77.3 2.8 %shard_map.94 = (bf16[64,1152]{1,0:T(8,128)(2,1)S(1)}, bf16[64,1152]{1,0:T(8,128)(2,1)S(1)}) custom-call(s32[1]{0:T(128)} %bitcast.me_ref, bf16[4,64,1152]{2,1,0:T(8,128)(2,1)S(1)} %all_gather.15.m_ref, bf16[4,64,1152]{2,1,0:T(8,128)(2,1)S(1)} %copy-done, bf16[864,1152]{1,0:T(8,128)(2,1)S(1)} %slice_bitcast_fusion.1.w_ref, ...), custom_call_target="tpu_custom_call" | custom-call | flops 50000000 | tf_op jit(solution)/shard_map/pallas_call | solution.py:258
  80.1 0.4 collective-permute-start.5
  80.6 2.8 %shard_map.89 = (bf16[64,1152]{1,0:T(8,128)(2,1)S(1)}, bf16[64,1152]{1,0:T(8,128)(2,1)S(1)}) custom-call(s32[1]{0:T(128)} %bitcast.me_ref, bf16[4,64,1152]{2,1,0:T(8,128)(2,1)S(1)} %all_gather.15.m_ref, bf16[4,64,1152]{2,1,0:T(8,128)(2,1)S(1)} %copy-done, bf16[864,1152]{1,0:T(8,128)(2,1)S(1)} %slice_bitcast_fusion.1.w_ref, ...), custom_call_target="tpu_custom_call" | custom-call | flops 350000000 | tf_op jit(solution)/shard_map/pallas_call | solution.py:258
  83.4 3.3 %collective-permute-start.6 = (bf16[64,1152]{1,0:T(8,128)(2,1)S(1)}, bf16[64,1152]{1,0:T(8,128)(2,1)S(1)}, u32[]{:S(2)}, u32[]{:S(2)}) collective-permute-start(bf16[64,1152]{1,0:T(8,128)(2,1)S(1)} %get-tuple-element.46), channel_id=1, source_target_pairs={{0,3},{1,0},{2,1},{3,2},{4,7},{5,4},{6,5},{7,6},{8,11},{9,8},{10,9... | collective-permute-start | bytes 442376 | tf_op jit(solution)/shard_map/ppermute | solution.py:275
  86.6 3.0 %collective-permute-start.7 = (bf16[64,1152]{1,0:T(8,128)(2,1)S(1)}, bf16[64,1152]{1,0:T(8,128)(2,1)S(1)}, u32[]{:S(2)}, u32[]{:S(2)}) collective-permute-start(bf16[64,1152]{1,0:T(8,128)(2,1)S(1)} %get-tuple-element.47), channel_id=1, source_target_pairs={{0,2},{1,3},{2,0},{3,1},{4,6},{5,7},{6,4},{7,5},{8,10},{9,11},{10,... | collective-permute-start | bytes 442376 | tf_op jit(solution)/shard_map/ppermute | solution.py:275
  89.8 1.1 shard_map.95
  90.9 7.5 %all-to-all-start.1 = ((bf16[64,2,576]{2,1,0:T(2,128)(2,1)}), bf16[64,2,576]{2,1,0:T(2,128)(2,1)S(1)}, u32[]{:S(2)}, u32[]{:S(2)}) async-start(bf16[64,2,576]{2,1,0:T(2,128)(2,1)} %shard_map.95), calls=%async_computation.1 | async-start | bytes 327680 | tf_op jit(solution)/shard_map/all_to_all | solution.py:279
  98.4 0.2 collective-permute-done.6.refs_3_
  98.7 2.3 %collective-permute-done.7.refs_4_ = bf16[64,1152]{1,0:T(8,128)(2,1)S(1)} collective-permute-done((bf16[64,1152]{1,0:T(8,128)(2,1)S(1)}, bf16[64,1152]{1,0:T(8,128)(2,1)S(1)}, u32[]{:S(2)}, u32[]{:S(2)}) %collective-permute-start.7) | collective-permute-done | bytes 147488 | tf_op jit(solution)/shard_map/ppermute | solution.py:275
  100.9 0.9 collective-permute-done.8.refs_5_
  101.8 0.1 shard_map.96.result_ref
  101.9 5.4 %all-to-all-done.1.grad_ref = bf16[64,2,576]{2,1,0:T(2,128)(2,1)S(1)} async-done(((bf16[64,2,576]{2,1,0:T(2,128)(2,1)}), bf16[64,2,576]{2,1,0:T(2,128)(2,1)S(1)}, u32[]{:S(2)}, u32[]{:S(2)}) %all-to-all-start.1) | async-done | bytes 147488 | tf_op jit(solution)/shard_map/all_to_all | solution.py:279
  107.4 0.1 slice_bitcast_fusion.2.ow_ref
  107.4 0.4 shard_map.97.g_ref
  107.8 19.7 %all-gather = bf16[384,1152]{1,0:T(8,128)(2,1)S(1)} all-gather(bf16[96,1152]{1,0:T(8,128)(2,1)S(1)} %shard_map.97.g_ref), channel_id=2, replica_groups=mesh['seq'=64,'tp'=4] {'tp'}, dimensions={0}, use_global_device_ids=true | all-gather | bytes 1105920 | tf_op jit(solution)/shard_map/all_gather | solution.py:364
  127.5 1.8 %slice_bitcast_fusion.w_ref = bf16[864,1152]{1,0:T(8,128)(2,1)S(1)} fusion(bf16[2,864,1152]{2,1,0:T(8,128)(2,1)} %bitcast.22), kind=kLoop, calls=%fused_computation | loop fusion | bytes 3981312 | tf_op jit(solution)/shard_map/squeeze | solution.py:284
  129.3 2.8 %shard_map.98 = (bf16[64,1152]{1,0:T(8,128)(2,1)S(1)}, bf16[64,1152]{1,0:T(8,128)(2,1)S(1)}, bf16[64,1152]{1,0:T(8,128)(2,1)S(1)}, bf16[64,1152]{1,0:T(8,128)(2,1)S(1)}) custom-call(s32[1]{0:T(128)} %bitcast.me_ref, bf16[4,96,1152]{2,1,0:T(8,128)(2,1)S(1)} %bitcast.18, bf16[3,256,288]{2,1,0:T(8,128)(2,1)S(1)} %copy-done.6, ...), custom_call_target="tpu_custom_call" | custom-call | flops 1500000000 | tf_op jit(solution)/shard_map/pallas_call | solution.py:258
  132.2 0.4 collective-permute-start.9
  132.6 3.4 %collective-permute-start.10 = (bf16[64,1152]{1,0:T(8,128)(2,1)S(1)}, bf16[64,1152]{1,0:T(8,128)(2,1)S(1)}, u32[]{:S(2)}, u32[]{:S(2)}) collective-permute-start(bf16[64,1152]{1,0:T(8,128)(2,1)S(1)} %get-tuple-element.54), channel_id=1, source_target_pairs={{0,2},{1,3},{2,0},{3,1},{4,6},{5,7},{6,4},{7,5},{8,10},{9,11},{10,... | collective-permute-start | bytes 442376 | tf_op jit(solution)/shard_map/ppermute | solution.py:275
  136.0 2.4 %collective-permute-start.11 = (bf16[64,1152]{1,0:T(8,128)(2,1)S(1)}, bf16[64,1152]{1,0:T(8,128)(2,1)S(1)}, u32[]{:S(2)}, u32[]{:S(2)}) collective-permute-start(bf16[64,1152]{1,0:T(8,128)(2,1)S(1)} %get-tuple-element.55), channel_id=1, source_target_pairs={{0,3},{1,0},{2,1},{3,2},{4,7},{5,4},{6,5},{7,6},{8,11},{9,8},{10,9... | collective-permute-start | bytes 442376 | tf_op jit(solution)/shard_map/ppermute | solution.py:275
  138.4 1.6 collective-permute-done.9.b1
  140.0 6.1 %collective-permute-done.10.b2 = bf16[64,1152]{1,0:T(8,128)(2,1)S(1)} collective-permute-done((bf16[64,1152]{1,0:T(8,128)(2,1)S(1)}, bf16[64,1152]{1,0:T(8,128)(2,1)S(1)}, u32[]{:S(2)}, u32[]{:S(2)}) %collective-permute-start.10) | collective-permute-done | bytes 147488 | tf_op jit(solution)/shard_map/ppermute | solution.py:275
  146.2 5.4 %collective-permute-done.11.b3 = bf16[64,1152]{1,0:T(8,128)(2,1)S(1)} collective-permute-done((bf16[64,1152]{1,0:T(8,128)(2,1)S(1)}, bf16[64,1152]{1,0:T(8,128)(2,1)S(1)}, u32[]{:S(2)}, u32[]{:S(2)}) %collective-permute-start.11) | collective-permute-done | bytes 147488 | tf_op jit(solution)/shard_map/ppermute | solution.py:275
  151.6 0.4 shard_map.99
  151.9 17.7 %all-gather.1 = bf16[384,1152]{1,0:T(8,128)(2,1)S(1)} all-gather(bf16[96,1152]{1,0:T(8,128)(2,1)S(1)} %shard_map.99), channel_id=3, replica_groups=mesh['seq'=64,'tp'=4] {'tp'}, dimensions={0}, use_global_device_ids=true | all-gather | bytes 1105920 | tf_op jit(solution)/shard_map/all_gather | solution.py:378
  169.7 1.4 shard_map.100
  (21 shorter events, 0.1 us)
Async XLA Ops:
  0.6 17.4 %copy-start.2 = (f32[2,1152]{1,0:T(2,128)S(1)}, f32[2,1152]{1,0:T(2,128)}, u32[]{:S(2)}) copy-start(f32[2,1152]{1,0:T(2,128)} %gate_ref.9) | copy-start | bytes 27652
  0.6 63.4 %copy-start.8 = (bf16[2,288,1152]{2,1,0:T(8,128)(2,1)S(1)}, bf16[2,288,1152]{2,1,0:T(8,128)(2,1)}, u32[]{:S(2)}) copy-start(bf16[2,288,1152]{2,1,0:T(8,128)(2,1)} %ow_hbm.1) | copy-start | bytes 3981316
  6.7 11.4 %collective-permute-start = (bf16[64,1152]{1,0:T(8,128)(2,1)}, bf16[64,1152]{1,0:T(8,128)(2,1)S(1)}, u32[]{:S(2)}, u32[]{:S(2)}) collective-permute-start(bf16[64,1152]{1,0:T(8,128)(2,1)} %get-tuple-element.32), channel_id=1, source_target_pairs={{0,1},{1,2},{2,3},{3,0},{4,5},{5,6},{6,7},{7,4},{8,9},{9,10},{10,1... | collective-permute-start | bytes 442376 | tf_op jit(solution)/shard_map/ppermute | solution.py:275
  10.6 14.8 %collective-permute-start.1 = (bf16[64,1152]{1,0:T(8,128)(2,1)}, bf16[64,1152]{1,0:T(8,128)(2,1)S(1)}, u32[]{:S(2)}, u32[]{:S(2)}) collective-permute-start(bf16[64,1152]{1,0:T(8,128)(2,1)} %get-tuple-element.33), channel_id=1, source_target_pairs={{0,3},{1,0},{2,1},{3,2},{4,7},{5,4},{6,5},{7,6},{8,11},{9,8},{10,9... | collective-permute-start | bytes 442376 | tf_op jit(solution)/shard_map/ppermute | solution.py:275
  13.7 13.5 %collective-permute-start.2 = (bf16[64,1152]{1,0:T(8,128)(2,1)}, bf16[64,1152]{1,0:T(8,128)(2,1)S(1)}, u32[]{:S(2)}, u32[]{:S(2)}) collective-permute-start(bf16[64,1152]{1,0:T(8,128)(2,1)} %get-tuple-element.34), channel_id=1, source_target_pairs={{0,2},{1,3},{2,0},{3,1},{4,6},{5,7},{6,4},{7,5},{8,10},{9,11},{10,... | collective-permute-start | bytes 442376 | tf_op jit(solution)/shard_map/ppermute | solution.py:275
  18.1 0.9 copy-start.4
  19.0 0.9 copy-start.7
  64.1 1.8 %copy-start = (bf16[4,64,1152]{2,1,0:T(8,128)(2,1)S(1)}, bf16[4,64,1152]{2,1,0:T(8,128)(2,1)}, u32[]{:S(2)}) copy-start(bf16[4,64,1152]{2,1,0:T(8,128)(2,1)} %refs_1_.6) | copy-start | bytes 1769476
  64.1 1.8 %copy-start.1 = (f32[2,1152]{1,0:T(2,128)S(1)}, f32[2,1152]{1,0:T(2,128)}, u32[]{:S(2)}) copy-start(f32[2,1152]{1,0:T(2,128)} %scale_ref.11) | copy-start | bytes 27652
  64.2 1.8 %copy-start.3 = (f32[2,1152]{1,0:T(2,128)S(1)}, f32[2,1152]{1,0:T(2,128)}, u32[]{:S(2)}) copy-start(f32[2,1152]{1,0:T(2,128)} %shift_ref.9) | copy-start | bytes 27652
  68.8 20.9 %collective-permute-start.3 = (bf16[64,1152]{1,0:T(8,128)(2,1)S(1)}, bf16[64,1152]{1,0:T(8,128)(2,1)S(1)}, u32[]{:S(2)}, u32[]{:S(2)}) collective-permute-start(bf16[64,1152]{1,0:T(8,128)(2,1)S(1)} %get-tuple-element.38), channel_id=1, source_target_pairs={{0,2},{1,3},{2,0},{3,1},{4,6},{5,7},{6,4},{7,5},{8,10},{9,11},{10,... | collective-permute-start | bytes 442376 | tf_op jit(solution)/shard_map/ppermute | solution.py:275
  75.1 14.6 %collective-permute-start.4 = (bf16[64,1152]{1,0:T(8,128)(2,1)S(1)}, bf16[64,1152]{1,0:T(8,128)(2,1)S(1)}, u32[]{:S(2)}, u32[]{:S(2)}) collective-permute-start(bf16[64,1152]{1,0:T(8,128)(2,1)S(1)} %get-tuple-element.39), channel_id=1, source_target_pairs={{0,3},{1,0},{2,1},{3,2},{4,7},{5,4},{6,5},{7,6},{8,11},{9,8},{10,9... | collective-permute-start | bytes 442376 | tf_op jit(solution)/shard_map/ppermute | solution.py:275
  80.1 9.6 %collective-permute-start.5 = (bf16[64,1152]{1,0:T(8,128)(2,1)S(1)}, bf16[64,1152]{1,0:T(8,128)(2,1)S(1)}, u32[]{:S(2)}, u32[]{:S(2)}) collective-permute-start(bf16[64,1152]{1,0:T(8,128)(2,1)S(1)} %get-tuple-element.40), channel_id=1, source_target_pairs={{0,1},{1,2},{2,3},{3,0},{4,5},{5,6},{6,7},{7,4},{8,9},{9,10},{10,1... | collective-permute-start | bytes 442376 | tf_op jit(solution)/shard_map/ppermute | solution.py:275
  83.4 15.3 %collective-permute-start.6 = (bf16[64,1152]{1,0:T(8,128)(2,1)S(1)}, bf16[64,1152]{1,0:T(8,128)(2,1)S(1)}, u32[]{:S(2)}, u32[]{:S(2)}) collective-permute-start(bf16[64,1152]{1,0:T(8,128)(2,1)S(1)} %get-tuple-element.46), channel_id=1, source_target_pairs={{0,3},{1,0},{2,1},{3,2},{4,7},{5,4},{6,5},{7,6},{8,11},{9,8},{10,9... | collective-permute-start | bytes 442376 | tf_op jit(solution)/shard_map/ppermute | solution.py:275
  86.6 14.3 %collective-permute-start.7 = (bf16[64,1152]{1,0:T(8,128)(2,1)S(1)}, bf16[64,1152]{1,0:T(8,128)(2,1)S(1)}, u32[]{:S(2)}, u32[]{:S(2)}) collective-permute-start(bf16[64,1152]{1,0:T(8,128)(2,1)S(1)} %get-tuple-element.47), channel_id=1, source_target_pairs={{0,2},{1,3},{2,0},{3,1},{4,6},{5,7},{6,4},{7,5},{8,10},{9,11},{10,... | collective-permute-start | bytes 442376 | tf_op jit(solution)/shard_map/ppermute | solution.py:275
  89.7 12.2 %collective-permute-start.8 = (bf16[64,1152]{1,0:T(8,128)(2,1)S(1)}, bf16[64,1152]{1,0:T(8,128)(2,1)S(1)}, u32[]{:S(2)}, u32[]{:S(2)}) collective-permute-start(bf16[64,1152]{1,0:T(8,128)(2,1)S(1)} %get-tuple-element.48), channel_id=1, source_target_pairs={{0,1},{1,2},{2,3},{3,0},{4,5},{5,6},{6,7},{7,4},{8,9},{9,10},{10,1... | collective-permute-start | bytes 442376 | tf_op jit(solution)/shard_map/ppermute | solution.py:275
  90.9 16.5 %all-to-all-start.1 = ((bf16[64,2,576]{2,1,0:T(2,128)(2,1)}), bf16[64,2,576]{2,1,0:T(2,128)(2,1)S(1)}, u32[]{:S(2)}, u32[]{:S(2)}) async-start(bf16[64,2,576]{2,1,0:T(2,128)(2,1)} %shard_map.95), calls=%async_computation.1 | async-start | bytes 327680 | tf_op jit(solution)/shard_map/all_to_all | solution.py:279
  127.5 1.8 %copy-start.6 = (bf16[3,256,288]{2,1,0:T(8,128)(2,1)S(1)}, bf16[3,256,288]{2,1,0:T(8,128)(2,1)}, u32[]{:S(2)}) copy-start(bf16[3,256,288]{2,1,0:T(8,128)(2,1)} %get-tuple-element.49.qkv_ref) | copy-start | bytes 1327108
  129.3 22.2 %copy-start.5 = (bf16[64,1152]{1,0:T(8,128)(2,1)S(1)}, bf16[64,1152]{1,0:T(8,128)(2,1)}, u32[]{:S(2)}) copy-start(bf16[64,1152]{1,0:T(8,128)(2,1)} %get-tuple-element.30.refs_0_.x_ref) | copy-start | bytes 442372
  132.2 7.9 %collective-permute-start.9 = (bf16[64,1152]{1,0:T(8,128)(2,1)S(1)}, bf16[64,1152]{1,0:T(8,128)(2,1)S(1)}, u32[]{:S(2)}, u32[]{:S(2)}) collective-permute-start(bf16[64,1152]{1,0:T(8,128)(2,1)S(1)} %get-tuple-element.53), channel_id=1, source_target_pairs={{0,1},{1,2},{2,3},{3,0},{4,5},{5,6},{6,7},{7,4},{8,9},{9,10},{10,1... | collective-permute-start | bytes 442376 | tf_op jit(solution)/shard_map/ppermute | solution.py:275
  132.6 13.6 %collective-permute-start.10 = (bf16[64,1152]{1,0:T(8,128)(2,1)S(1)}, bf16[64,1152]{1,0:T(8,128)(2,1)S(1)}, u32[]{:S(2)}, u32[]{:S(2)}) collective-permute-start(bf16[64,1152]{1,0:T(8,128)(2,1)S(1)} %get-tuple-element.54), channel_id=1, source_target_pairs={{0,2},{1,3},{2,0},{3,1},{4,6},{5,7},{6,4},{7,5},{8,10},{9,11},{10,... | collective-permute-start | bytes 442376 | tf_op jit(solution)/shard_map/ppermute | solution.py:275
  136.0 15.6 %collective-permute-start.11 = (bf16[64,1152]{1,0:T(8,128)(2,1)S(1)}, bf16[64,1152]{1,0:T(8,128)(2,1)S(1)}, u32[]{:S(2)}, u32[]{:S(2)}) collective-permute-start(bf16[64,1152]{1,0:T(8,128)(2,1)S(1)} %get-tuple-element.55), channel_id=1, source_target_pairs={{0,3},{1,0},{2,1},{3,2},{4,7},{5,4},{6,5},{7,6},{8,11},{9,8},{10,9... | collective-permute-start | bytes 442376 | tf_op jit(solution)/shard_map/ppermute | solution.py:275

commit v5 on v4

--- a/solution.py
+++ b/solution.py
@@ -1,3 +1,4 @@
+import functools
 import math
 
 import jax
@@ -14,6 +15,7 @@
 N_TP = 4
 ROWS = 64
 HALF = 32
+GROUPS = ((2,), (1,), (3,), (0,))
 RESULT_FLOPS = 3_000_000_000
 INV_ROOT = 1.0 / math.sqrt(HEAD_DIM)
 F32 = jnp.float32
@@ -122,12 +124,16 @@
         part[...] = attended_ref[chunk_rows((me + k) % 4), :]
 
 
-def temporal(me_ref, m_ref, g_ref, w_ref, ow_ref, shift_ref, scale_ref, gate_ref, part_ref, out_part_ref):
-    mid = m_ref[...]
-    normed, _ = normalize(mid)
-    modded = (normed * (1.0 + scale_ref[1:2]) + shift_ref[1:2]).astype(BF16)
-    grad_proj = (gate_ref[1:2] * g_ref[...].astype(F32)).astype(BF16)
-    queries, key_heads, value_heads = project(modded, w_ref[...])
+def temporal(count, me_ref, *refs):
+    mids, grads = refs[:count], refs[count : 2 * count]
+    w_ref, ow_ref, shift_ref, scale_ref, gate_ref = refs[2 * count : 2 * count + 5]
+    part_refs, out_refs = refs[2 * count + 5 : 3 * count + 5], refs[3 * count + 5 :]
+
+    def rows_of(array, i):
+        return array[i * ROWS : (i + 1) * ROWS]
+
+    def stack(pieces):
+        return jnp.concatenate(pieces, axis=0) if len(pieces) > 1 else pieces[0]
 
     def spread(array):
         return jnp.concatenate([of_head(array, head) for head in range(HERE)], axis=0)
@@ -135,24 +141,38 @@
     def gather_heads(array):
         total = of_head(array[:ROWS], 0)
         for head in range(1, HERE):
-            total = total + of_head(array[head * ROWS : (head + 1) * ROWS], head)
+            total = total + of_head(rows_of(array, head), head)
         return total
 
-    queries_4 = spread(queries)
-    probs = softmax(nt(queries_4, key_heads) * INV_ROOT)
-    probs_low = probs.astype(BF16)
-    grad_attn_4 = spread(nt(grad_proj, ow_ref[...]).astype(BF16))
-    grad_probs = nt(grad_attn_4, value_heads)
-    grad_scores = (
-        probs * (grad_probs - jnp.sum(probs * grad_probs, axis=-1, keepdims=True)) * INV_ROOT
-    ).astype(BF16)
-    grad_query = gather_heads(nn(grad_scores, key_heads))
-    grad_keys = tn(grad_scores, queries_4)
-    grad_values = tn(probs_low, grad_attn_4)
-    joined = jnp.concatenate([grad_query, grad_keys, grad_values], axis=1).astype(BF16)
-    part_ref[...] = nn(joined, w_ref[...]).astype(BF16)
-    attended = gather_heads(nn(probs_low, value_heads)).astype(BF16)
-    out_part_ref[...] = nn(attended, ow_ref[...]).astype(BF16)
+    normed, _ = normalize(stack([ref[...] for ref in mids]))
+    modded = (normed * (1.0 + scale_ref[1:2]) + shift_ref[1:2]).astype(BF16)
+    grad = stack([ref[...] for ref in grads]).astype(F32)
+    grad_proj = (gate_ref[1:2] * grad).astype(BF16)
+    queries, key_heads, value_heads = project(modded, w_ref[...])
+    grad_attn = nt(grad_proj, ow_ref[...]).astype(BF16)
+    joined, attended = [], []
+    for i in range(count):
+        keys_i, values_i = rows_of(key_heads, i), rows_of(value_heads, i)
+        queries_4 = spread(rows_of(queries, i))
+        probs = softmax(nt(queries_4, keys_i) * INV_ROOT)
+        probs_low = probs.astype(BF16)
+        grad_attn_4 = spread(rows_of(grad_attn, i))
+        grad_probs = nt(grad_attn_4, values_i)
+        grad_scores = (
+            probs * (grad_probs - jnp.sum(probs * grad_probs, axis=-1, keepdims=True)) * INV_ROOT
+        ).astype(BF16)
+        grad_query = gather_heads(nn(grad_scores, keys_i))
+        grad_keys = tn(grad_scores, queries_4)
+        grad_values = tn(probs_low, grad_attn_4)
+        joined.append(
+            jnp.concatenate([grad_query, grad_keys, grad_values], axis=1).astype(BF16)
+        )
+        attended.append(gather_heads(nn(probs_low, values_i)).astype(BF16))
+    part = nn(stack(joined), w_ref[...]).astype(BF16)
+    out = nn(stack(attended), ow_ref[...]).astype(BF16)
+    for i in range(count):
+        part_refs[i][...] = rows_of(part, i)
+        out_refs[i][...] = rows_of(out, i)
 
 
 def spatial_backward(
@@ -324,15 +344,22 @@
 
     mids = lax.all_gather(mid_own, "tp")
     sent, outs = {}, {}
-    for k in (2, 1, 3, 0):
-        chunk = pl.BlockSpec((None, ROWS, D), lambda _, at, k=k: ((at[0] + 4 - k) % 4, 0, 0))
-        sent[k], outs[k] = run(
-            temporal, me, (mids, grad_out, w1, ow1, mod_shift, mod_scale, mod_gate),
-            [chunk, chunk, w_spec, ow_spec, VECTORS, VECTORS, VECTORS],
-            (rows_out(), rows_out()), (QUARTER, QUARTER), 50_000_000 if k else 350_000_000,
+    for group in GROUPS:
+        chunks = [
+            pl.BlockSpec((None, ROWS, D), lambda _, at, k=k: ((at[0] + 4 - k) % 4, 0, 0))
+            for k in group
+        ]
+        count = len(group)
+        made = run(
+            functools.partial(temporal, count), me,
+            (mids,) * count + (grad_out,) * count + (w1, ow1, mod_shift, mod_scale, mod_gate),
+            chunks * 2 + [w_spec, ow_spec, VECTORS, VECTORS, VECTORS],
+            (rows_out(),) * (2 * count), (QUARTER,) * (2 * count),
+            50_000_000 if group[-1] else 350_000_000,
         )
-        if k:
-            sent[k] = shift(sent[k], 4 - k)
+        for i, k in enumerate(group):
+            sent[k] = shift(made[i], 4 - k) if k else made[i]
+            outs[k] = made[count + i]
     total = sent[0]
     for k in (2, 1):
         total = run(

time: 172 us -> 169 us (0.983)
  blocking collectives: 73.9 us -> 76.6 us
  waiting for transfers between devices: 29.2 us -> 26.8 us
  Pallas kernels: 23.6 us -> 21.7 us
    all_to_all x1, waiting for transfers between devices: 5.43 us -> 3.29 us  [across(): return lax.all_to_all(array, 'seq', split_axis=0, concat_axis=0, tiled=True)]
    pallas_call x15, Pallas kernels: 23.6 us -> 21.7 us  [run(): pl.pallas_call(body, grid_spec=pltpu.PrefetchScalarGridSpec(num_scalar_pr...]
  transfers between devices with their start and end apart: 13 -> 13, of which waited for: 9 -> 9; matrix products, arithmetic and copies ran while one was open for 0% -> 0% of each run, Pallas kernels for 6% -> 5%
where the time goes in v5:
time: 169 us
  blocking collectives  76.6 us (45%)
  starting transfers between devices  36.9 us (22%)
  waiting for transfers between devices  26.8 us (16%)
  Pallas kernels  21.7 us (13%)
  local copies, waits for them, and re-layouts  5.77 us (3%)
    ppermute x12, starting transfers between devices, shift(): return lax.ppermute(array, 'tp', [(i, (i + k) % N_TP) for i in range(N_TP)])  29.3 us
    ppermute x12, waiting for transfers between devices, shift(): return lax.ppermute(array, 'tp', [(i, (i + k) % N_TP) for i in range(N_TP)])  23.5 us
    pallas_call x15, Pallas kernels, run(): pl.pallas_call(body, grid_spec=pltpu.PrefetchScalarGridSpec(num_scalar_pr...  21.7 us
    all_to_all x1, blocking collectives, across(): return lax.all_to_all(array, 'seq', split_axis=0, concat_axis=0, tiled=True)  21.4 us
    all_gather x1, blocking collectives, per_device(): grads = lax.all_gather(packed, 'tp')  21.2 us
    all_gather x1, blocking collectives, per_device(): ends = lax.all_gather(packed, 'tp')  18.9 us
    all_gather x1, blocking collectives, per_device(): mids = lax.all_gather(mid_own, 'tp')  15 us
    all_to_all x1, starting transfers between devices, across(): return lax.all_to_all(array, 'seq', split_axis=0, concat_axis=0, tiled=True)  7.64 us
  transfers between devices with their start and end apart: 13, of which 9 were waited for; matrix products, arithmetic and copies ran while one was open for 0% of the time, Pallas kernels for 5%

profile of v5, /device:TPU:1, one launch (start us, length us, event | category | flops | bytes accessed | tf_op | source)
XLA Modules:
  0.0 168.6 jit_solution(1428871648111737101)
XLA Ops:
  0.7 6.0 %shard_map.86 = (bf16[64,1152]{1,0:T(8,128)(2,1)}, bf16[64,1152]{1,0:T(8,128)(2,1)}, bf16[64,1152]{1,0:T(8,128)(2,1)}, bf16[64,1152]{1,0:T(8,128)(2,1)}, bf16[3,...) custom-call(s32[1]{0:T(128)} %bitcast.me_ref, bf16[256,1152]{1,0:T(8,128)(2,1)} %bitcast.23, ...), custom_call_target="tpu_custom_call" | custom-call | flops 1000000000 | tf_op jit(solution)/shard_map/pallas_call | solution.py:278
  6.7 3.9 %collective-permute-start = (bf16[64,1152]{1,0:T(8,128)(2,1)}, bf16[64,1152]{1,0:T(8,128)(2,1)S(1)}, u32[]{:S(2)}, u32[]{:S(2)}) collective-permute-start(bf16[64,1152]{1,0:T(8,128)(2,1)} %get-tuple-element.32), channel_id=1, source_target_pairs={{0,1},{1,2},{2,3},{3,0},{4,5},{5,6},{6,7},{7,4},{8,9},{9,10},{10,1... | collective-permute-start | bytes 442376 | tf_op jit(solution)/shard_map/ppermute | solution.py:295
  10.6 3.1 %collective-permute-start.1 = (bf16[64,1152]{1,0:T(8,128)(2,1)}, bf16[64,1152]{1,0:T(8,128)(2,1)S(1)}, u32[]{:S(2)}, u32[]{:S(2)}) collective-permute-start(bf16[64,1152]{1,0:T(8,128)(2,1)} %get-tuple-element.33), channel_id=1, source_target_pairs={{0,3},{1,0},{2,1},{3,2},{4,7},{5,4},{6,5},{7,6},{8,11},{9,8},{10,9... | collective-permute-start | bytes 442376 | tf_op jit(solution)/shard_map/ppermute | solution.py:295
  13.7 4.4 %collective-permute-start.2 = (bf16[64,1152]{1,0:T(8,128)(2,1)}, bf16[64,1152]{1,0:T(8,128)(2,1)S(1)}, u32[]{:S(2)}, u32[]{:S(2)}) collective-permute-start(bf16[64,1152]{1,0:T(8,128)(2,1)} %get-tuple-element.34), channel_id=1, source_target_pairs={{0,2},{1,3},{2,0},{3,1},{4,6},{5,7},{6,4},{7,5},{8,10},{9,11},{10,... | collective-permute-start | bytes 442376 | tf_op jit(solution)/shard_map/ppermute | solution.py:295
  18.1 0.9 copy-done.4
  19.0 0.9 copy-done.7
  19.9 0.1 shard_map.87.refs_0_
  20.0 5.4 %collective-permute-done.1.refs_2_ = bf16[64,1152]{1,0:T(8,128)(2,1)S(1)} collective-permute-done((bf16[64,1152]{1,0:T(8,128)(2,1)}, bf16[64,1152]{1,0:T(8,128)(2,1)S(1)}, u32[]{:S(2)}, u32[]{:S(2)}) %collective-permute-start.1) | collective-permute-done | bytes 147488 | tf_op jit(solution)/shard_map/ppermute | solution.py:295
  25.3 1.8 %collective-permute-done.2.refs_3_ = bf16[64,1152]{1,0:T(8,128)(2,1)S(1)} collective-permute-done((bf16[64,1152]{1,0:T(8,128)(2,1)}, bf16[64,1152]{1,0:T(8,128)(2,1)S(1)}, u32[]{:S(2)}, u32[]{:S(2)}) %collective-permute-start.2) | collective-permute-done | bytes 147488 | tf_op jit(solution)/shard_map/ppermute | solution.py:295
  27.1 0.2 shard_map.88
  27.3 21.4 %all_to_all.10 = bf16[64,2,576]{2,1,0:T(2,128)(2,1)S(1)} all-to-all(bf16[64,2,576]{2,1,0:T(2,128)(2,1)S(1)} %shard_map.88), channel_id=1, replica_groups=mesh['seq'=64,'tp'=4] {'seq'}, dimensions={0} | all-to-all | bytes 294912 | tf_op jit(solution)/shard_map/all_to_all | solution.py:299
  48.8 0.1 reshape.22.refs_0_
  48.9 0.1 all_gather_reshape.3
  49.0 15.0 %all_gather.15.refs_0_ = bf16[4,64,1152]{2,1,0:T(8,128)(2,1)S(1)} all-gather(bf16[1,64,1152]{2,1,0:T(8,128)(2,1)S(1)} %all_gather_reshape.3), channel_id=1, replica_groups=mesh['seq'=64,'tp'=4] {'tp'}, dimensions={0}, use_global_device_ids=true | all-gather | bytes 737280 | tf_op jit(solution)/shard_map/all_gather | solution.py:345
  64.1 0.1 slice_bitcast_fusion.3.refs_3_
  64.1 0.0 copy-start
  64.2 0.0 copy-start.3
  64.2 1.8 %slice_bitcast_fusion.1.refs_2_ = bf16[864,1152]{1,0:T(8,128)(2,1)S(1)} fusion(bf16[2,864,1152]{2,1,0:T(8,128)(2,1)} %bitcast.21), kind=kLoop, calls=%fused_computation.1 | loop fusion | bytes 3981312 | tf_op jit(solution)/shard_map/squeeze | solution.py:304
  66.0 2.3 %shard_map.90 = (bf16[64,1152]{1,0:T(8,128)(2,1)S(1)}, bf16[64,1152]{1,0:T(8,128)(2,1)S(1)}) custom-call(s32[1]{0:T(128)} %bitcast.me_ref, bf16[4,64,1152]{2,1,0:T(8,128)(2,1)S(1)} %all_gather.15.refs_0_, bf16[4,64,1152]{2,1,0:T(8,128)(2,1)S(1)} %copy-done, bf16[864,1152]{1,0:T(8,128)(2,1)S(1)} %slice_bitcast_fusion.1.refs_2_, ...), custom_call_target="tpu_custom_call" | custom-call | flops 50000000 | tf_op jit(solution)/shard_map/pallas_call | solution.py:278
  68.3 3.5 %collective-permute-start.3 = (bf16[64,1152]{1,0:T(8,128)(2,1)S(1)}, bf16[64,1152]{1,0:T(8,128)(2,1)S(1)}, u32[]{:S(2)}, u32[]{:S(2)}) collective-permute-start(bf16[64,1152]{1,0:T(8,128)(2,1)S(1)} %get-tuple-element.38), channel_id=1, source_target_pairs={{0,2},{1,3},{2,0},{3,1},{4,6},{5,7},{6,4},{7,5},{8,10},{9,11},{10,... | collective-permute-start | bytes 442376 | tf_op jit(solution)/shard_map/ppermute | solution.py:295
  71.8 2.3 %shard_map.92 = (bf16[64,1152]{1,0:T(8,128)(2,1)S(1)}, bf16[64,1152]{1,0:T(8,128)(2,1)S(1)}) custom-call(s32[1]{0:T(128)} %bitcast.me_ref, bf16[4,64,1152]{2,1,0:T(8,128)(2,1)S(1)} %all_gather.15.refs_0_, bf16[4,64,1152]{2,1,0:T(8,128)(2,1)S(1)} %copy-done, bf16[864,1152]{1,0:T(8,128)(2,1)S(1)} %slice_bitcast_fusion.1.refs_2_, ...), custom_call_target="tpu_custom_call" | custom-call | flops 50000000 | tf_op jit(solution)/shard_map/pallas_call | solution.py:278
  74.1 2.2 %collective-permute-start.4 = (bf16[64,1152]{1,0:T(8,128)(2,1)S(1)}, bf16[64,1152]{1,0:T(8,128)(2,1)S(1)}, u32[]{:S(2)}, u32[]{:S(2)}) collective-permute-start(bf16[64,1152]{1,0:T(8,128)(2,1)S(1)} %get-tuple-element.39), channel_id=1, source_target_pairs={{0,3},{1,0},{2,1},{3,2},{4,7},{5,4},{6,5},{7,6},{8,11},{9,8},{10,9... | collective-permute-start | bytes 442376 | tf_op jit(solution)/shard_map/ppermute | solution.py:295
  76.3 2.3 %shard_map.94 = (bf16[64,1152]{1,0:T(8,128)(2,1)S(1)}, bf16[64,1152]{1,0:T(8,128)(2,1)S(1)}) custom-call(s32[1]{0:T(128)} %bitcast.me_ref, bf16[4,64,1152]{2,1,0:T(8,128)(2,1)S(1)} %all_gather.15.refs_0_, bf16[4,64,1152]{2,1,0:T(8,128)(2,1)S(1)} %copy-done, bf16[864,1152]{1,0:T(8,128)(2,1)S(1)} %slice_bitcast_fusion.1.refs_2_, ...), custom_call_target="tpu_custom_call" | custom-call | flops 50000000 | tf_op jit(solution)/shard_map/pallas_call | solution.py:278
  78.6 0.5 collective-permute-start.5
  79.1 2.3 %shard_map.89 = (bf16[64,1152]{1,0:T(8,128)(2,1)S(1)}, bf16[64,1152]{1,0:T(8,128)(2,1)S(1)}) custom-call(s32[1]{0:T(128)} %bitcast.me_ref, bf16[4,64,1152]{2,1,0:T(8,128)(2,1)S(1)} %all_gather.15.refs_0_, bf16[4,64,1152]{2,1,0:T(8,128)(2,1)S(1)} %copy-done, bf16[864,1152]{1,0:T(8,128)(2,1)S(1)} %slice_bitcast_fusion.1.refs_2_, ...), custom_call_target="tpu_custom_call" | custom-call | flops 350000000 | tf_op jit(solution)/shard_map/pallas_call | solution.py:278
  81.4 3.3 %collective-permute-start.6 = (bf16[64,1152]{1,0:T(8,128)(2,1)S(1)}, bf16[64,1152]{1,0:T(8,128)(2,1)S(1)}, u32[]{:S(2)}, u32[]{:S(2)}) collective-permute-start(bf16[64,1152]{1,0:T(8,128)(2,1)S(1)} %get-tuple-element.46), channel_id=1, source_target_pairs={{0,3},{1,0},{2,1},{3,2},{4,7},{5,4},{6,5},{7,6},{8,11},{9,8},{10,9... | collective-permute-start | bytes 442376 | tf_op jit(solution)/shard_map/ppermute | solution.py:295
  84.7 3.0 %collective-permute-start.7 = (bf16[64,1152]{1,0:T(8,128)(2,1)S(1)}, bf16[64,1152]{1,0:T(8,128)(2,1)S(1)}, u32[]{:S(2)}, u32[]{:S(2)}) collective-permute-start(bf16[64,1152]{1,0:T(8,128)(2,1)S(1)} %get-tuple-element.47), channel_id=1, source_target_pairs={{0,2},{1,3},{2,0},{3,1},{4,6},{5,7},{6,4},{7,5},{8,10},{9,11},{10,... | collective-permute-start | bytes 442376 | tf_op jit(solution)/shard_map/ppermute | solution.py:295
  87.8 1.1 shard_map.95
  88.9 7.6 %all-to-all-start.1 = ((bf16[64,2,576]{2,1,0:T(2,128)(2,1)}), bf16[64,2,576]{2,1,0:T(2,128)(2,1)S(1)}, u32[]{:S(2)}, u32[]{:S(2)}) async-start(bf16[64,2,576]{2,1,0:T(2,128)(2,1)} %shard_map.95), calls=%async_computation.1 | async-start | bytes 327680 | tf_op jit(solution)/shard_map/all_to_all | solution.py:299
  96.5 2.3 %collective-permute-done.6.refs_3_ = bf16[64,1152]{1,0:T(8,128)(2,1)S(1)} collective-permute-done((bf16[64,1152]{1,0:T(8,128)(2,1)S(1)}, bf16[64,1152]{1,0:T(8,128)(2,1)S(1)}, u32[]{:S(2)}, u32[]{:S(2)}) %collective-permute-start.6) | collective-permute-done | bytes 147488 | tf_op jit(solution)/shard_map/ppermute | solution.py:295
  98.9 1.1 collective-permute-done.7.refs_4_
  100.0 2.0 %collective-permute-done.8.refs_5_ = bf16[64,1152]{1,0:T(8,128)(2,1)S(1)} collective-permute-done((bf16[64,1152]{1,0:T(8,128)(2,1)S(1)}, bf16[64,1152]{1,0:T(8,128)(2,1)S(1)}, u32[]{:S(2)}, u32[]{:S(2)}) %collective-permute-start.8) | collective-permute-done | bytes 147488 | tf_op jit(solution)/shard_map/ppermute | solution.py:295
  102.0 0.1 shard_map.96.result_ref
  102.1 3.3 %all-to-all-done.1.grad_ref = bf16[64,2,576]{2,1,0:T(2,128)(2,1)S(1)} async-done(((bf16[64,2,576]{2,1,0:T(2,128)(2,1)}), bf16[64,2,576]{2,1,0:T(2,128)(2,1)S(1)}, u32[]{:S(2)}, u32[]{:S(2)}) %all-to-all-start.1) | async-done | bytes 147488 | tf_op jit(solution)/shard_map/all_to_all | solution.py:299
  105.4 0.1 slice_bitcast_fusion.2.ow_ref
  105.4 0.4 shard_map.97.g_ref
  105.8 21.2 %all-gather = bf16[384,1152]{1,0:T(8,128)(2,1)S(1)} all-gather(bf16[96,1152]{1,0:T(8,128)(2,1)S(1)} %shard_map.97.g_ref), channel_id=2, replica_groups=mesh['seq'=64,'tp'=4] {'tp'}, dimensions={0}, use_global_device_ids=true | all-gather | bytes 1105920 | tf_op jit(solution)/shard_map/all_gather | solution.py:391
  127.0 1.8 %slice_bitcast_fusion.w_ref = bf16[864,1152]{1,0:T(8,128)(2,1)S(1)} fusion(bf16[2,864,1152]{2,1,0:T(8,128)(2,1)} %bitcast.22), kind=kLoop, calls=%fused_computation | loop fusion | bytes 3981312 | tf_op jit(solution)/shard_map/squeeze | solution.py:304
  128.8 2.8 %shard_map.98 = (bf16[64,1152]{1,0:T(8,128)(2,1)S(1)}, bf16[64,1152]{1,0:T(8,128)(2,1)S(1)}, bf16[64,1152]{1,0:T(8,128)(2,1)S(1)}, bf16[64,1152]{1,0:T(8,128)(2,1)S(1)}) custom-call(s32[1]{0:T(128)} %bitcast.me_ref, bf16[4,96,1152]{2,1,0:T(8,128)(2,1)S(1)} %bitcast.18, bf16[3,256,288]{2,1,0:T(8,128)(2,1)S(1)} %copy-done.6, ...), custom_call_target="tpu_custom_call" | custom-call | flops 1500000000 | tf_op jit(solution)/shard_map/pallas_call | solution.py:278
  131.6 0.9 collective-permute-start.9
  132.5 2.7 %collective-permute-start.10 = (bf16[64,1152]{1,0:T(8,128)(2,1)S(1)}, bf16[64,1152]{1,0:T(8,128)(2,1)S(1)}, u32[]{:S(2)}, u32[]{:S(2)}) collective-permute-start(bf16[64,1152]{1,0:T(8,128)(2,1)S(1)} %get-tuple-element.54), channel_id=1, source_target_pairs={{0,2},{1,3},{2,0},{3,1},{4,6},{5,7},{6,4},{7,5},{8,10},{9,11},{10,... | collective-permute-start | bytes 442376 | tf_op jit(solution)/shard_map/ppermute | solution.py:295
  135.2 1.8 %collective-permute-start.11 = (bf16[64,1152]{1,0:T(8,128)(2,1)S(1)}, bf16[64,1152]{1,0:T(8,128)(2,1)S(1)}, u32[]{:S(2)}, u32[]{:S(2)}) collective-permute-start(bf16[64,1152]{1,0:T(8,128)(2,1)S(1)} %get-tuple-element.55), channel_id=1, source_target_pairs={{0,3},{1,0},{2,1},{3,2},{4,7},{5,4},{6,5},{7,6},{8,11},{9,8},{10,9... | collective-permute-start | bytes 442376 | tf_op jit(solution)/shard_map/ppermute | solution.py:295
  137.0 0.9 collective-permute-done.9.b1
  137.9 6.6 %collective-permute-done.10.b2 = bf16[64,1152]{1,0:T(8,128)(2,1)S(1)} collective-permute-done((bf16[64,1152]{1,0:T(8,128)(2,1)S(1)}, bf16[64,1152]{1,0:T(8,128)(2,1)S(1)}, u32[]{:S(2)}, u32[]{:S(2)}) %collective-permute-start.10) | collective-permute-done | bytes 147488 | tf_op jit(solution)/shard_map/ppermute | solution.py:295
  144.5 3.3 %collective-permute-done.11.b3 = bf16[64,1152]{1,0:T(8,128)(2,1)S(1)} collective-permute-done((bf16[64,1152]{1,0:T(8,128)(2,1)S(1)}, bf16[64,1152]{1,0:T(8,128)(2,1)S(1)}, u32[]{:S(2)}, u32[]{:S(2)}) %collective-permute-start.11) | collective-permute-done | bytes 147488 | tf_op jit(solution)/shard_map/ppermute | solution.py:295
  147.9 0.4 shard_map.99
  148.3 18.9 %all-gather.1 = bf16[384,1152]{1,0:T(8,128)(2,1)S(1)} all-gather(bf16[96,1152]{1,0:T(8,128)(2,1)S(1)} %shard_map.99), channel_id=3, replica_groups=mesh['seq'=64,'tp'=4] {'tp'}, dimensions={0}, use_global_device_ids=true | all-gather | bytes 1105920 | tf_op jit(solution)/shard_map/all_gather | solution.py:405
  167.2 1.4 shard_map.100
  (21 shorter events, 0.1 us)
Async XLA Ops:
  0.6 17.4 %copy-start.2 = (f32[2,1152]{1,0:T(2,128)S(1)}, f32[2,1152]{1,0:T(2,128)}, u32[]{:S(2)}) copy-start(f32[2,1152]{1,0:T(2,128)} %gate_ref.1) | copy-start | bytes 27652
  0.6 63.4 %copy-start.8 = (bf16[2,288,1152]{2,1,0:T(8,128)(2,1)S(1)}, bf16[2,288,1152]{2,1,0:T(8,128)(2,1)}, u32[]{:S(2)}) copy-start(bf16[2,288,1152]{2,1,0:T(8,128)(2,1)} %ow_hbm.1) | copy-start | bytes 3981316
  6.7 11.4 %collective-permute-start = (bf16[64,1152]{1,0:T(8,128)(2,1)}, bf16[64,1152]{1,0:T(8,128)(2,1)S(1)}, u32[]{:S(2)}, u32[]{:S(2)}) collective-permute-start(bf16[64,1152]{1,0:T(8,128)(2,1)} %get-tuple-element.32), channel_id=1, source_target_pairs={{0,1},{1,2},{2,3},{3,0},{4,5},{5,6},{6,7},{7,4},{8,9},{9,10},{10,1... | collective-permute-start | bytes 442376 | tf_op jit(solution)/shard_map/ppermute | solution.py:295
  10.6 14.8 %collective-permute-start.1 = (bf16[64,1152]{1,0:T(8,128)(2,1)}, bf16[64,1152]{1,0:T(8,128)(2,1)S(1)}, u32[]{:S(2)}, u32[]{:S(2)}) collective-permute-start(bf16[64,1152]{1,0:T(8,128)(2,1)} %get-tuple-element.33), channel_id=1, source_target_pairs={{0,3},{1,0},{2,1},{3,2},{4,7},{5,4},{6,5},{7,6},{8,11},{9,8},{10,9... | collective-permute-start | bytes 442376 | tf_op jit(solution)/shard_map/ppermute | solution.py:295
  13.7 13.5 %collective-permute-start.2 = (bf16[64,1152]{1,0:T(8,128)(2,1)}, bf16[64,1152]{1,0:T(8,128)(2,1)S(1)}, u32[]{:S(2)}, u32[]{:S(2)}) collective-permute-start(bf16[64,1152]{1,0:T(8,128)(2,1)} %get-tuple-element.34), channel_id=1, source_target_pairs={{0,2},{1,3},{2,0},{3,1},{4,6},{5,7},{6,4},{7,5},{8,10},{9,11},{10,... | collective-permute-start | bytes 442376 | tf_op jit(solution)/shard_map/ppermute | solution.py:295
  18.1 0.9 copy-start.4
  19.0 0.9 copy-start.7
  64.1 1.8 %copy-start = (bf16[4,64,1152]{2,1,0:T(8,128)(2,1)S(1)}, bf16[4,64,1152]{2,1,0:T(8,128)(2,1)}, u32[]{:S(2)}) copy-start(bf16[4,64,1152]{2,1,0:T(8,128)(2,1)} %refs_1_.14) | copy-start | bytes 1769476
  64.1 1.8 %copy-start.1 = (f32[2,1152]{1,0:T(2,128)S(1)}, f32[2,1152]{1,0:T(2,128)}, u32[]{:S(2)}) copy-start(f32[2,1152]{1,0:T(2,128)} %scale_ref.3) | copy-start | bytes 27652
  64.2 1.8 %copy-start.3 = (f32[2,1152]{1,0:T(2,128)S(1)}, f32[2,1152]{1,0:T(2,128)}, u32[]{:S(2)}) copy-start(f32[2,1152]{1,0:T(2,128)} %refs_4_.7) | copy-start | bytes 27652
  68.3 19.4 %collective-permute-start.3 = (bf16[64,1152]{1,0:T(8,128)(2,1)S(1)}, bf16[64,1152]{1,0:T(8,128)(2,1)S(1)}, u32[]{:S(2)}, u32[]{:S(2)}) collective-permute-start(bf16[64,1152]{1,0:T(8,128)(2,1)S(1)} %get-tuple-element.38), channel_id=1, source_target_pairs={{0,2},{1,3},{2,0},{3,1},{4,6},{5,7},{6,4},{7,5},{8,10},{9,11},{10,... | collective-permute-start | bytes 442376 | tf_op jit(solution)/shard_map/ppermute | solution.py:295
  74.1 13.6 %collective-permute-start.4 = (bf16[64,1152]{1,0:T(8,128)(2,1)S(1)}, bf16[64,1152]{1,0:T(8,128)(2,1)S(1)}, u32[]{:S(2)}, u32[]{:S(2)}) collective-permute-start(bf16[64,1152]{1,0:T(8,128)(2,1)S(1)} %get-tuple-element.39), channel_id=1, source_target_pairs={{0,3},{1,0},{2,1},{3,2},{4,7},{5,4},{6,5},{7,6},{8,11},{9,8},{10,9... | collective-permute-start | bytes 442376 | tf_op jit(solution)/shard_map/ppermute | solution.py:295
  78.6 9.1 %collective-permute-start.5 = (bf16[64,1152]{1,0:T(8,128)(2,1)S(1)}, bf16[64,1152]{1,0:T(8,128)(2,1)S(1)}, u32[]{:S(2)}, u32[]{:S(2)}) collective-permute-start(bf16[64,1152]{1,0:T(8,128)(2,1)S(1)} %get-tuple-element.40), channel_id=1, source_target_pairs={{0,1},{1,2},{2,3},{3,0},{4,5},{5,6},{6,7},{7,4},{8,9},{9,10},{10,1... | collective-permute-start | bytes 442376 | tf_op jit(solution)/shard_map/ppermute | solution.py:295
  81.4 17.5 %collective-permute-start.6 = (bf16[64,1152]{1,0:T(8,128)(2,1)S(1)}, bf16[64,1152]{1,0:T(8,128)(2,1)S(1)}, u32[]{:S(2)}, u32[]{:S(2)}) collective-permute-start(bf16[64,1152]{1,0:T(8,128)(2,1)S(1)} %get-tuple-element.46), channel_id=1, source_target_pairs={{0,3},{1,0},{2,1},{3,2},{4,7},{5,4},{6,5},{7,6},{8,11},{9,8},{10,9... | collective-permute-start | bytes 442376 | tf_op jit(solution)/shard_map/ppermute | solution.py:295
  84.7 15.3 %collective-permute-start.7 = (bf16[64,1152]{1,0:T(8,128)(2,1)S(1)}, bf16[64,1152]{1,0:T(8,128)(2,1)S(1)}, u32[]{:S(2)}, u32[]{:S(2)}) collective-permute-start(bf16[64,1152]{1,0:T(8,128)(2,1)S(1)} %get-tuple-element.47), channel_id=1, source_target_pairs={{0,2},{1,3},{2,0},{3,1},{4,6},{5,7},{6,4},{7,5},{8,10},{9,11},{10,... | collective-permute-start | bytes 442376 | tf_op jit(solution)/shard_map/ppermute | solution.py:295
  87.7 14.3 %collective-permute-start.8 = (bf16[64,1152]{1,0:T(8,128)(2,1)S(1)}, bf16[64,1152]{1,0:T(8,128)(2,1)S(1)}, u32[]{:S(2)}, u32[]{:S(2)}) collective-permute-start(bf16[64,1152]{1,0:T(8,128)(2,1)S(1)} %get-tuple-element.48), channel_id=1, source_target_pairs={{0,1},{1,2},{2,3},{3,0},{4,5},{5,6},{6,7},{7,4},{8,9},{9,10},{10,1... | collective-permute-start | bytes 442376 | tf_op jit(solution)/shard_map/ppermute | solution.py:295
  88.9 16.5 %all-to-all-start.1 = ((bf16[64,2,576]{2,1,0:T(2,128)(2,1)}), bf16[64,2,576]{2,1,0:T(2,128)(2,1)S(1)}, u32[]{:S(2)}, u32[]{:S(2)}) async-start(bf16[64,2,576]{2,1,0:T(2,128)(2,1)} %shard_map.95), calls=%async_computation.1 | async-start | bytes 327680 | tf_op jit(solution)/shard_map/all_to_all | solution.py:299
  127.0 1.8 %copy-start.6 = (bf16[3,256,288]{2,1,0:T(8,128)(2,1)S(1)}, bf16[3,256,288]{2,1,0:T(8,128)(2,1)}, u32[]{:S(2)}) copy-start(bf16[3,256,288]{2,1,0:T(8,128)(2,1)} %get-tuple-element.49.qkv_ref) | copy-start | bytes 1327108
  128.7 19.1 %copy-start.5 = (bf16[64,1152]{1,0:T(8,128)(2,1)S(1)}, bf16[64,1152]{1,0:T(8,128)(2,1)}, u32[]{:S(2)}) copy-start(bf16[64,1152]{1,0:T(8,128)(2,1)} %get-tuple-element.30.refs_0_.x_ref) | copy-start | bytes 442372
  131.6 6.3 %collective-permute-start.9 = (bf16[64,1152]{1,0:T(8,128)(2,1)S(1)}, bf16[64,1152]{1,0:T(8,128)(2,1)S(1)}, u32[]{:S(2)}, u32[]{:S(2)}) collective-permute-start(bf16[64,1152]{1,0:T(8,128)(2,1)S(1)} %get-tuple-element.53), channel_id=1, source_target_pairs={{0,1},{1,2},{2,3},{3,0},{4,5},{5,6},{6,7},{7,4},{8,9},{9,10},{10,1... | collective-permute-start | bytes 442376 | tf_op jit(solution)/shard_map/ppermute | solution.py:295
  132.5 12.0 %collective-permute-start.10 = (bf16[64,1152]{1,0:T(8,128)(2,1)S(1)}, bf16[64,1152]{1,0:T(8,128)(2,1)S(1)}, u32[]{:S(2)}, u32[]{:S(2)}) collective-permute-start(bf16[64,1152]{1,0:T(8,128)(2,1)S(1)} %get-tuple-element.54), channel_id=1, source_target_pairs={{0,2},{1,3},{2,0},{3,1},{4,6},{5,7},{6,4},{7,5},{8,10},{9,11},{10,... | collective-permute-start | bytes 442376 | tf_op jit(solution)/shard_map/ppermute | solution.py:295
  135.2 12.7 %collective-permute-start.11 = (bf16[64,1152]{1,0:T(8,128)(2,1)S(1)}, bf16[64,1152]{1,0:T(8,128)(2,1)S(1)}, u32[]{:S(2)}, u32[]{:S(2)}) collective-permute-start(bf16[64,1152]{1,0:T(8,128)(2,1)S(1)} %get-tuple-element.55), channel_id=1, source_target_pairs={{0,3},{1,0},{2,1},{3,2},{4,7},{5,4},{6,5},{7,6},{8,11},{9,8},{10,9... | collective-permute-start | bytes 442376 | tf_op jit(solution)/shard_map/ppermute | solution.py:295

commit v6 on v5

--- a/solution.py
+++ b/solution.py
@@ -243,14 +243,17 @@
     sent_ref[ROWS:] = result_ref[:HALF]
 
 
-def pack_last(x_ref, g_ref, scale_ref, b0, b1, b2, b3, result_ref, sent_ref):
-    grad_of(0, x_ref, g_ref, scale_ref, b0, b1, b2, b3, sent_ref.at[:ROWS])
+def pack_last(x_ref, g_ref, scale_ref, early, b3, b2, result_ref, sent_ref):
+    grad_of(0, x_ref, g_ref, scale_ref, early, b3, b2, sent_ref.at[:ROWS])
     sent_ref[ROWS:] = result_ref[HALF:]
 
 
 def unpack(first_ref, last_ref, ends_ref, result_ref, grad_ref):
     stacked = jnp.concatenate([ends_ref[chunk] for chunk in range(4)], axis=0)
-    grad_ref[...] = tn(order_matrix(0, 256), stacked).astype(BF16)
+    patch = lax.broadcasted_iota(jnp.int32, (256, 256), 0)
+    place = lax.broadcasted_iota(jnp.int32, (256, 256), 1)
+    order = (patch == 4 * (place % ROWS) + place // ROWS).astype(F32).astype(BF16)
+    grad_ref[...] = nn(order, stacked).astype(BF16)
     result_ref[:, :HALF] = first_ref[...]
     result_ref[:, HALF:] = last_ref[...]
 
@@ -397,9 +400,10 @@
         scratch=(pltpu.VMEM((256, D), BF16),),
     )
     b1, b3, b2 = shift(b1, 1), shift(b3, 3), shift(b2, 2)
+    early = run(add_in, None, (b0, b2), [QUARTER] * 2, rows_out(F32), QUARTER, 350_000_000)
     packed = run(
-        pack_last, None, (own, packed, mod_scale, b0, b1, b2, b3, result_own),
-        [QUARTER] * 2 + [VECTORS] + [QUARTER] * 5,
+        pack_last, None, (own, packed, mod_scale, early, b1, b3, result_own),
+        [QUARTER] * 2 + [VECTORS] + [QUARTER] * 4,
         message, whole((ROWS + HALF, D)), 1_000_000,
     )
     ends = lax.all_gather(packed, "tp")

time: 169 us -> 168 us (level); the launches traced: 169 us -> 166 us
  blocking collectives: 76.6 us -> 74 us
    all_gather x1, blocking collectives: 18.9 us -> 16.3 us  [per_device(): ends = lax.all_gather(packed, 'tp')]
    pallas_call x15 -> x16, Pallas kernels: 21.7 us -> 21.6 us  [run(): pl.pallas_call(body, grid_spec=pltpu.PrefetchScalarGridSpec(num_scalar_pr...]
  transfers between devices with their start and end apart: 13 -> 13, of which waited for: 9 -> 8; matrix products, arithmetic and copies ran while one was open for 0% -> 0% of each run, Pallas kernels for 5% -> 5%
where the time goes in v6:
time: 168 us; the launch traced here: 166 us
  blocking collectives  74 us (44%)
  starting transfers between devices  36.9 us (22%)
  waiting for transfers between devices  26.7 us (16%)
  Pallas kernels  21.6 us (13%)
  local copies, waits for them, and re-layouts  5.77 us (3%)
    ppermute x12, starting transfers between devices, shift(): return lax.ppermute(array, 'tp', [(i, (i + k) % N_TP) for i in range(N_TP)])  29.3 us
    ppermute x12, waiting for transfers between devices, shift(): return lax.ppermute(array, 'tp', [(i, (i + k) % N_TP) for i in range(N_TP)])  23.4 us
    pallas_call x16, Pallas kernels, run(): pl.pallas_call(body, grid_spec=pltpu.PrefetchScalarGridSpec(num_scalar_pr...  21.6 us
    all_to_all x1, blocking collectives, across(): return lax.all_to_all(array, 'seq', split_axis=0, concat_axis=0, tiled=True)  21.4 us
    all_gather x1, blocking collectives, per_device(): grads = lax.all_gather(packed, 'tp')  21.2 us
    all_gather x1, blocking collectives, per_device(): ends = lax.all_gather(packed, 'tp')  16.3 us
    all_gather x1, blocking collectives, per_device(): mids = lax.all_gather(mid_own, 'tp')  15 us
    all_to_all x1, starting transfers between devices, across(): return lax.all_to_all(array, 'seq', split_axis=0, concat_axis=0, tiled=True)  7.64 us
  transfers between devices with their start and end apart: 13, of which 8 were waited for; matrix products, arithmetic and copies ran while one was open for 0% of the time, Pallas kernels for 5%

profile of v6, /device:TPU:1, one launch (start us, length us, event | category | flops | bytes accessed | tf_op | source)
XLA Modules:
  0.0 165.9 jit_solution(15829059347521680388)
XLA Ops:
  0.7 6.0 %shard_map.86 = (bf16[64,1152]{1,0:T(8,128)(2,1)}, bf16[64,1152]{1,0:T(8,128)(2,1)}, bf16[64,1152]{1,0:T(8,128)(2,1)}, bf16[64,1152]{1,0:T(8,128)(2,1)}, bf16[3,...) custom-call(s32[1]{0:T(128)} %bitcast.me_ref, bf16[256,1152]{1,0:T(8,128)(2,1)} %bitcast.23, ...), custom_call_target="tpu_custom_call" | custom-call | flops 1000000000 | tf_op jit(solution)/shard_map/pallas_call | solution.py:281
  6.7 3.9 %collective-permute-start = (bf16[64,1152]{1,0:T(8,128)(2,1)}, bf16[64,1152]{1,0:T(8,128)(2,1)S(1)}, u32[]{:S(2)}, u32[]{:S(2)}) collective-permute-start(bf16[64,1152]{1,0:T(8,128)(2,1)} %get-tuple-element.32), channel_id=1, source_target_pairs={{0,1},{1,2},{2,3},{3,0},{4,5},{5,6},{6,7},{7,4},{8,9},{9,10},{10,1... | collective-permute-start | bytes 442376 | tf_op jit(solution)/shard_map/ppermute | solution.py:298
  10.6 3.1 %collective-permute-start.1 = (bf16[64,1152]{1,0:T(8,128)(2,1)}, bf16[64,1152]{1,0:T(8,128)(2,1)S(1)}, u32[]{:S(2)}, u32[]{:S(2)}) collective-permute-start(bf16[64,1152]{1,0:T(8,128)(2,1)} %get-tuple-element.33), channel_id=1, source_target_pairs={{0,3},{1,0},{2,1},{3,2},{4,7},{5,4},{6,5},{7,6},{8,11},{9,8},{10,9... | collective-permute-start | bytes 442376 | tf_op jit(solution)/shard_map/ppermute | solution.py:298
  13.7 4.4 %collective-permute-start.2 = (bf16[64,1152]{1,0:T(8,128)(2,1)}, bf16[64,1152]{1,0:T(8,128)(2,1)S(1)}, u32[]{:S(2)}, u32[]{:S(2)}) collective-permute-start(bf16[64,1152]{1,0:T(8,128)(2,1)} %get-tuple-element.34), channel_id=1, source_target_pairs={{0,2},{1,3},{2,0},{3,1},{4,6},{5,7},{6,4},{7,5},{8,10},{9,11},{10,... | collective-permute-start | bytes 442376 | tf_op jit(solution)/shard_map/ppermute | solution.py:298
  18.1 0.9 copy-done.4
  19.0 0.9 copy-done.7
  19.9 0.1 shard_map.87.refs_0_
  20.0 5.4 %collective-permute-done.1.refs_2_ = bf16[64,1152]{1,0:T(8,128)(2,1)S(1)} collective-permute-done((bf16[64,1152]{1,0:T(8,128)(2,1)}, bf16[64,1152]{1,0:T(8,128)(2,1)S(1)}, u32[]{:S(2)}, u32[]{:S(2)}) %collective-permute-start.1) | collective-permute-done | bytes 147488 | tf_op jit(solution)/shard_map/ppermute | solution.py:298
  25.3 1.8 %collective-permute-done.2.refs_3_ = bf16[64,1152]{1,0:T(8,128)(2,1)S(1)} collective-permute-done((bf16[64,1152]{1,0:T(8,128)(2,1)}, bf16[64,1152]{1,0:T(8,128)(2,1)S(1)}, u32[]{:S(2)}, u32[]{:S(2)}) %collective-permute-start.2) | collective-permute-done | bytes 147488 | tf_op jit(solution)/shard_map/ppermute | solution.py:298
  27.1 0.2 shard_map.88
  27.3 21.4 %all_to_all.10 = bf16[64,2,576]{2,1,0:T(2,128)(2,1)S(1)} all-to-all(bf16[64,2,576]{2,1,0:T(2,128)(2,1)S(1)} %shard_map.88), channel_id=1, replica_groups=mesh['seq'=64,'tp'=4] {'seq'}, dimensions={0} | all-to-all | bytes 294912 | tf_op jit(solution)/shard_map/all_to_all | solution.py:302
  48.8 0.1 reshape.22.refs_0_
  48.9 0.1 all_gather_reshape.3
  49.0 15.0 %all_gather.15.refs_0_ = bf16[4,64,1152]{2,1,0:T(8,128)(2,1)S(1)} all-gather(bf16[1,64,1152]{2,1,0:T(8,128)(2,1)S(1)} %all_gather_reshape.3), channel_id=1, replica_groups=mesh['seq'=64,'tp'=4] {'tp'}, dimensions={0}, use_global_device_ids=true | all-gather | bytes 737280 | tf_op jit(solution)/shard_map/all_gather | solution.py:348
  64.1 0.1 slice_bitcast_fusion.3.refs_3_
  64.1 0.0 copy-start
  64.1 0.0 copy-start.1
  64.2 0.0 copy-start.3
  64.2 1.8 %slice_bitcast_fusion.1.refs_2_ = bf16[864,1152]{1,0:T(8,128)(2,1)S(1)} fusion(bf16[2,864,1152]{2,1,0:T(8,128)(2,1)} %bitcast.21), kind=kLoop, calls=%fused_computation.1 | loop fusion | bytes 3981312 | tf_op jit(solution)/shard_map/squeeze | solution.py:307
  66.0 2.3 %shard_map.90 = (bf16[64,1152]{1,0:T(8,128)(2,1)S(1)}, bf16[64,1152]{1,0:T(8,128)(2,1)S(1)}) custom-call(s32[1]{0:T(128)} %bitcast.me_ref, bf16[4,64,1152]{2,1,0:T(8,128)(2,1)S(1)} %all_gather.15.refs_0_, bf16[4,64,1152]{2,1,0:T(8,128)(2,1)S(1)} %copy-done, bf16[864,1152]{1,0:T(8,128)(2,1)S(1)} %slice_bitcast_fusion.1.refs_2_, ...), custom_call_target="tpu_custom_call" | custom-call | flops 50000000 | tf_op jit(solution)/shard_map/pallas_call | solution.py:281
  68.3 3.5 %collective-permute-start.3 = (bf16[64,1152]{1,0:T(8,128)(2,1)S(1)}, bf16[64,1152]{1,0:T(8,128)(2,1)S(1)}, u32[]{:S(2)}, u32[]{:S(2)}) collective-permute-start(bf16[64,1152]{1,0:T(8,128)(2,1)S(1)} %get-tuple-element.38), channel_id=1, source_target_pairs={{0,2},{1,3},{2,0},{3,1},{4,6},{5,7},{6,4},{7,5},{8,10},{9,11},{10,... | collective-permute-start | bytes 442376 | tf_op jit(solution)/shard_map/ppermute | solution.py:298
  71.8 2.3 %shard_map.92 = (bf16[64,1152]{1,0:T(8,128)(2,1)S(1)}, bf16[64,1152]{1,0:T(8,128)(2,1)S(1)}) custom-call(s32[1]{0:T(128)} %bitcast.me_ref, bf16[4,64,1152]{2,1,0:T(8,128)(2,1)S(1)} %all_gather.15.refs_0_, bf16[4,64,1152]{2,1,0:T(8,128)(2,1)S(1)} %copy-done, bf16[864,1152]{1,0:T(8,128)(2,1)S(1)} %slice_bitcast_fusion.1.refs_2_, ...), custom_call_target="tpu_custom_call" | custom-call | flops 50000000 | tf_op jit(solution)/shard_map/pallas_call | solution.py:281
  74.1 2.2 %collective-permute-start.4 = (bf16[64,1152]{1,0:T(8,128)(2,1)S(1)}, bf16[64,1152]{1,0:T(8,128)(2,1)S(1)}, u32[]{:S(2)}, u32[]{:S(2)}) collective-permute-start(bf16[64,1152]{1,0:T(8,128)(2,1)S(1)} %get-tuple-element.39), channel_id=1, source_target_pairs={{0,3},{1,0},{2,1},{3,2},{4,7},{5,4},{6,5},{7,6},{8,11},{9,8},{10,9... | collective-permute-start | bytes 442376 | tf_op jit(solution)/shard_map/ppermute | solution.py:298
  76.3 2.3 %shard_map.94 = (bf16[64,1152]{1,0:T(8,128)(2,1)S(1)}, bf16[64,1152]{1,0:T(8,128)(2,1)S(1)}) custom-call(s32[1]{0:T(128)} %bitcast.me_ref, bf16[4,64,1152]{2,1,0:T(8,128)(2,1)S(1)} %all_gather.15.refs_0_, bf16[4,64,1152]{2,1,0:T(8,128)(2,1)S(1)} %copy-done, bf16[864,1152]{1,0:T(8,128)(2,1)S(1)} %slice_bitcast_fusion.1.refs_2_, ...), custom_call_target="tpu_custom_call" | custom-call | flops 50000000 | tf_op jit(solution)/shard_map/pallas_call | solution.py:281
  78.6 0.5 collective-permute-start.5
  79.1 2.3 %shard_map.89 = (bf16[64,1152]{1,0:T(8,128)(2,1)S(1)}, bf16[64,1152]{1,0:T(8,128)(2,1)S(1)}) custom-call(s32[1]{0:T(128)} %bitcast.me_ref, bf16[4,64,1152]{2,1,0:T(8,128)(2,1)S(1)} %all_gather.15.refs_0_, bf16[4,64,1152]{2,1,0:T(8,128)(2,1)S(1)} %copy-done, bf16[864,1152]{1,0:T(8,128)(2,1)S(1)} %slice_bitcast_fusion.1.refs_2_, ...), custom_call_target="tpu_custom_call" | custom-call | flops 350000000 | tf_op jit(solution)/shard_map/pallas_call | solution.py:281
  81.4 3.3 %collective-permute-start.6 = (bf16[64,1152]{1,0:T(8,128)(2,1)S(1)}, bf16[64,1152]{1,0:T(8,128)(2,1)S(1)}, u32[]{:S(2)}, u32[]{:S(2)}) collective-permute-start(bf16[64,1152]{1,0:T(8,128)(2,1)S(1)} %get-tuple-element.46), channel_id=1, source_target_pairs={{0,3},{1,0},{2,1},{3,2},{4,7},{5,4},{6,5},{7,6},{8,11},{9,8},{10,9... | collective-permute-start | bytes 442376 | tf_op jit(solution)/shard_map/ppermute | solution.py:298
  84.7 3.0 %collective-permute-start.7 = (bf16[64,1152]{1,0:T(8,128)(2,1)S(1)}, bf16[64,1152]{1,0:T(8,128)(2,1)S(1)}, u32[]{:S(2)}, u32[]{:S(2)}) collective-permute-start(bf16[64,1152]{1,0:T(8,128)(2,1)S(1)} %get-tuple-element.47), channel_id=1, source_target_pairs={{0,2},{1,3},{2,0},{3,1},{4,6},{5,7},{6,4},{7,5},{8,10},{9,11},{10,... | collective-permute-start | bytes 442376 | tf_op jit(solution)/shard_map/ppermute | solution.py:298
  87.8 1.1 shard_map.95
  88.9 7.6 %all-to-all-start.1 = ((bf16[64,2,576]{2,1,0:T(2,128)(2,1)}), bf16[64,2,576]{2,1,0:T(2,128)(2,1)S(1)}, u32[]{:S(2)}, u32[]{:S(2)}) async-start(bf16[64,2,576]{2,1,0:T(2,128)(2,1)} %shard_map.95), calls=%async_computation.1 | async-start | bytes 327680 | tf_op jit(solution)/shard_map/all_to_all | solution.py:302
  96.5 2.3 %collective-permute-done.6.refs_3_ = bf16[64,1152]{1,0:T(8,128)(2,1)S(1)} collective-permute-done((bf16[64,1152]{1,0:T(8,128)(2,1)S(1)}, bf16[64,1152]{1,0:T(8,128)(2,1)S(1)}, u32[]{:S(2)}, u32[]{:S(2)}) %collective-permute-start.6) | collective-permute-done | bytes 147488 | tf_op jit(solution)/shard_map/ppermute | solution.py:298
  98.9 1.1 collective-permute-done.7.refs_4_
  100.0 2.0 %collective-permute-done.8.refs_5_ = bf16[64,1152]{1,0:T(8,128)(2,1)S(1)} collective-permute-done((bf16[64,1152]{1,0:T(8,128)(2,1)S(1)}, bf16[64,1152]{1,0:T(8,128)(2,1)S(1)}, u32[]{:S(2)}, u32[]{:S(2)}) %collective-permute-start.8) | collective-permute-done | bytes 147488 | tf_op jit(solution)/shard_map/ppermute | solution.py:298
  102.0 0.1 shard_map.96.result_ref
  102.1 3.3 %all-to-all-done.1.grad_ref = bf16[64,2,576]{2,1,0:T(2,128)(2,1)S(1)} async-done(((bf16[64,2,576]{2,1,0:T(2,128)(2,1)}), bf16[64,2,576]{2,1,0:T(2,128)(2,1)S(1)}, u32[]{:S(2)}, u32[]{:S(2)}) %all-to-all-start.1) | async-done | bytes 147488 | tf_op jit(solution)/shard_map/all_to_all | solution.py:302
  105.4 0.1 slice_bitcast_fusion.2.ow_ref
  105.4 0.4 shard_map.97.g_ref
  105.8 21.2 %all-gather = bf16[384,1152]{1,0:T(8,128)(2,1)S(1)} all-gather(bf16[96,1152]{1,0:T(8,128)(2,1)S(1)} %shard_map.97.g_ref), channel_id=2, replica_groups=mesh['seq'=64,'tp'=4] {'tp'}, dimensions={0}, use_global_device_ids=true | all-gather | bytes 1105920 | tf_op jit(solution)/shard_map/all_gather | solution.py:394
  127.0 1.8 %slice_bitcast_fusion.w_ref = bf16[864,1152]{1,0:T(8,128)(2,1)S(1)} fusion(bf16[2,864,1152]{2,1,0:T(8,128)(2,1)} %bitcast.22), kind=kLoop, calls=%fused_computation | loop fusion | bytes 3981312 | tf_op jit(solution)/shard_map/squeeze | solution.py:307
  128.8 2.8 %shard_map.98 = (bf16[64,1152]{1,0:T(8,128)(2,1)S(1)}, bf16[64,1152]{1,0:T(8,128)(2,1)S(1)}, bf16[64,1152]{1,0:T(8,128)(2,1)S(1)}, bf16[64,1152]{1,0:T(8,128)(2,1)S(1)}) custom-call(s32[1]{0:T(128)} %bitcast.me_ref, bf16[4,96,1152]{2,1,0:T(8,128)(2,1)S(1)} %bitcast.18, bf16[3,256,288]{2,1,0:T(8,128)(2,1)S(1)} %copy-done.6, ...), custom_call_target="tpu_custom_call" | custom-call | flops 1500000000 | tf_op jit(solution)/shard_map/pallas_call | solution.py:281
  131.6 1.8 %collective-permute-start.9 = (bf16[64,1152]{1,0:T(8,128)(2,1)S(1)}, bf16[64,1152]{1,0:T(8,128)(2,1)S(1)}, u32[]{:S(2)}, u32[]{:S(2)}) collective-permute-start(bf16[64,1152]{1,0:T(8,128)(2,1)S(1)} %get-tuple-element.53), channel_id=1, source_target_pairs={{0,2},{1,3},{2,0},{3,1},{4,6},{5,7},{6,4},{7,5},{8,10},{9,11},{10,... | collective-permute-start | bytes 442376 | tf_op jit(solution)/shard_map/ppermute | solution.py:298
  133.4 1.8 %collective-permute-start.10 = (bf16[64,1152]{1,0:T(8,128)(2,1)S(1)}, bf16[64,1152]{1,0:T(8,128)(2,1)S(1)}, u32[]{:S(2)}, u32[]{:S(2)}) collective-permute-start(bf16[64,1152]{1,0:T(8,128)(2,1)S(1)} %get-tuple-element.54), channel_id=1, source_target_pairs={{0,1},{1,2},{2,3},{3,0},{4,5},{5,6},{6,7},{7,4},{8,9},{9,10},{10,1... | collective-permute-start | bytes 442376 | tf_op jit(solution)/shard_map/ppermute | solution.py:298
  135.2 1.8 %collective-permute-start.11 = (bf16[64,1152]{1,0:T(8,128)(2,1)S(1)}, bf16[64,1152]{1,0:T(8,128)(2,1)S(1)}, u32[]{:S(2)}, u32[]{:S(2)}) collective-permute-start(bf16[64,1152]{1,0:T(8,128)(2,1)S(1)} %get-tuple-element.55), channel_id=1, source_target_pairs={{0,3},{1,0},{2,1},{3,2},{4,7},{5,4},{6,5},{7,6},{8,11},{9,8},{10,9... | collective-permute-start | bytes 442376 | tf_op jit(solution)/shard_map/ppermute | solution.py:298
  137.0 2.7 %collective-permute-done.9.b_ref = bf16[64,1152]{1,0:T(8,128)(2,1)S(1)} collective-permute-done((bf16[64,1152]{1,0:T(8,128)(2,1)S(1)}, bf16[64,1152]{1,0:T(8,128)(2,1)S(1)}, u32[]{:S(2)}, u32[]{:S(2)}) %collective-permute-start.9) | collective-permute-done | bytes 147488 | tf_op jit(solution)/shard_map/ppermute | solution.py:298
  139.8 8.0 %collective-permute-done.10.b3 = bf16[64,1152]{1,0:T(8,128)(2,1)S(1)} collective-permute-done((bf16[64,1152]{1,0:T(8,128)(2,1)S(1)}, bf16[64,1152]{1,0:T(8,128)(2,1)S(1)}, u32[]{:S(2)}, u32[]{:S(2)}) %collective-permute-start.10) | collective-permute-done | bytes 147488 | tf_op jit(solution)/shard_map/ppermute | solution.py:298
  147.8 0.3 shard_map.100
  148.2 16.3 %all-gather.1 = bf16[384,1152]{1,0:T(8,128)(2,1)S(1)} all-gather(bf16[96,1152]{1,0:T(8,128)(2,1)S(1)} %shard_map.100), channel_id=3, replica_groups=mesh['seq'=64,'tp'=4] {'tp'}, dimensions={0}, use_global_device_ids=true | all-gather | bytes 1105920 | tf_op jit(solution)/shard_map/all_gather | solution.py:409
  164.5 1.3 shard_map.101
  (22 shorter events, 0.1 us)
Async XLA Ops:
  0.6 17.4 %copy-start.2 = (f32[2,1152]{1,0:T(2,128)S(1)}, f32[2,1152]{1,0:T(2,128)}, u32[]{:S(2)}) copy-start(f32[2,1152]{1,0:T(2,128)} %gate_ref.1) | copy-start | bytes 27652
  0.6 63.4 %copy-start.8 = (bf16[2,288,1152]{2,1,0:T(8,128)(2,1)S(1)}, bf16[2,288,1152]{2,1,0:T(8,128)(2,1)}, u32[]{:S(2)}) copy-start(bf16[2,288,1152]{2,1,0:T(8,128)(2,1)} %ow_hbm.1) | copy-start | bytes 3981316
  6.7 11.4 %collective-permute-start = (bf16[64,1152]{1,0:T(8,128)(2,1)}, bf16[64,1152]{1,0:T(8,128)(2,1)S(1)}, u32[]{:S(2)}, u32[]{:S(2)}) collective-permute-start(bf16[64,1152]{1,0:T(8,128)(2,1)} %get-tuple-element.32), channel_id=1, source_target_pairs={{0,1},{1,2},{2,3},{3,0},{4,5},{5,6},{6,7},{7,4},{8,9},{9,10},{10,1... | collective-permute-start | bytes 442376 | tf_op jit(solution)/shard_map/ppermute | solution.py:298
  10.6 14.8 %collective-permute-start.1 = (bf16[64,1152]{1,0:T(8,128)(2,1)}, bf16[64,1152]{1,0:T(8,128)(2,1)S(1)}, u32[]{:S(2)}, u32[]{:S(2)}) collective-permute-start(bf16[64,1152]{1,0:T(8,128)(2,1)} %get-tuple-element.33), channel_id=1, source_target_pairs={{0,3},{1,0},{2,1},{3,2},{4,7},{5,4},{6,5},{7,6},{8,11},{9,8},{10,9... | collective-permute-start | bytes 442376 | tf_op jit(solution)/shard_map/ppermute | solution.py:298
  13.7 13.5 %collective-permute-start.2 = (bf16[64,1152]{1,0:T(8,128)(2,1)}, bf16[64,1152]{1,0:T(8,128)(2,1)S(1)}, u32[]{:S(2)}, u32[]{:S(2)}) collective-permute-start(bf16[64,1152]{1,0:T(8,128)(2,1)} %get-tuple-element.34), channel_id=1, source_target_pairs={{0,2},{1,3},{2,0},{3,1},{4,6},{5,7},{6,4},{7,5},{8,10},{9,11},{10,... | collective-permute-start | bytes 442376 | tf_op jit(solution)/shard_map/ppermute | solution.py:298
  18.1 0.9 copy-start.4
  19.0 0.9 copy-start.7
  64.1 1.8 %copy-start = (bf16[4,64,1152]{2,1,0:T(8,128)(2,1)S(1)}, bf16[4,64,1152]{2,1,0:T(8,128)(2,1)}, u32[]{:S(2)}) copy-start(bf16[4,64,1152]{2,1,0:T(8,128)(2,1)} %refs_1_.14) | copy-start | bytes 1769476
  64.1 1.8 %copy-start.1 = (f32[2,1152]{1,0:T(2,128)S(1)}, f32[2,1152]{1,0:T(2,128)}, u32[]{:S(2)}) copy-start(f32[2,1152]{1,0:T(2,128)} %scale_ref.3) | copy-start | bytes 27652
  64.2 1.8 %copy-start.3 = (f32[2,1152]{1,0:T(2,128)S(1)}, f32[2,1152]{1,0:T(2,128)}, u32[]{:S(2)}) copy-start(f32[2,1152]{1,0:T(2,128)} %refs_4_.7) | copy-start | bytes 27652
  68.3 19.4 %collective-permute-start.3 = (bf16[64,1152]{1,0:T(8,128)(2,1)S(1)}, bf16[64,1152]{1,0:T(8,128)(2,1)S(1)}, u32[]{:S(2)}, u32[]{:S(2)}) collective-permute-start(bf16[64,1152]{1,0:T(8,128)(2,1)S(1)} %get-tuple-element.38), channel_id=1, source_target_pairs={{0,2},{1,3},{2,0},{3,1},{4,6},{5,7},{6,4},{7,5},{8,10},{9,11},{10,... | collective-permute-start | bytes 442376 | tf_op jit(solution)/shard_map/ppermute | solution.py:298
  74.1 13.6 %collective-permute-start.4 = (bf16[64,1152]{1,0:T(8,128)(2,1)S(1)}, bf16[64,1152]{1,0:T(8,128)(2,1)S(1)}, u32[]{:S(2)}, u32[]{:S(2)}) collective-permute-start(bf16[64,1152]{1,0:T(8,128)(2,1)S(1)} %get-tuple-element.39), channel_id=1, source_target_pairs={{0,3},{1,0},{2,1},{3,2},{4,7},{5,4},{6,5},{7,6},{8,11},{9,8},{10,9... | collective-permute-start | bytes 442376 | tf_op jit(solution)/shard_map/ppermute | solution.py:298
  78.6 9.1 %collective-permute-start.5 = (bf16[64,1152]{1,0:T(8,128)(2,1)S(1)}, bf16[64,1152]{1,0:T(8,128)(2,1)S(1)}, u32[]{:S(2)}, u32[]{:S(2)}) collective-permute-start(bf16[64,1152]{1,0:T(8,128)(2,1)S(1)} %get-tuple-element.40), channel_id=1, source_target_pairs={{0,1},{1,2},{2,3},{3,0},{4,5},{5,6},{6,7},{7,4},{8,9},{9,10},{10,1... | collective-permute-start | bytes 442376 | tf_op jit(solution)/shard_map/ppermute | solution.py:298
  81.4 17.5 %collective-permute-start.6 = (bf16[64,1152]{1,0:T(8,128)(2,1)S(1)}, bf16[64,1152]{1,0:T(8,128)(2,1)S(1)}, u32[]{:S(2)}, u32[]{:S(2)}) collective-permute-start(bf16[64,1152]{1,0:T(8,128)(2,1)S(1)} %get-tuple-element.46), channel_id=1, source_target_pairs={{0,3},{1,0},{2,1},{3,2},{4,7},{5,4},{6,5},{7,6},{8,11},{9,8},{10,9... | collective-permute-start | bytes 442376 | tf_op jit(solution)/shard_map/ppermute | solution.py:298
  84.7 15.3 %collective-permute-start.7 = (bf16[64,1152]{1,0:T(8,128)(2,1)S(1)}, bf16[64,1152]{1,0:T(8,128)(2,1)S(1)}, u32[]{:S(2)}, u32[]{:S(2)}) collective-permute-start(bf16[64,1152]{1,0:T(8,128)(2,1)S(1)} %get-tuple-element.47), channel_id=1, source_target_pairs={{0,2},{1,3},{2,0},{3,1},{4,6},{5,7},{6,4},{7,5},{8,10},{9,11},{10,... | collective-permute-start | bytes 442376 | tf_op jit(solution)/shard_map/ppermute | solution.py:298
  87.7 14.3 %collective-permute-start.8 = (bf16[64,1152]{1,0:T(8,128)(2,1)S(1)}, bf16[64,1152]{1,0:T(8,128)(2,1)S(1)}, u32[]{:S(2)}, u32[]{:S(2)}) collective-permute-start(bf16[64,1152]{1,0:T(8,128)(2,1)S(1)} %get-tuple-element.48), channel_id=1, source_target_pairs={{0,1},{1,2},{2,3},{3,0},{4,5},{5,6},{6,7},{7,4},{8,9},{9,10},{10,1... | collective-permute-start | bytes 442376 | tf_op jit(solution)/shard_map/ppermute | solution.py:298
  88.9 16.5 %all-to-all-start.1 = ((bf16[64,2,576]{2,1,0:T(2,128)(2,1)}), bf16[64,2,576]{2,1,0:T(2,128)(2,1)S(1)}, u32[]{:S(2)}, u32[]{:S(2)}) async-start(bf16[64,2,576]{2,1,0:T(2,128)(2,1)} %shard_map.95), calls=%async_computation.1 | async-start | bytes 327680 | tf_op jit(solution)/shard_map/all_to_all | solution.py:302
  127.0 1.8 %copy-start.6 = (bf16[3,256,288]{2,1,0:T(8,128)(2,1)S(1)}, bf16[3,256,288]{2,1,0:T(8,128)(2,1)}, u32[]{:S(2)}) copy-start(bf16[3,256,288]{2,1,0:T(8,128)(2,1)} %get-tuple-element.49.qkv_ref) | copy-start | bytes 1327108
  128.7 19.1 %copy-start.5 = (bf16[64,1152]{1,0:T(8,128)(2,1)S(1)}, bf16[64,1152]{1,0:T(8,128)(2,1)}, u32[]{:S(2)}) copy-start(bf16[64,1152]{1,0:T(8,128)(2,1)} %get-tuple-element.30.refs_0_.x_ref) | copy-start | bytes 442372
  131.6 8.1 %collective-permute-start.9 = (bf16[64,1152]{1,0:T(8,128)(2,1)S(1)}, bf16[64,1152]{1,0:T(8,128)(2,1)S(1)}, u32[]{:S(2)}, u32[]{:S(2)}) collective-permute-start(bf16[64,1152]{1,0:T(8,128)(2,1)S(1)} %get-tuple-element.53), channel_id=1, source_target_pairs={{0,2},{1,3},{2,0},{3,1},{4,6},{5,7},{6,4},{7,5},{8,10},{9,11},{10,... | collective-permute-start | bytes 442376 | tf_op jit(solution)/shard_map/ppermute | solution.py:298
  133.4 14.4 %collective-permute-start.10 = (bf16[64,1152]{1,0:T(8,128)(2,1)S(1)}, bf16[64,1152]{1,0:T(8,128)(2,1)S(1)}, u32[]{:S(2)}, u32[]{:S(2)}) collective-permute-start(bf16[64,1152]{1,0:T(8,128)(2,1)S(1)} %get-tuple-element.54), channel_id=1, source_target_pairs={{0,1},{1,2},{2,3},{3,0},{4,5},{5,6},{6,7},{7,4},{8,9},{9,10},{10,1... | collective-permute-start | bytes 442376 | tf_op jit(solution)/shard_map/ppermute | solution.py:298
  135.2 12.6 %collective-permute-start.11 = (bf16[64,1152]{1,0:T(8,128)(2,1)S(1)}, bf16[64,1152]{1,0:T(8,128)(2,1)S(1)}, u32[]{:S(2)}, u32[]{:S(2)}) collective-permute-start(bf16[64,1152]{1,0:T(8,128)(2,1)S(1)} %get-tuple-element.55), channel_id=1, source_target_pairs={{0,3},{1,0},{2,1},{3,2},{4,7},{5,4},{6,5},{7,6},{8,11},{9,8},{10,9... | collective-permute-start | bytes 442376 | tf_op jit(solution)/shard_map/ppermute | solution.py:298

commit v7 on v6

--- a/solution.py
+++ b/solution.py
@@ -53,7 +53,7 @@
 def softmax(scores):
     top = jnp.max(scores, axis=-1, keepdims=True)
     raised = jnp.exp(scores - top)
-    return raised / jnp.sum(raised, axis=-1, keepdims=True)
+    return raised * (1.0 / jnp.sum(raised, axis=-1, keepdims=True))
 
 
 def of_head(array, head):

time: 168 us -> 168 us (level)
  no operation moved by 1% of the time
where the time goes in v7:
time: 168 us; the launch traced here: 166 us
  blocking collectives  74 us (44%)
  starting transfers between devices  36.9 us (22%)
  waiting for transfers between devices  26.7 us (16%)
  Pallas kernels  21.6 us (13%)
  local copies, waits for them, and re-layouts  5.77 us (3%)
    ppermute x12, starting transfers between devices, shift(): return lax.ppermute(array, 'tp', [(i, (i + k) % N_TP) for i in range(N_TP)])  29.3 us
    ppermute x12, waiting for transfers between devices, shift(): return lax.ppermute(array, 'tp', [(i, (i + k) % N_TP) for i in range(N_TP)])  23.4 us
    pallas_call x16, Pallas kernels, run(): pl.pallas_call(body, grid_spec=pltpu.PrefetchScalarGridSpec(num_scalar_pr...  21.6 us
    all_to_all x1, blocking collectives, across(): return lax.all_to_all(array, 'seq', split_axis=0, concat_axis=0, tiled=True)  21.4 us
    all_gather x1, blocking collectives, per_device(): grads = lax.all_gather(packed, 'tp')  21.2 us
    all_gather x1, blocking collectives, per_device(): ends = lax.all_gather(packed, 'tp')  16.3 us
    all_gather x1, blocking collectives, per_device(): mids = lax.all_gather(mid_own, 'tp')  15 us
    all_to_all x1, starting transfers between devices, across(): return lax.all_to_all(array, 'seq', split_axis=0, concat_axis=0, tiled=True)  7.64 us
  transfers between devices with their start and end apart: 13, of which 8 were waited for; matrix products, arithmetic and copies ran while one was open for 0% of the time, Pallas kernels for 5%

profile of v7, /device:TPU:1, one launch (start us, length us, event | category | flops | bytes accessed | tf_op | source)
XLA Modules:
  0.0 165.9 jit_solution(15829059347521680388)
XLA Ops:
  0.7 6.0 %shard_map.86 = (bf16[64,1152]{1,0:T(8,128)(2,1)}, bf16[64,1152]{1,0:T(8,128)(2,1)}, bf16[64,1152]{1,0:T(8,128)(2,1)}, bf16[64,1152]{1,0:T(8,128)(2,1)}, bf16[3,...) custom-call(s32[1]{0:T(128)} %bitcast.me_ref, bf16[256,1152]{1,0:T(8,128)(2,1)} %bitcast.23, ...), custom_call_target="tpu_custom_call" | custom-call | flops 1000000000 | tf_op jit(solution)/shard_map/pallas_call | solution.py:281
  6.7 3.9 %collective-permute-start = (bf16[64,1152]{1,0:T(8,128)(2,1)}, bf16[64,1152]{1,0:T(8,128)(2,1)S(1)}, u32[]{:S(2)}, u32[]{:S(2)}) collective-permute-start(bf16[64,1152]{1,0:T(8,128)(2,1)} %get-tuple-element.32), channel_id=1, source_target_pairs={{0,1},{1,2},{2,3},{3,0},{4,5},{5,6},{6,7},{7,4},{8,9},{9,10},{10,1... | collective-permute-start | bytes 442376 | tf_op jit(solution)/shard_map/ppermute | solution.py:298
  10.6 3.1 %collective-permute-start.1 = (bf16[64,1152]{1,0:T(8,128)(2,1)}, bf16[64,1152]{1,0:T(8,128)(2,1)S(1)}, u32[]{:S(2)}, u32[]{:S(2)}) collective-permute-start(bf16[64,1152]{1,0:T(8,128)(2,1)} %get-tuple-element.33), channel_id=1, source_target_pairs={{0,3},{1,0},{2,1},{3,2},{4,7},{5,4},{6,5},{7,6},{8,11},{9,8},{10,9... | collective-permute-start | bytes 442376 | tf_op jit(solution)/shard_map/ppermute | solution.py:298
  13.7 4.4 %collective-permute-start.2 = (bf16[64,1152]{1,0:T(8,128)(2,1)}, bf16[64,1152]{1,0:T(8,128)(2,1)S(1)}, u32[]{:S(2)}, u32[]{:S(2)}) collective-permute-start(bf16[64,1152]{1,0:T(8,128)(2,1)} %get-tuple-element.34), channel_id=1, source_target_pairs={{0,2},{1,3},{2,0},{3,1},{4,6},{5,7},{6,4},{7,5},{8,10},{9,11},{10,... | collective-permute-start | bytes 442376 | tf_op jit(solution)/shard_map/ppermute | solution.py:298
  18.1 0.9 copy-done.4
  19.0 0.9 copy-done.7
  19.9 0.1 shard_map.87.refs_0_
  20.0 5.4 %collective-permute-done.1.refs_2_ = bf16[64,1152]{1,0:T(8,128)(2,1)S(1)} collective-permute-done((bf16[64,1152]{1,0:T(8,128)(2,1)}, bf16[64,1152]{1,0:T(8,128)(2,1)S(1)}, u32[]{:S(2)}, u32[]{:S(2)}) %collective-permute-start.1) | collective-permute-done | bytes 147488 | tf_op jit(solution)/shard_map/ppermute | solution.py:298
  25.3 1.8 %collective-permute-done.2.refs_3_ = bf16[64,1152]{1,0:T(8,128)(2,1)S(1)} collective-permute-done((bf16[64,1152]{1,0:T(8,128)(2,1)}, bf16[64,1152]{1,0:T(8,128)(2,1)S(1)}, u32[]{:S(2)}, u32[]{:S(2)}) %collective-permute-start.2) | collective-permute-done | bytes 147488 | tf_op jit(solution)/shard_map/ppermute | solution.py:298
  27.1 0.2 shard_map.88
  27.3 21.4 %all_to_all.10 = bf16[64,2,576]{2,1,0:T(2,128)(2,1)S(1)} all-to-all(bf16[64,2,576]{2,1,0:T(2,128)(2,1)S(1)} %shard_map.88), channel_id=1, replica_groups=mesh['seq'=64,'tp'=4] {'seq'}, dimensions={0} | all-to-all | bytes 294912 | tf_op jit(solution)/shard_map/all_to_all | solution.py:302
  48.8 0.1 reshape.22.refs_0_
  48.9 0.1 all_gather_reshape.3
  49.0 15.0 %all_gather.15.refs_0_ = bf16[4,64,1152]{2,1,0:T(8,128)(2,1)S(1)} all-gather(bf16[1,64,1152]{2,1,0:T(8,128)(2,1)S(1)} %all_gather_reshape.3), channel_id=1, replica_groups=mesh['seq'=64,'tp'=4] {'tp'}, dimensions={0}, use_global_device_ids=true | all-gather | bytes 737280 | tf_op jit(solution)/shard_map/all_gather | solution.py:348
  64.1 0.1 slice_bitcast_fusion.3.refs_3_
  64.1 0.0 copy-start
  64.1 0.0 copy-start.1
  64.2 0.0 copy-start.3
  64.2 1.8 %slice_bitcast_fusion.1.refs_2_ = bf16[864,1152]{1,0:T(8,128)(2,1)S(1)} fusion(bf16[2,864,1152]{2,1,0:T(8,128)(2,1)} %bitcast.21), kind=kLoop, calls=%fused_computation.1 | loop fusion | bytes 3981312 | tf_op jit(solution)/shard_map/squeeze | solution.py:307
  66.0 2.3 %shard_map.90 = (bf16[64,1152]{1,0:T(8,128)(2,1)S(1)}, bf16[64,1152]{1,0:T(8,128)(2,1)S(1)}) custom-call(s32[1]{0:T(128)} %bitcast.me_ref, bf16[4,64,1152]{2,1,0:T(8,128)(2,1)S(1)} %all_gather.15.refs_0_, bf16[4,64,1152]{2,1,0:T(8,128)(2,1)S(1)} %copy-done, bf16[864,1152]{1,0:T(8,128)(2,1)S(1)} %slice_bitcast_fusion.1.refs_2_, ...), custom_call_target="tpu_custom_call" | custom-call | flops 50000000 | tf_op jit(solution)/shard_map/pallas_call | solution.py:281
  68.3 3.5 %collective-permute-start.3 = (bf16[64,1152]{1,0:T(8,128)(2,1)S(1)}, bf16[64,1152]{1,0:T(8,128)(2,1)S(1)}, u32[]{:S(2)}, u32[]{:S(2)}) collective-permute-start(bf16[64,1152]{1,0:T(8,128)(2,1)S(1)} %get-tuple-element.38), channel_id=1, source_target_pairs={{0,2},{1,3},{2,0},{3,1},{4,6},{5,7},{6,4},{7,5},{8,10},{9,11},{10,... | collective-permute-start | bytes 442376 | tf_op jit(solution)/shard_map/ppermute | solution.py:298
  71.8 2.3 %shard_map.92 = (bf16[64,1152]{1,0:T(8,128)(2,1)S(1)}, bf16[64,1152]{1,0:T(8,128)(2,1)S(1)}) custom-call(s32[1]{0:T(128)} %bitcast.me_ref, bf16[4,64,1152]{2,1,0:T(8,128)(2,1)S(1)} %all_gather.15.refs_0_, bf16[4,64,1152]{2,1,0:T(8,128)(2,1)S(1)} %copy-done, bf16[864,1152]{1,0:T(8,128)(2,1)S(1)} %slice_bitcast_fusion.1.refs_2_, ...), custom_call_target="tpu_custom_call" | custom-call | flops 50000000 | tf_op jit(solution)/shard_map/pallas_call | solution.py:281
  74.1 2.2 %collective-permute-start.4 = (bf16[64,1152]{1,0:T(8,128)(2,1)S(1)}, bf16[64,1152]{1,0:T(8,128)(2,1)S(1)}, u32[]{:S(2)}, u32[]{:S(2)}) collective-permute-start(bf16[64,1152]{1,0:T(8,128)(2,1)S(1)} %get-tuple-element.39), channel_id=1, source_target_pairs={{0,3},{1,0},{2,1},{3,2},{4,7},{5,4},{6,5},{7,6},{8,11},{9,8},{10,9... | collective-permute-start | bytes 442376 | tf_op jit(solution)/shard_map/ppermute | solution.py:298
  76.3 2.3 %shard_map.94 = (bf16[64,1152]{1,0:T(8,128)(2,1)S(1)}, bf16[64,1152]{1,0:T(8,128)(2,1)S(1)}) custom-call(s32[1]{0:T(128)} %bitcast.me_ref, bf16[4,64,1152]{2,1,0:T(8,128)(2,1)S(1)} %all_gather.15.refs_0_, bf16[4,64,1152]{2,1,0:T(8,128)(2,1)S(1)} %copy-done, bf16[864,1152]{1,0:T(8,128)(2,1)S(1)} %slice_bitcast_fusion.1.refs_2_, ...), custom_call_target="tpu_custom_call" | custom-call | flops 50000000 | tf_op jit(solution)/shard_map/pallas_call | solution.py:281
  78.6 0.5 collective-permute-start.5
  79.1 2.3 %shard_map.89 = (bf16[64,1152]{1,0:T(8,128)(2,1)S(1)}, bf16[64,1152]{1,0:T(8,128)(2,1)S(1)}) custom-call(s32[1]{0:T(128)} %bitcast.me_ref, bf16[4,64,1152]{2,1,0:T(8,128)(2,1)S(1)} %all_gather.15.refs_0_, bf16[4,64,1152]{2,1,0:T(8,128)(2,1)S(1)} %copy-done, bf16[864,1152]{1,0:T(8,128)(2,1)S(1)} %slice_bitcast_fusion.1.refs_2_, ...), custom_call_target="tpu_custom_call" | custom-call | flops 350000000 | tf_op jit(solution)/shard_map/pallas_call | solution.py:281
  81.4 3.3 %collective-permute-start.6 = (bf16[64,1152]{1,0:T(8,128)(2,1)S(1)}, bf16[64,1152]{1,0:T(8,128)(2,1)S(1)}, u32[]{:S(2)}, u32[]{:S(2)}) collective-permute-start(bf16[64,1152]{1,0:T(8,128)(2,1)S(1)} %get-tuple-element.46), channel_id=1, source_target_pairs={{0,3},{1,0},{2,1},{3,2},{4,7},{5,4},{6,5},{7,6},{8,11},{9,8},{10,9... | collective-permute-start | bytes 442376 | tf_op jit(solution)/shard_map/ppermute | solution.py:298
  84.7 3.0 %collective-permute-start.7 = (bf16[64,1152]{1,0:T(8,128)(2,1)S(1)}, bf16[64,1152]{1,0:T(8,128)(2,1)S(1)}, u32[]{:S(2)}, u32[]{:S(2)}) collective-permute-start(bf16[64,1152]{1,0:T(8,128)(2,1)S(1)} %get-tuple-element.47), channel_id=1, source_target_pairs={{0,2},{1,3},{2,0},{3,1},{4,6},{5,7},{6,4},{7,5},{8,10},{9,11},{10,... | collective-permute-start | bytes 442376 | tf_op jit(solution)/shard_map/ppermute | solution.py:298
  87.8 1.1 shard_map.95
  88.9 7.6 %all-to-all-start.1 = ((bf16[64,2,576]{2,1,0:T(2,128)(2,1)}), bf16[64,2,576]{2,1,0:T(2,128)(2,1)S(1)}, u32[]{:S(2)}, u32[]{:S(2)}) async-start(bf16[64,2,576]{2,1,0:T(2,128)(2,1)} %shard_map.95), calls=%async_computation.1 | async-start | bytes 327680 | tf_op jit(solution)/shard_map/all_to_all | solution.py:302
  96.5 2.3 %collective-permute-done.6.refs_3_ = bf16[64,1152]{1,0:T(8,128)(2,1)S(1)} collective-permute-done((bf16[64,1152]{1,0:T(8,128)(2,1)S(1)}, bf16[64,1152]{1,0:T(8,128)(2,1)S(1)}, u32[]{:S(2)}, u32[]{:S(2)}) %collective-permute-start.6) | collective-permute-done | bytes 147488 | tf_op jit(solution)/shard_map/ppermute | solution.py:298
  98.9 1.1 collective-permute-done.7.refs_4_
  100.0 2.0 %collective-permute-done.8.refs_5_ = bf16[64,1152]{1,0:T(8,128)(2,1)S(1)} collective-permute-done((bf16[64,1152]{1,0:T(8,128)(2,1)S(1)}, bf16[64,1152]{1,0:T(8,128)(2,1)S(1)}, u32[]{:S(2)}, u32[]{:S(2)}) %collective-permute-start.8) | collective-permute-done | bytes 147488 | tf_op jit(solution)/shard_map/ppermute | solution.py:298
  102.0 0.1 shard_map.96.result_ref
  102.1 3.3 %all-to-all-done.1.grad_ref = bf16[64,2,576]{2,1,0:T(2,128)(2,1)S(1)} async-done(((bf16[64,2,576]{2,1,0:T(2,128)(2,1)}), bf16[64,2,576]{2,1,0:T(2,128)(2,1)S(1)}, u32[]{:S(2)}, u32[]{:S(2)}) %all-to-all-start.1) | async-done | bytes 147488 | tf_op jit(solution)/shard_map/all_to_all | solution.py:302
  105.4 0.1 slice_bitcast_fusion.2.ow_ref
  105.4 0.4 shard_map.97.g_ref
  105.8 21.2 %all-gather = bf16[384,1152]{1,0:T(8,128)(2,1)S(1)} all-gather(bf16[96,1152]{1,0:T(8,128)(2,1)S(1)} %shard_map.97.g_ref), channel_id=2, replica_groups=mesh['seq'=64,'tp'=4] {'tp'}, dimensions={0}, use_global_device_ids=true | all-gather | bytes 1105920 | tf_op jit(solution)/shard_map/all_gather | solution.py:394
  127.0 1.8 %slice_bitcast_fusion.w_ref = bf16[864,1152]{1,0:T(8,128)(2,1)S(1)} fusion(bf16[2,864,1152]{2,1,0:T(8,128)(2,1)} %bitcast.22), kind=kLoop, calls=%fused_computation | loop fusion | bytes 3981312 | tf_op jit(solution)/shard_map/squeeze | solution.py:307
  128.8 2.8 %shard_map.98 = (bf16[64,1152]{1,0:T(8,128)(2,1)S(1)}, bf16[64,1152]{1,0:T(8,128)(2,1)S(1)}, bf16[64,1152]{1,0:T(8,128)(2,1)S(1)}, bf16[64,1152]{1,0:T(8,128)(2,1)S(1)}) custom-call(s32[1]{0:T(128)} %bitcast.me_ref, bf16[4,96,1152]{2,1,0:T(8,128)(2,1)S(1)} %bitcast.18, bf16[3,256,288]{2,1,0:T(8,128)(2,1)S(1)} %copy-done.6, ...), custom_call_target="tpu_custom_call" | custom-call | flops 1500000000 | tf_op jit(solution)/shard_map/pallas_call | solution.py:281
  131.6 1.8 %collective-permute-start.9 = (bf16[64,1152]{1,0:T(8,128)(2,1)S(1)}, bf16[64,1152]{1,0:T(8,128)(2,1)S(1)}, u32[]{:S(2)}, u32[]{:S(2)}) collective-permute-start(bf16[64,1152]{1,0:T(8,128)(2,1)S(1)} %get-tuple-element.53), channel_id=1, source_target_pairs={{0,2},{1,3},{2,0},{3,1},{4,6},{5,7},{6,4},{7,5},{8,10},{9,11},{10,... | collective-permute-start | bytes 442376 | tf_op jit(solution)/shard_map/ppermute | solution.py:298
  133.4 1.8 %collective-permute-start.10 = (bf16[64,1152]{1,0:T(8,128)(2,1)S(1)}, bf16[64,1152]{1,0:T(8,128)(2,1)S(1)}, u32[]{:S(2)}, u32[]{:S(2)}) collective-permute-start(bf16[64,1152]{1,0:T(8,128)(2,1)S(1)} %get-tuple-element.54), channel_id=1, source_target_pairs={{0,1},{1,2},{2,3},{3,0},{4,5},{5,6},{6,7},{7,4},{8,9},{9,10},{10,1... | collective-permute-start | bytes 442376 | tf_op jit(solution)/shard_map/ppermute | solution.py:298
  135.2 1.8 %collective-permute-start.11 = (bf16[64,1152]{1,0:T(8,128)(2,1)S(1)}, bf16[64,1152]{1,0:T(8,128)(2,1)S(1)}, u32[]{:S(2)}, u32[]{:S(2)}) collective-permute-start(bf16[64,1152]{1,0:T(8,128)(2,1)S(1)} %get-tuple-element.55), channel_id=1, source_target_pairs={{0,3},{1,0},{2,1},{3,2},{4,7},{5,4},{6,5},{7,6},{8,11},{9,8},{10,9... | collective-permute-start | bytes 442376 | tf_op jit(solution)/shard_map/ppermute | solution.py:298
  137.0 2.7 %collective-permute-done.9.b_ref = bf16[64,1152]{1,0:T(8,128)(2,1)S(1)} collective-permute-done((bf16[64,1152]{1,0:T(8,128)(2,1)S(1)}, bf16[64,1152]{1,0:T(8,128)(2,1)S(1)}, u32[]{:S(2)}, u32[]{:S(2)}) %collective-permute-start.9) | collective-permute-done | bytes 147488 | tf_op jit(solution)/shard_map/ppermute | solution.py:298
  139.8 8.0 %collective-permute-done.10.b3 = bf16[64,1152]{1,0:T(8,128)(2,1)S(1)} collective-permute-done((bf16[64,1152]{1,0:T(8,128)(2,1)S(1)}, bf16[64,1152]{1,0:T(8,128)(2,1)S(1)}, u32[]{:S(2)}, u32[]{:S(2)}) %collective-permute-start.10) | collective-permute-done | bytes 147488 | tf_op jit(solution)/shard_map/ppermute | solution.py:298
  147.8 0.3 shard_map.100
  148.2 16.3 %all-gather.1 = bf16[384,1152]{1,0:T(8,128)(2,1)S(1)} all-gather(bf16[96,1152]{1,0:T(8,128)(2,1)S(1)} %shard_map.100), channel_id=3, replica_groups=mesh['seq'=64,'tp'=4] {'tp'}, dimensions={0}, use_global_device_ids=true | all-gather | bytes 1105920 | tf_op jit(solution)/shard_map/all_gather | solution.py:409
  164.5 1.3 shard_map.101
  (22 shorter events, 0.1 us)
Async XLA Ops:
  0.6 17.4 %copy-start.2 = (f32[2,1152]{1,0:T(2,128)S(1)}, f32[2,1152]{1,0:T(2,128)}, u32[]{:S(2)}) copy-start(f32[2,1152]{1,0:T(2,128)} %gate_ref.1) | copy-start | bytes 27652
  0.6 63.4 %copy-start.8 = (bf16[2,288,1152]{2,1,0:T(8,128)(2,1)S(1)}, bf16[2,288,1152]{2,1,0:T(8,128)(2,1)}, u32[]{:S(2)}) copy-start(bf16[2,288,1152]{2,1,0:T(8,128)(2,1)} %ow_hbm.1) | copy-start | bytes 3981316
  6.7 11.4 %collective-permute-start = (bf16[64,1152]{1,0:T(8,128)(2,1)}, bf16[64,1152]{1,0:T(8,128)(2,1)S(1)}, u32[]{:S(2)}, u32[]{:S(2)}) collective-permute-start(bf16[64,1152]{1,0:T(8,128)(2,1)} %get-tuple-element.32), channel_id=1, source_target_pairs={{0,1},{1,2},{2,3},{3,0},{4,5},{5,6},{6,7},{7,4},{8,9},{9,10},{10,1... | collective-permute-start | bytes 442376 | tf_op jit(solution)/shard_map/ppermute | solution.py:298
  10.6 14.8 %collective-permute-start.1 = (bf16[64,1152]{1,0:T(8,128)(2,1)}, bf16[64,1152]{1,0:T(8,128)(2,1)S(1)}, u32[]{:S(2)}, u32[]{:S(2)}) collective-permute-start(bf16[64,1152]{1,0:T(8,128)(2,1)} %get-tuple-element.33), channel_id=1, source_target_pairs={{0,3},{1,0},{2,1},{3,2},{4,7},{5,4},{6,5},{7,6},{8,11},{9,8},{10,9... | collective-permute-start | bytes 442376 | tf_op jit(solution)/shard_map/ppermute | solution.py:298
  13.7 13.5 %collective-permute-start.2 = (bf16[64,1152]{1,0:T(8,128)(2,1)}, bf16[64,1152]{1,0:T(8,128)(2,1)S(1)}, u32[]{:S(2)}, u32[]{:S(2)}) collective-permute-start(bf16[64,1152]{1,0:T(8,128)(2,1)} %get-tuple-element.34), channel_id=1, source_target_pairs={{0,2},{1,3},{2,0},{3,1},{4,6},{5,7},{6,4},{7,5},{8,10},{9,11},{10,... | collective-permute-start | bytes 442376 | tf_op jit(solution)/shard_map/ppermute | solution.py:298
  18.1 0.9 copy-start.4
  19.0 0.9 copy-start.7
  64.1 1.8 %copy-start = (bf16[4,64,1152]{2,1,0:T(8,128)(2,1)S(1)}, bf16[4,64,1152]{2,1,0:T(8,128)(2,1)}, u32[]{:S(2)}) copy-start(bf16[4,64,1152]{2,1,0:T(8,128)(2,1)} %refs_1_.14) | copy-start | bytes 1769476
  64.1 1.8 %copy-start.1 = (f32[2,1152]{1,0:T(2,128)S(1)}, f32[2,1152]{1,0:T(2,128)}, u32[]{:S(2)}) copy-start(f32[2,1152]{1,0:T(2,128)} %scale_ref.3) | copy-start | bytes 27652
  64.2 1.8 %copy-start.3 = (f32[2,1152]{1,0:T(2,128)S(1)}, f32[2,1152]{1,0:T(2,128)}, u32[]{:S(2)}) copy-start(f32[2,1152]{1,0:T(2,128)} %refs_4_.7) | copy-start | bytes 27652
  68.3 19.4 %collective-permute-start.3 = (bf16[64,1152]{1,0:T(8,128)(2,1)S(1)}, bf16[64,1152]{1,0:T(8,128)(2,1)S(1)}, u32[]{:S(2)}, u32[]{:S(2)}) collective-permute-start(bf16[64,1152]{1,0:T(8,128)(2,1)S(1)} %get-tuple-element.38), channel_id=1, source_target_pairs={{0,2},{1,3},{2,0},{3,1},{4,6},{5,7},{6,4},{7,5},{8,10},{9,11},{10,... | collective-permute-start | bytes 442376 | tf_op jit(solution)/shard_map/ppermute | solution.py:298
  74.1 13.6 %collective-permute-start.4 = (bf16[64,1152]{1,0:T(8,128)(2,1)S(1)}, bf16[64,1152]{1,0:T(8,128)(2,1)S(1)}, u32[]{:S(2)}, u32[]{:S(2)}) collective-permute-start(bf16[64,1152]{1,0:T(8,128)(2,1)S(1)} %get-tuple-element.39), channel_id=1, source_target_pairs={{0,3},{1,0},{2,1},{3,2},{4,7},{5,4},{6,5},{7,6},{8,11},{9,8},{10,9... | collective-permute-start | bytes 442376 | tf_op jit(solution)/shard_map/ppermute | solution.py:298
  78.6 9.1 %collective-permute-start.5 = (bf16[64,1152]{1,0:T(8,128)(2,1)S(1)}, bf16[64,1152]{1,0:T(8,128)(2,1)S(1)}, u32[]{:S(2)}, u32[]{:S(2)}) collective-permute-start(bf16[64,1152]{1,0:T(8,128)(2,1)S(1)} %get-tuple-element.40), channel_id=1, source_target_pairs={{0,1},{1,2},{2,3},{3,0},{4,5},{5,6},{6,7},{7,4},{8,9},{9,10},{10,1... | collective-permute-start | bytes 442376 | tf_op jit(solution)/shard_map/ppermute | solution.py:298
  81.4 17.5 %collective-permute-start.6 = (bf16[64,1152]{1,0:T(8,128)(2,1)S(1)}, bf16[64,1152]{1,0:T(8,128)(2,1)S(1)}, u32[]{:S(2)}, u32[]{:S(2)}) collective-permute-start(bf16[64,1152]{1,0:T(8,128)(2,1)S(1)} %get-tuple-element.46), channel_id=1, source_target_pairs={{0,3},{1,0},{2,1},{3,2},{4,7},{5,4},{6,5},{7,6},{8,11},{9,8},{10,9... | collective-permute-start | bytes 442376 | tf_op jit(solution)/shard_map/ppermute | solution.py:298
  84.7 15.3 %collective-permute-start.7 = (bf16[64,1152]{1,0:T(8,128)(2,1)S(1)}, bf16[64,1152]{1,0:T(8,128)(2,1)S(1)}, u32[]{:S(2)}, u32[]{:S(2)}) collective-permute-start(bf16[64,1152]{1,0:T(8,128)(2,1)S(1)} %get-tuple-element.47), channel_id=1, source_target_pairs={{0,2},{1,3},{2,0},{3,1},{4,6},{5,7},{6,4},{7,5},{8,10},{9,11},{10,... | collective-permute-start | bytes 442376 | tf_op jit(solution)/shard_map/ppermute | solution.py:298
  87.7 14.3 %collective-permute-start.8 = (bf16[64,1152]{1,0:T(8,128)(2,1)S(1)}, bf16[64,1152]{1,0:T(8,128)(2,1)S(1)}, u32[]{:S(2)}, u32[]{:S(2)}) collective-permute-start(bf16[64,1152]{1,0:T(8,128)(2,1)S(1)} %get-tuple-element.48), channel_id=1, source_target_pairs={{0,1},{1,2},{2,3},{3,0},{4,5},{5,6},{6,7},{7,4},{8,9},{9,10},{10,1... | collective-permute-start | bytes 442376 | tf_op jit(solution)/shard_map/ppermute | solution.py:298
  88.9 16.5 %all-to-all-start.1 = ((bf16[64,2,576]{2,1,0:T(2,128)(2,1)}), bf16[64,2,576]{2,1,0:T(2,128)(2,1)S(1)}, u32[]{:S(2)}, u32[]{:S(2)}) async-start(bf16[64,2,576]{2,1,0:T(2,128)(2,1)} %shard_map.95), calls=%async_computation.1 | async-start | bytes 327680 | tf_op jit(solution)/shard_map/all_to_all | solution.py:302
  127.0 1.8 %copy-start.6 = (bf16[3,256,288]{2,1,0:T(8,128)(2,1)S(1)}, bf16[3,256,288]{2,1,0:T(8,128)(2,1)}, u32[]{:S(2)}) copy-start(bf16[3,256,288]{2,1,0:T(8,128)(2,1)} %get-tuple-element.49.qkv_ref) | copy-start | bytes 1327108
  128.7 19.1 %copy-start.5 = (bf16[64,1152]{1,0:T(8,128)(2,1)S(1)}, bf16[64,1152]{1,0:T(8,128)(2,1)}, u32[]{:S(2)}) copy-start(bf16[64,1152]{1,0:T(8,128)(2,1)} %get-tuple-element.30.refs_0_.x_ref) | copy-start | bytes 442372
  131.6 8.1 %collective-permute-start.9 = (bf16[64,1152]{1,0:T(8,128)(2,1)S(1)}, bf16[64,1152]{1,0:T(8,128)(2,1)S(1)}, u32[]{:S(2)}, u32[]{:S(2)}) collective-permute-start(bf16[64,1152]{1,0:T(8,128)(2,1)S(1)} %get-tuple-element.53), channel_id=1, source_target_pairs={{0,2},{1,3},{2,0},{3,1},{4,6},{5,7},{6,4},{7,5},{8,10},{9,11},{10,... | collective-permute-start | bytes 442376 | tf_op jit(solution)/shard_map/ppermute | solution.py:298
  133.4 14.4 %collective-permute-start.10 = (bf16[64,1152]{1,0:T(8,128)(2,1)S(1)}, bf16[64,1152]{1,0:T(8,128)(2,1)S(1)}, u32[]{:S(2)}, u32[]{:S(2)}) collective-permute-start(bf16[64,1152]{1,0:T(8,128)(2,1)S(1)} %get-tuple-element.54), channel_id=1, source_target_pairs={{0,1},{1,2},{2,3},{3,0},{4,5},{5,6},{6,7},{7,4},{8,9},{9,10},{10,1... | collective-permute-start | bytes 442376 | tf_op jit(solution)/shard_map/ppermute | solution.py:298
  135.2 12.6 %collective-permute-start.11 = (bf16[64,1152]{1,0:T(8,128)(2,1)S(1)}, bf16[64,1152]{1,0:T(8,128)(2,1)S(1)}, u32[]{:S(2)}, u32[]{:S(2)}) collective-permute-start(bf16[64,1152]{1,0:T(8,128)(2,1)S(1)} %get-tuple-element.55), channel_id=1, source_target_pairs={{0,3},{1,0},{2,1},{3,2},{4,7},{5,4},{6,5},{7,6},{8,11},{9,8},{10,9... | collective-permute-start | bytes 442376 | tf_op jit(solution)/shard_map/ppermute | solution.py:298
